TPU v7x, 256 devices: a whole 4x4x8 slice. The times are simulated.
256 devices in a mesh: gx: 32 (over x_lo, z, core), gy: 8 (over x_hi, y).
Axes of the slice: x: 4 (x_hi: 2, x_lo: 2; x = x_hi * 2 + x_lo), y: 4, z: 8, core: 2. Of those that a mesh axis runs over, the one named last changes fastest.
Arguments:
- e_field: float32 [2, 3, 16, 1024, 1024], P(None, None, None, 'gx', 'gy'), may hold values from -6 to 6
- h_field: float32 [2, 3, 16, 1024, 1024], P(None, None, None, 'gx', 'gy'), may hold values from -6 to 6
- material: int32 [16, 1024, 1024], P(None, 'gx', 'gy'), may hold values from 0 to 7
- pattern: int32 [16, 1024, 1024], P(None, 'gx', 'gy'), may hold values from 0 to 15
- base_eps: float32 [8], replicated, may hold values from 2 to 12
- mode_table: float32 [4, 16], replicated, may hold values from -0.1 to 0.1
- nodes: float32 [4], replicated, may hold values from -1 to 1
- bloch_phase: float32 [2], replicated, may hold values from -3.140625 to 3.140625
- monitor_z: int32 [1], replicated, may hold values from 0 to 15
Outputs:
- e_out: float32 [2, 3, 16, 1024, 1024], P(None, None, None, 'gx', 'gy')
- h_out: float32 [2, 3, 16, 1024, 1024], P(None, None, None, 'gx', 'gy')
- orders: float32 [2, 2, 256, 256], P(None, None, 'gx', 'gy')
All inputs are finite; a program needn't handle non-finite values.
Results may differ from a plain program's by a relative error of at most 0.000078.
Values sent between devices are 32-bit elements; how exact they have to be, the bound alone decides.
No kernel may reach another device: no remote copies, remote signals or barrier semaphores. Data moves between devices by JAX's collectives and lax.ppermute only.
A program may use at most 64 MiB of HBM per device.

v0:
```python
import math

import jax
import jax.numpy as jnp
from jax import lax
from jax.sharding import PartitionSpec as P

STEPS = 2
ORD_X = 256
ORD_Y = 256


STEP_DT = 0.5


def passed_along(block, axis, distance):
    devices = range(lax.axis_size(axis))
    route = [((i - distance) % len(devices), i) for i in devices]
    return lax.ppermute(block, axis, route)


def rotate(values, twist_cos, twist_sin):
    return jnp.stack(
        [
            values[0] * twist_cos - values[1] * twist_sin,
            values[1] * twist_cos + values[0] * twist_sin,
        ]
    )


def next_layer(values):
    return jnp.concatenate([values[:, 1:], jnp.zeros_like(values[:, :1])], axis=1)


def prev_layer(values):
    return jnp.concatenate([jnp.zeros_like(values[:, :1]), values[:, :-1]], axis=1)


def pair_xz(values):
    return jnp.stack([values[:, 0], values[:, 2]], axis=1)


def h_update(electric, magnetic, x_next, y_next):
    e_xcomp, e_ycomp, e_zcomp = (electric[:, 0], electric[:, 1], electric[:, 2])
    curl_xcomp = y_next[:, 1] - e_zcomp - (next_layer(e_ycomp) - e_ycomp)
    curl_ycomp = next_layer(e_xcomp) - e_xcomp - (x_next[:, 1] - e_zcomp)
    curl_zcomp = x_next[:, 0] - e_ycomp - (y_next[:, 0] - e_xcomp)
    return magnetic - STEP_DT * jnp.stack([curl_xcomp, curl_ycomp, curl_zcomp], axis=1)


def e_update(electric, magnetic, x_prev, y_prev, coef):
    h_xcomp, h_ycomp, h_zcomp = (magnetic[:, 0], magnetic[:, 1], magnetic[:, 2])
    curl_xcomp = h_zcomp - y_prev[:, 1] - (h_ycomp - prev_layer(h_ycomp))
    curl_ycomp = h_xcomp - prev_layer(h_xcomp) - (h_zcomp - x_prev[:, 1])
    curl_zcomp = h_ycomp - x_prev[:, 0] - (h_xcomp - y_prev[:, 0])
    return electric + coef * jnp.stack([curl_xcomp, curl_ycomp, curl_zcomp], axis=1)


def twiddles(count, half, offset, length, total, theta):
    order_index = lax.iota(jnp.int32, count) - half
    place = offset + lax.iota(jnp.int32, length)
    product = jnp.mod(order_index[:, None] * place[None, :], total)
    angle = (
        2.0 * math.pi * product.astype(jnp.float32) + theta * place.astype(jnp.float32)[None, :]
    ) / total
    return (jnp.cos(angle), jnp.sin(angle))


def y_section(planes, wave_cos, wave_sin):
    width = planes.shape[1]
    count = wave_cos.shape[0]
    with_cos = jnp.einsum(
        "kxy,qy->kxq",
        planes,
        wave_cos,
        precision=lax.Precision.HIGHEST,
        preferred_element_type=jnp.float32,
    ).reshape(2, 2, width, count)
    with_sin = jnp.einsum(
        "kxy,qy->kxq",
        planes,
        wave_sin,
        precision=lax.Precision.HIGHEST,
        preferred_element_type=jnp.float32,
    ).reshape(2, 2, width, count)
    return jnp.stack([with_cos[:, 0] + with_sin[:, 1], with_cos[:, 1] - with_sin[:, 0]], axis=1)


def x_section(spread, wave_cos, wave_sin):
    count = wave_cos.shape[0]
    columns = spread.shape[2]
    with_cos = jnp.einsum(
        "px,kxq->pkq",
        wave_cos,
        spread,
        precision=lax.Precision.HIGHEST,
        preferred_element_type=jnp.float32,
    ).reshape(count, 2, 2, columns)
    with_sin = jnp.einsum(
        "px,kxq->pkq",
        wave_sin,
        spread,
        precision=lax.Precision.HIGHEST,
        preferred_element_type=jnp.float32,
    ).reshape(count, 2, 2, columns)
    return jnp.stack(
        [with_cos[:, :, 0] + with_sin[:, :, 1], with_cos[:, :, 1] - with_sin[:, :, 0]], axis=2
    )


def lookup(indices, table):
    labels = jnp.arange(table.shape[0], dtype=jnp.int32)
    hits = indices[None] == labels[:, None, None, None]
    return jnp.sum(jnp.where(hits, table[:, None, None, None], 0.0), axis=0)


def shards(
    e_field, h_field, material, pattern, base_eps, mode_table, nodes, bloch_phase, monitor_z
):
    count_x = lax.axis_size("gx")
    count_y = lax.axis_size("gy")
    index_x = lax.axis_index("gx")
    index_y = lax.axis_index("gy")
    cells_x = e_field.shape[3]
    cells_y = e_field.shape[4]
    total_x = cells_x * count_x
    total_y = cells_y * count_y
    xwrap_cos = jnp.cos(bloch_phase[0])
    xwrap_sin = jnp.sin(bloch_phase[0])
    ywrap_cos = jnp.cos(bloch_phase[1])
    ywrap_sin = jnp.sin(bloch_phase[1])
    factor = 1.0 + jnp.sum(nodes[:, None] * mode_table, axis=0)
    coef = STEP_DT / (lookup(material, base_eps) * lookup(pattern, factor))

    def x_prev_of(magnetic):
        chosen = magnetic[:, 1:3]
        arrived = passed_along(chosen[:, :, :, -1:, :], "gx", 1)
        arrived = jnp.where(index_x == 0, rotate(arrived, xwrap_cos, -xwrap_sin), arrived)
        return jnp.concatenate([arrived, chosen[:, :, :, :-1, :]], axis=3)

    def y_prev_of(magnetic):
        chosen = pair_xz(magnetic)
        arrived = passed_along(chosen[:, :, :, :, -1:], "gy", 1)
        arrived = jnp.where(index_y == 0, rotate(arrived, ywrap_cos, -ywrap_sin), arrived)
        return jnp.concatenate([arrived, chosen[:, :, :, :, :-1]], axis=4)

    electric, magnetic = (e_field, h_field)
    for instant in range(STEPS):
        x_chosen = electric[:, 1:3]
        x_arrived = passed_along(x_chosen[:, :, :, 0:1, :], "gx", -1)
        x_arrived = jnp.where(
            index_x == count_x - 1, rotate(x_arrived, xwrap_cos, xwrap_sin), x_arrived
        )
        y_chosen = pair_xz(electric)
        y_arrived = passed_along(y_chosen[:, :, :, :, 0:1], "gy", -1)
        y_arrived = jnp.where(
            index_y == count_y - 1, rotate(y_arrived, ywrap_cos, ywrap_sin), y_arrived
        )
        magnetic = h_update(
            electric,
            magnetic,
            jnp.concatenate([x_chosen[:, :, :, 1:, :], x_arrived], axis=3),
            jnp.concatenate([y_chosen[:, :, :, :, 1:], y_arrived], axis=4),
        )
        electric = e_update(electric, magnetic, x_prev_of(magnetic), y_prev_of(magnetic), coef)
    plane = lax.dynamic_index_in_dim(electric, monitor_z[0], axis=2, keepdims=False)
    scale = 1.0 / math.sqrt(total_x * total_y)
    planes = jnp.transpose(plane[:, 0:2], (1, 0, 2, 3)).reshape(4, cells_x, cells_y) * scale
    offset_x = index_x * cells_x
    offset_y = index_y * cells_y
    ycos, ysin = twiddles(ORD_Y, ORD_Y // 2, offset_y, cells_y, total_y, bloch_phase[1])
    spread = y_section(planes, ycos, ysin).reshape(4, cells_x, ORD_Y)
    xcos, xsin = twiddles(
        lax.axis_size("gx") * (ORD_X // count_x),
        ORD_X // 2,
        offset_x,
        cells_x,
        total_x,
        bloch_phase[0],
    )
    owned_rows = lax.psum_scatter(
        x_section(spread, xcos, xsin), "gx", scatter_dimension=0, tiled=True
    )
    owned = lax.psum_scatter(owned_rows, "gy", scatter_dimension=3, tiled=True)
    return (electric, magnetic, jnp.transpose(owned, (1, 2, 0, 3)))


def solution(mesh):
    return jax.shard_map(
        shards,
        mesh=mesh,
        in_specs=(
            P(None, None, None, "gx", "gy"),
            P(None, None, None, "gx", "gy"),
            P(None, "gx", "gy"),
            P(None, "gx", "gy"),
            P(),
            P(),
            P(),
            P(),
            P(),
        ),
        out_specs=(
            P(None, None, None, "gx", "gy"),
            P(None, None, None, "gx", "gy"),
            P(None, None, "gx", "gy"),
        ),
        check_vma=False,
    )
```

profile of v0, /device:TPU:1, one launch (start us, length us, event | category | flops | bytes accessed | tf_op | source)
XLA Modules:
  0.0 304.9 jit_solution(13832192741157641497)
XLA Ops:
  7.2 1.3 slice_bitcast_fusion.15
  9.9 6.1 %collective-permute-start = (f32[2,2,16,32,1]{3,2,4,1,0:T(8,128)S(1)}, f32[2,2,16,32,1]{3,2,4,1,0:T(8,128)S(1)}, u32[]{:S(2)}, u32[]{:S(2)}) collective-permute-start(f32[2,2,16,32,1]{3,2,4,1,0:T(8,128)S(1)} %copy.296), channel_id=1, source_target_pairs={{1,0},{2,1},{3,2},{4,3},{5,4},{6,5},{7,6},{0,7},{9,8},{10,9},{11,1... | collective-permute-start | bytes 24584 | tf_op jit(solution)/shard_map/ppermute | solution.py:19
  16.0 1.0 collective-permute-start.1
  17.1 1.4 slice_maximum_fusion.3
  20.9 1.2 select_reduce_fusion.1
  25.7 1.2 slice.288
  26.9 1.4 copy.297
  28.3 1.4 copy.298
  29.8 1.5 broadcast_select_fusion.3
  32.5 0.9 copy-done.7
  33.8 1.1 slice_bitcast_fusion.9
  35.9 1.3 slice_maximum_fusion.2
  37.2 1.7 copy.311
  39.7 1.1 slice.381
  40.8 1.5 collective-permute-start.3
  44.0 1.4 collective-permute-done.2
  45.3 1.4 copy.312
  46.8 1.4 copy.313
  48.2 1.5 broadcast_select_fusion.1
  53.6 1.2 slice_bitcast_fusion.6
  55.7 1.1 pad_maximum_fusion.1
  56.8 1.7 copy.325
  58.4 4.2 %collective-permute-start.4 = (f32[2,2,16,32,1]{3,2,4,1,0:T(8,128)S(1)}, f32[2,2,16,32,1]{3,2,4,1,0:T(8,128)S(1)}, u32[]{:S(2)}, u32[]{:S(2)}) collective-permute-start(f32[2,2,16,32,1]{3,2,4,1,0:T(8,128)S(1)} %copy.325), channel_id=1, source_target_pairs={{1,0},{2,1},{3,2},{4,3},{5,4},{6,5},{7,6},{0,7},{9,8},{10,9},{11,1... | collective-permute-start | bytes 24584 | tf_op jit(solution)/shard_map/ppermute | solution.py:19
  62.6 2.6 slice_maximum_fusion.1
  65.2 1.1 slice.396
  66.4 3.8 %collective-permute-start.5 = (f32[2,2,16,1,128]{4,2,3,1,0:T(8,128)S(1)}, f32[2,2,16,1,128]{4,2,3,1,0:T(8,128)S(1)}, u32[]{:S(2)}, u32[]{:S(2)}) collective-permute-start(f32[2,2,16,1,128]{4,2,3,1,0:T(8,128)S(1)} %bitcast.314), channel_id=1, source_target_pairs={{8,0},{16,8},{24,16},{32,24},{40,32},{48,40},{56,48},{64,56},{72,6... | collective-permute-start | bytes 98312 | tf_op jit(solution)/shard_map/ppermute | solution.py:19
  70.2 0.8 slice.394
  71.9 1.4 copy.326
  73.3 1.4 copy.327
  74.7 1.6 broadcast_select_fusion.2
  78.3 0.9 copy-done.8
  80.2 1.3 slice_bitcast_fusion.3
  82.5 1.3 slice_maximum_fusion
  83.8 1.7 copy.338
  86.4 1.1 slice.415
  89.2 2.8 collective-permute-done.6
  91.9 1.4 copy.339
  93.4 1.4 copy.340
  94.8 1.5 broadcast_select_fusion
  100.8 0.8 fusion.68
  101.6 0.8 fusion.66
  102.5 1.2 fusion.73
  103.7 1.2 fusion.72
  105.1 1.1 pad_maximum_fusion.4
  106.3 113.8 %reduce-scatter.5.cloned.1.call-done = f32[8,2,2,256]{3,0,2,1:T(8,128)} async-done(((f32[256,2,2,256]{3,0,2,1:T(8,128)}), f32[8,2,2,256]{3,0,2,1:T(8,128)}) %reduce-scatter.5.cloned.1.call-update) | async-done | bytes 32784 | tf_op jit(solution)/shard_map/reduce_scatter | solution.py:181
  220.1 1.1 copy.354
  221.2 1.1 reshape.178
  222.3 74.2 %reduce-scatter.7.cloned.1.call-done = f32[32,32]{1,0:T(8,128)} async-done(((f32[256,32]{1,0:T(8,128)}), f32[32,32]{1,0:T(8,128)}) %reduce-scatter.7.cloned.1.call-update) | async-done | bytes 4112
  (173 shorter events, 27.0 us)
Async XLA Ops:
  7.2 212.9 %reduce-scatter.5.cloned.1.call-start = ((), (), s32[]{:S(2)}) async-start(), calls=%async_computation.2 | async-start | bytes 1081344 | tf_op jit(solution)/shard_map/reduce_scatter | solution.py:181
  9.3 6.7 %copy-start = (f32[2,3,16,32,128]{4,3,2,1,0:T(8,128)S(1)}, f32[2,3,16,32,128]{4,3,2,1,0:T(8,128)}, u32[]{:S(2)}) copy-start(f32[2,3,16,32,128]{4,3,2,1,0:T(8,128)} %param.9) | copy-start | bytes 4718596
  9.4 9.0 %copy-start.47 = (f32[2]{0:T(128)S(1)}, f32[2]{0:T(128)}, u32[]{:S(2)}) copy-start(f32[2]{0:T(128)} %param.16) | copy-start | bytes 28
  9.4 9.6 %copy-start.46 = (f32[4,16]{1,0:T(4,128)S(1)}, f32[4,16]{1,0:T(4,128)}, u32[]{:S(2)}) copy-start(f32[4,16]{1,0:T(4,128)} %param.14) | copy-start | bytes 772
  9.4 10.9 %copy-start.45 = (s32[16,32,128]{2,1,0:T(8,128)S(1)}, s32[16,32,128]{2,1,0:T(8,128)}, u32[]{:S(2)}) copy-start(s32[16,32,128]{2,1,0:T(8,128)} %param.12) | copy-start | bytes 786436
  9.9 11.0 %copy-start.48 = (f32[8]{0:T(128)S(1)}, f32[8]{0:T(128)}, u32[]{:S(2)}) copy-start(f32[8]{0:T(128)} %param.13) | copy-start | bytes 100
  9.9 17.0 %collective-permute-start = (f32[2,2,16,32,1]{3,2,4,1,0:T(8,128)S(1)}, f32[2,2,16,32,1]{3,2,4,1,0:T(8,128)S(1)}, u32[]{:S(2)}, u32[]{:S(2)}) collective-permute-start(f32[2,2,16,32,1]{3,2,4,1,0:T(8,128)S(1)} %copy.296), channel_id=1, source_target_pairs={{1,0},{2,1},{3,2},{4,3},{5,4},{6,5},{7,6},{0,7},{9,8},{10,9},{11,1... | collective-permute-start | bytes 24584 | tf_op jit(solution)/shard_map/ppermute | solution.py:19
  16.0 15.3 %collective-permute-start.1 = (f32[2,2,16,1,128]{4,2,3,1,0:T(8,128)S(1)}, f32[2,2,16,1,128]{4,2,3,1,0:T(8,128)S(1)}, u32[]{:S(2)}, u32[]{:S(2)}) collective-permute-start(f32[2,2,16,1,128]{4,2,3,1,0:T(8,128)S(1)} %bitcast.311), channel_id=1, source_target_pairs={{8,0},{16,8},{24,16},{32,24},{40,32},{48,40},{56,48},{64,56},{72,6... | collective-permute-start | bytes 98312 | tf_op jit(solution)/shard_map/ppermute | solution.py:19
  29.8 1.6 copy-start.4
  31.8 1.6 copy-start.7
  32.4 1.4 copy-start.15
  32.4 1.4 copy-start.17
  38.9 6.4 %collective-permute-start.2 = (f32[2,2,16,32,1]{3,2,4,1,0:T(8,128)S(1)}, f32[2,2,16,32,1]{3,2,4,1,0:T(8,128)S(1)}, u32[]{:S(2)}, u32[]{:S(2)}) collective-permute-start(f32[2,2,16,32,1]{3,2,4,1,0:T(8,128)S(1)} %copy.311), channel_id=1, source_target_pairs={{7,0},{0,1},{1,2},{2,3},{3,4},{4,5},{5,6},{6,7},{15,8},{8,9},{9,10... | collective-permute-start | bytes 24584 | tf_op jit(solution)/shard_map/ppermute | solution.py:19
  39.6 2.7 copy-start.35
  39.6 3.5 %copy-start.34 = (f32[2,16,32,128]{3,2,1,0:T(8,128)S(1)}, f32[2,16,32,128]{3,2,1,0:T(8,128)}, u32[]{:S(2)}) copy-start(f32[2,16,32,128]{3,2,1,0:T(8,128)} %get-tuple-element.29) | copy-start | bytes 1572868
  40.8 9.3 %collective-permute-start.3 = (f32[2,2,16,1,128]{4,2,3,1,0:T(8,128)S(1)}, f32[2,2,16,1,128]{4,2,3,1,0:T(8,128)S(1)}, u32[]{:S(2)}, u32[]{:S(2)}) collective-permute-start(f32[2,2,16,1,128]{4,2,3,1,0:T(8,128)S(1)} %bitcast.313), channel_id=1, source_target_pairs={{248,0},{0,8},{8,16},{16,24},{24,32},{32,40},{40,48},{48,56},{56,6... | collective-permute-start | bytes 98312 | tf_op jit(solution)/shard_map/ppermute | solution.py:19
  48.2 1.5 copy-start.26
  48.2 1.5 copy-start.28
  49.7 1.2 copy-start.3
  51.0 1.0 copy-start.41
  51.0 1.2 copy-start.43
  58.4 13.4 %collective-permute-start.4 = (f32[2,2,16,32,1]{3,2,4,1,0:T(8,128)S(1)}, f32[2,2,16,32,1]{3,2,4,1,0:T(8,128)S(1)}, u32[]{:S(2)}, u32[]{:S(2)}) collective-permute-start(f32[2,2,16,32,1]{3,2,4,1,0:T(8,128)S(1)} %copy.325), channel_id=1, source_target_pairs={{1,0},{2,1},{3,2},{4,3},{5,4},{6,5},{7,6},{0,7},{9,8},{10,9},{11,1... | collective-permute-start | bytes 24584 | tf_op jit(solution)/shard_map/ppermute | solution.py:19
  65.2 5.0 %copy-start.37 = (f32[2,16,32,128]{3,2,1,0:T(8,128)S(1)}, f32[2,16,32,128]{3,2,1,0:T(8,128)}, u32[]{:S(2)}) copy-start(f32[2,16,32,128]{3,2,1,0:T(8,128)} %get-tuple-element.22) | copy-start | bytes 1572868
  65.2 5.8 %copy-start.36 = (f32[2,16,32,128]{3,2,1,0:T(8,128)S(1)}, f32[2,16,32,128]{3,2,1,0:T(8,128)}, u32[]{:S(2)}) copy-start(f32[2,16,32,128]{3,2,1,0:T(8,128)} %get-tuple-element.23) | copy-start | bytes 1572868
  66.4 9.9 %collective-permute-start.5 = (f32[2,2,16,1,128]{4,2,3,1,0:T(8,128)S(1)}, f32[2,2,16,1,128]{4,2,3,1,0:T(8,128)S(1)}, u32[]{:S(2)}, u32[]{:S(2)}) collective-permute-start(f32[2,2,16,1,128]{4,2,3,1,0:T(8,128)S(1)} %bitcast.314), channel_id=1, source_target_pairs={{8,0},{16,8},{24,16},{32,24},{40,32},{48,40},{56,48},{64,56},{72,6... | collective-permute-start | bytes 98312 | tf_op jit(solution)/shard_map/ppermute | solution.py:19
  74.7 1.6 copy-start.5
  74.7 1.9 copy-start.6
  76.6 1.0 copy-start.40
  76.6 1.2 copy-start.42
  77.7 1.4 copy-start.8
  77.7 1.5 copy-start.16
  77.7 1.7 copy-start.18
  77.8 1.8 copy-start.20
  80.1 17.7 %copy-start.1 = (f32[2,3,16,32,128]{4,3,2,1,0:T(8,128)}, f32[2,3,16,32,128]{4,3,2,1,0:T(8,128)S(1)}, u32[]{:S(2)}) copy-start(f32[2,3,16,32,128]{4,3,2,1,0:T(8,128)S(1)} %fusion.2) | copy-start | bytes 4718596
  85.5 6.4 %collective-permute-start.6 = (f32[2,2,16,32,1]{3,2,4,1,0:T(8,128)S(1)}, f32[2,2,16,32,1]{3,2,4,1,0:T(8,128)S(1)}, u32[]{:S(2)}, u32[]{:S(2)}) collective-permute-start(f32[2,2,16,32,1]{3,2,4,1,0:T(8,128)S(1)} %copy.338), channel_id=1, source_target_pairs={{7,0},{0,1},{1,2},{2,3},{3,4},{4,5},{5,6},{6,7},{15,8},{8,9},{9,10... | collective-permute-start | bytes 24584 | tf_op jit(solution)/shard_map/ppermute | solution.py:19
  86.4 1.2 copy-start.33
  86.4 2.0 copy-start.32
  87.5 9.2 %collective-permute-start.7 = (f32[2,2,16,1,128]{4,2,3,1,0:T(8,128)S(1)}, f32[2,2,16,1,128]{4,2,3,1,0:T(8,128)S(1)}, u32[]{:S(2)}, u32[]{:S(2)}) collective-permute-start(f32[2,2,16,1,128]{4,2,3,1,0:T(8,128)S(1)} %bitcast.312), channel_id=1, source_target_pairs={{248,0},{0,8},{8,16},{16,24},{24,32},{32,40},{40,48},{48,56},{56,6... | collective-permute-start | bytes 98312 | tf_op jit(solution)/shard_map/ppermute | solution.py:19
  94.8 1.5 copy-start.22
  94.8 1.5 copy-start.24
  96.3 1.2 copy-start.2
  97.6 1.0 copy-start.38
  97.6 1.2 copy-start.39
  98.8 1.0 copy-start.10
  98.8 1.2 copy-start.12
  98.8 1.4 copy-start.14
  100.7 4.2 %copy-start.44 = (f32[2,3,16,32,128]{4,3,2,1,0:T(8,128)}, f32[2,3,16,32,128]{4,3,2,1,0:T(8,128)S(1)}, u32[]{:S(2)}) copy-start(f32[2,3,16,32,128]{4,3,2,1,0:T(8,128)S(1)} %fusion.3) | copy-start | bytes 4718596
  106.3 190.2 %reduce-scatter.7.cloned.1.call-start = ((), (), s32[]{:S(2)}) async-start(), calls=%async_computation.3 | async-start | bytes 147456
  (12 other events, 10.2 us)
Sparse Core Ops, SparseCore 0:
  106.4 113.6 reduce-scatter.4
  224.4 72.0 reduce-scatter.6
where the time goes:
time: 306 us; the launch traced here: 305 us
  waiting for transfers between devices  192 us (63%)
  local copies, waits for them, and re-layouts  47.9 us (16%)
  other arithmetic  25.4 us (8%)
  between operations  18.3 us (6%)
  starting transfers between devices  17.1 us (6%)
  matrix products  4.12 us (1%)
    reduce_scatter x1, waiting for transfers between devices, shards(): lax.psum_scatter(x_section(spread, xcos, xsin), 'gx', scatter_dimension=0...  114 us
    unnamed x3, waiting for transfers between devices  74.2 us
    unnamed x105, local copies, waits for them, and re-layouts  17.2 us
    ppermute x8, starting transfers between devices, passed_along(): return lax.ppermute(block, axis, route)  17 us
    another operation x6, other arithmetic, pair_xz(): return jnp.stack([values[:, 0], values[:, 2]], axis=1)  7.68 us
  transfers between devices with their start and end apart: 10, of which 4 were waited for; matrix products, arithmetic and copies ran while one was open for 12% of the time, Pallas kernels for 0%

commit v1 on v0

v1 whole, which is shorter than its diff:
```python
import math

import jax
import jax.numpy as jnp
from jax import lax
from jax.experimental import pallas as pl
from jax.experimental.pallas import tpu as pltpu
from jax.sharding import PartitionSpec as P

STEP_DT = 0.5
ORD_X = 256
ORD_Y = 256
NZ = 16
ROWS = 32
COLS = 128
EXT = 40
MAIN_BLOCKS = 52
EDGE_BLOCKS = 58
VMEM = pltpu.VMEM
SMEM = pltpu.SMEM


def passed_along(block, axis, distance):
    devices = range(lax.axis_size(axis))
    route = [((i - distance) % len(devices), i) for i in devices]
    return lax.ppermute(block, axis, route)


def roll(values, shift, axis):
    size = values.shape[axis]
    if isinstance(shift, int):
        shift = shift % size
        if shift == 0:
            return values
    return pltpu.roll(values, shift, axis)


def lanes_of(shape):
    return lax.broadcasted_iota(jnp.int32, shape, len(shape) - 1)


def coef_table(base_ref, mode_ref, node_ref):
    lane = lanes_of((8, 128))
    material = lane // 16
    pattern = lane % 16
    base = jnp.zeros((8, 128), jnp.float32)
    for m in range(8):
        base = jnp.where(material == m, base_ref[m], base)
    change = jnp.zeros((8, 128), jnp.float32)
    for k in range(4):
        mode = jnp.zeros((8, 128), jnp.float32)
        for p in range(16):
            mode = jnp.where(pattern == p, mode_ref[k, p], mode)
        change = change + node_ref[k] * mode
    return STEP_DT / (base * (1.0 + change))


def look_up(table, pair):
    rows = [
        jnp.take_along_axis(table, pair[8 * r : 8 * r + 8], axis=1)
        for r in range(pair.shape[0] // 8)
    ]
    return jnp.concatenate(rows, axis=0)


def pack_kernel(
    e_ref,
    h_ref,
    material_ref,
    pattern_ref,
    base_ref,
    mode_ref,
    node_ref,
    coef_ref,
    own_ref,
    right_ref,
    left_ref,
    first_ref,
    last_ref,
):
    table = coef_table(base_ref, mode_ref, node_ref)
    lane = lanes_of((ROWS, COLS))
    group = lane // 8
    place = lane % 8

    def coef_plane(z, carry):
        pair = material_ref[z] * 16 + pattern_ref[z]
        coef_ref[z] = look_up(table, pair)
        return carry

    lax.fori_loop(0, NZ, coef_plane, 0)

    def plane(index, z):
        if index == 12:
            return coef_ref.at[z]
        ref = e_ref if index < 6 else h_ref
        return ref.at[(index % 6) // 3, index % 3, z]

    for index in range(13):
        packed = jnp.zeros((ROWS, COLS), jnp.float32)
        for z in range(NZ):
            values = plane(index, z)[...]
            packed = jnp.where(group == z, roll(values, 8 * z + 6, 1), packed)
            block = index * 4 + z // 4
            slot = 2 * (z % 4)
            first_ref[block, slot : slot + 2, :] = values[0:2]
            last_ref[block, slot : slot + 2, :] = values[ROWS - 2 : ROWS]
        own_ref[index] = packed
        block = MAIN_BLOCKS + index // 4
        slot = 2 * (index % 4)
        first_ref[block, slot : slot + 2, :] = packed[0:2]
        last_ref[block, slot : slot + 2, :] = packed[ROWS - 2 : ROWS]
    for c in range(3):
        e_re, e_im, h_re, h_im = (own_ref[3 * k + c] for k in range(4))
        right_ref[c] = jnp.where(
            place < 4,
            jnp.where(place < 2, roll(h_re, -4, 1), roll(h_im, -2, 1)),
            jnp.where(place < 6, e_re, roll(e_im, 2, 1)),
        )
        left_ref[c] = jnp.where(
            place < 4,
            jnp.where(place < 2, roll(h_im, -6, 1), roll(h_re, -4, 1)),
            jnp.where(place < 6, roll(e_im, -2, 1), e_re),
        )
    right_ref[3] = own_ref[12]
    left_ref[3] = own_ref[12]


def turned(re, im, cos, sin):
    return re * cos - im * sin, im * cos + re * sin


def strip_of(own, right, left, rot):
    place = lanes_of(own[0].shape) % 8

    def joined(index, from_right, from_left):
        return jnp.where(
            place < 4,
            jnp.where(place < 2, roll(own[index], -4, 1), from_left),
            jnp.where(place < 6, from_right, own[index]),
        )

    strip = [None] * 13
    for c in range(3):
        r = right[c]
        l = left[c]
        e_right = turned(r, roll(r, -2, 1), rot[4], rot[5])
        h_right = turned(roll(r, 4, 1), roll(r, 2, 1), rot[4], rot[5])
        e_left = turned(roll(l, -4, 1), roll(l, -2, 1), rot[6], rot[7])
        h_left = turned(l, roll(l, 2, 1), rot[6], rot[7])
        for part in range(2):
            strip[3 * part + c] = joined(3 * part + c, e_right[part], e_left[part])
            strip[6 + 3 * part + c] = joined(6 + 3 * part + c, h_right[part], h_left[part])
    strip[12] = joined(12, right[3], roll(left[3], -4, 1))
    return strip


def next_row(values):
    return roll(values, -1, 0)


def prev_row(values):
    return roll(values, 1, 0)


def h_new(h, e, e_up, e_xn, e_yn):
    return (
        h[0] - STEP_DT * (e_yn[1] - e[2] - (e_up[1] - e[1])),
        h[1] - STEP_DT * (e_up[0] - e[0] - (e_xn[1] - e[2])),
        h[2] - STEP_DT * (e_xn[0] - e[1] - (e_yn[0] - e[0])),
    )


def e_new(e, h, h_down, h_xp, h_yp, coef):
    return (
        e[0] + coef * (h[2] - h_yp[1] - (h[1] - h_down[1])),
        e[1] + coef * (h[0] - h_down[0] - (h[2] - h_xp[1])),
        e[2] + coef * (h[1] - h_xp[0] - (h[0] - h_yp[0])),
    )


def strip_h(h, e):
    up = lanes_of((EXT, COLS)) < 8 * (NZ - 1)
    above = [jnp.where(up, roll(e[c], -8, 1), 0.0) for c in range(2)]
    return h_new(
        h,
        e,
        above,
        (next_row(e[1]), next_row(e[2])),
        (roll(e[0], -1, 1), roll(e[2], -1, 1)),
    )


def strip_e(e, h, coef):
    up = lanes_of((EXT, COLS)) >= 8
    below = [jnp.where(up, roll(h[c], 8, 1), 0.0) for c in range(2)]
    return e_new(
        e,
        h,
        below,
        (prev_row(h[1]), prev_row(h[2])),
        (roll(h[0], 1, 1), roll(h[2], 1, 1)),
        coef,
    )


def field_kernel(
    e_hbm,
    h_hbm,
    coef_ref,
    own_ref,
    right_ref,
    left_ref,
    next_ref,
    prev_ref,
    rot_ref,
    monitor_ref,
    wave_ref,
    e_out,
    h_out,
    spread_ref,
    e_all,
    h_all,
    coef_all,
    strip_ref,
    edge_ref,
    sem,
):
    load_e = pltpu.make_async_copy(e_hbm, e_all.at[:, :, 0:NZ, 0:ROWS, :], sem.at[0])
    load_h = pltpu.make_async_copy(h_hbm, h_all.at[:, :, 1 : NZ + 1, 0:ROWS, :], sem.at[1])
    load_e.start()
    load_h.start()
    rot = [rot_ref[k] for k in range(8)]

    for part in range(2):
        for c in range(3):
            e_all[part, c, NZ] = jnp.zeros((EXT, COLS), jnp.float32)
            h_all[part, c, 0] = jnp.zeros((EXT, COLS), jnp.float32)
    for ref, row, cos, sin in ((next_ref, 32, rot[0], rot[1]), (prev_ref, 38, rot[2], rot[3])):
        for field in range(2):
            for c in range(3):
                for quad in range(4):
                    re = ref[(6 * field + c) * 4 + quad]
                    im = ref[(6 * field + 3 + c) * 4 + quad]
                    for part, values in enumerate(turned(re, im, cos, sin)):
                        for k in range(4):
                            dest = h_all if field else e_all
                            z = 4 * quad + k + field
                            dest[part, c, z, row : row + 2, :] = values[2 * k : 2 * k + 2]
        for quad in range(4):
            values = ref[48 + quad]
            for k in range(4):
                coef_all[4 * quad + k, row : row + 2, :] = values[2 * k : 2 * k + 2]
        pieces = [
            ref[MAIN_BLOCKS + a // 4, 2 * (a % 4) : 2 * (a % 4) + 2, :] for a in range(24)
        ]
        strip = strip_of(pieces[0:13], pieces[16:20], pieces[20:24], rot)
        for field in range(2):
            for c in range(3):
                for part, values in enumerate(
                    turned(strip[6 * field + c], strip[6 * field + 3 + c], cos, sin)
                ):
                    strip_ref[6 * field + 3 * part + c, row : row + 2, :] = values
        strip_ref[12, row : row + 2, :] = strip[12]
    strip = strip_of(
        [own_ref[a] for a in range(13)],
        [right_ref[a] for a in range(4)],
        [left_ref[a] for a in range(4)],
        rot,
    )
    for a in range(13):
        strip_ref[a, 0:ROWS, :] = strip[a]
    for z in range(NZ):
        coef_all[z, 0:ROWS, :] = coef_ref[z]

    strip_coef = strip_ref[12]
    for part in range(2):
        e = tuple(strip_ref[3 * part + c] for c in range(3))
        h = tuple(strip_ref[6 + 3 * part + c] for c in range(3))
        for step in range(2):
            edge_ref[part, 2 * step, 0] = e[0]
            edge_ref[part, 2 * step, 1] = e[2]
            h = strip_h(h, e)
            edge_ref[part, 2 * step + 1, 0] = h[0]
            edge_ref[part, 2 * step + 1, 1] = h[2]
            if step == 0:
                e = strip_e(e, h, strip_coef)

    lane = lanes_of((EXT, COLS))

    def next_col(values, edge, z):
        arrived = roll(edge, lax.rem(COLS + 125 - 8 * z, COLS), 1)
        return jnp.where(lane == COLS - 1, arrived, roll(values, -1, 1))

    def prev_col(values, edge, z):
        arrived = roll(edge, lax.rem(COLS + 123 - 8 * z, COLS), 1)
        return jnp.where(lane == 0, arrived, roll(values, 1, 1))

    def do_h(step, z):
        for part in range(2):
            e = tuple(e_all[part, c, z] for c in range(3))
            h = tuple(h_all[part, c, z + 1] for c in range(3))
            e_up = (e_all[part, 0, z + 1], e_all[part, 1, z + 1])
            e_yn = (
                next_col(e[0], edge_ref[part, 2 * step, 0], z),
                next_col(e[2], edge_ref[part, 2 * step, 1], z),
            )
            new = h_new(h, e, e_up, (next_row(e[1]), next_row(e[2])), e_yn)
            for c in range(3):
                h_all[part, c, z + 1] = new[c]

    def do_e(step, z):
        coef = coef_all[z]
        for part in range(2):
            e = tuple(e_all[part, c, z] for c in range(3))
            h = tuple(h_all[part, c, z + 1] for c in range(3))
            h_down = (h_all[part, 0, z], h_all[part, 1, z])
            h_yp = (
                prev_col(h[0], edge_ref[part, 2 * step + 1, 0], z),
                prev_col(h[2], edge_ref[part, 2 * step + 1, 1], z),
            )
            new = e_new(e, h, h_down, (prev_row(h[1]), prev_row(h[2])), h_yp, coef)
            for c in range(3):
                e_all[part, c, z] = new[c]

    load_e.wait()
    load_h.wait()

    def sweep(update, step):
        def body(z, carry):
            update(step, z)
            return carry

        lax.fori_loop(0, NZ, body, 0)

    for step in range(2):
        sweep(do_h, step)
        if step == 1:
            store_h = pltpu.make_async_copy(
                h_all.at[:, :, 1 : NZ + 1, 0:ROWS, :], h_out, sem.at[1]
            )
            store_h.start()
        sweep(do_e, step)
    store_e = pltpu.make_async_copy(e_all.at[:, :, 0:NZ, 0:ROWS, :], e_out, sem.at[0])
    store_e.start()

    level = monitor_ref[0]
    re = jnp.concatenate([e_all[0, c, level, 0:ROWS, :] for c in range(2)], axis=0)
    im = jnp.concatenate([e_all[1, c, level, 0:ROWS, :] for c in range(2)], axis=0)
    y_section(re, im, wave_ref, spread_ref)
    store_h.wait()
    store_e.wait()


def y_section(re, im, wave_ref, spread_ref):
    wave = wave_ref[...]
    owners, _, lanes = spread_ref.shape
    each = lanes // 4
    out = [
        jnp.dot(
            jnp.concatenate(pair, axis=1),
            wave,
            precision=lax.Precision.HIGHEST,
            preferred_element_type=jnp.float32,
        )
        for pair in ((re, im), (im, -re))
    ]
    for owner in range(owners):
        pieces = [
            out[part][c * ROWS : (c + 1) * ROWS, owner * each : (owner + 1) * each]
            for part in range(2)
            for c in range(2)
        ]
        spread_ref[owner] = jnp.concatenate(pieces, axis=1)


def x_kernel(got_ref, wave_ref, part_ref):
    total = got_ref[0]
    for source in range(1, got_ref.shape[0]):
        total = total + got_ref[source]
    half = total.shape[1] // 2
    other = roll(total, half, 1)
    other = jnp.where(lanes_of(other.shape) < half, other, -other)
    result = jnp.dot(
        wave_ref[...],
        jnp.concatenate([total, other], axis=0),
        precision=lax.Precision.HIGHEST,
        preferred_element_type=jnp.float32,
    )
    part_ref[...] = result.reshape(part_ref.shape)


def sum_kernel(got_ref, out_ref):
    total = got_ref[0]
    for source in range(1, got_ref.shape[0]):
        total = total + got_ref[source]
    each = total.shape[1] // 4
    for c in range(2):
        for part in range(2):
            start = (2 * part + c) * each
            out_ref[c, part] = total[:, start : start + each]


def angles(count, half, offset, length, total, theta, order_axis):
    shape = (count, length) if order_axis == 0 else (length, count)
    order_index = lax.broadcasted_iota(jnp.int32, shape, order_axis) - half
    place = offset + lax.broadcasted_iota(jnp.int32, shape, 1 - order_axis)
    product = jnp.mod(order_index * place, total)
    return (
        2.0 * math.pi * product.astype(jnp.float32) + theta * place.astype(jnp.float32)
    ) / total


def f32(*shape):
    return jax.ShapeDtypeStruct(shape, jnp.float32)


def shards(
    e_field, h_field, material, pattern, base_eps, mode_table, nodes, bloch_phase, monitor_z
):
    count_x = lax.axis_size("gx")
    count_y = lax.axis_size("gy")
    index_x = lax.axis_index("gx")
    index_y = lax.axis_index("gy")
    total_x = ROWS * count_x
    total_y = COLS * count_y
    each_p = ORD_X // count_x
    each_q = ORD_Y // count_y
    vmem = pl.BlockSpec(memory_space=VMEM)
    smem = pl.BlockSpec(memory_space=SMEM)
    hbm = pl.BlockSpec(memory_space=pl.ANY)

    cos_x, sin_x = jnp.cos(bloch_phase[0]), jnp.sin(bloch_phase[0])
    cos_y, sin_y = jnp.cos(bloch_phase[1]), jnp.sin(bloch_phase[1])
    last_x = index_x == count_x - 1
    last_y = index_y == count_y - 1
    rot = jnp.stack(
        [
            jnp.where(last_x, cos_x, 1.0),
            jnp.where(last_x, sin_x, 0.0),
            jnp.where(index_x == 0, cos_x, 1.0),
            jnp.where(index_x == 0, -sin_x, 0.0),
            jnp.where(index_y == 0, cos_y, 1.0),
            jnp.where(index_y == 0, -sin_y, 0.0),
            jnp.where(last_y, cos_y, 1.0),
            jnp.where(last_y, sin_y, 0.0),
        ]
    )
    y_angle = angles(
        ORD_Y, ORD_Y // 2, index_y * COLS, COLS, total_y, bloch_phase[1], 1
    )
    scale = 1.0 / math.sqrt(total_x * total_y)
    y_wave = jnp.concatenate([jnp.cos(y_angle), jnp.sin(y_angle)], axis=0) * scale
    x_angle = angles(
        ORD_X, ORD_X // 2, index_x * ROWS, ROWS, total_x, bloch_phase[0], 0
    )
    x_wave = jnp.concatenate([jnp.cos(x_angle), jnp.sin(x_angle)], axis=1)

    coef, own, right, left, first, last = pl.pallas_call(
        pack_kernel,
        out_shape=(
            f32(NZ, ROWS, COLS),
            f32(13, ROWS, COLS),
            f32(4, ROWS, COLS),
            f32(4, ROWS, COLS),
            f32(EDGE_BLOCKS, 8, COLS),
            f32(EDGE_BLOCKS, 8, COLS),
        ),
        in_specs=[vmem] * 4 + [smem] * 3,
        out_specs=(vmem,) * 6,
        compiler_params=pltpu.CompilerParams(vmem_limit_bytes=32 << 20),
        name="pack",
    )(e_field, h_field, material, pattern, base_eps, mode_table, nodes)
    from_right = passed_along(right, "gy", 1)
    from_left = passed_along(left, "gy", -1)
    corner_first = jnp.concatenate([from_right[:, 0:2], from_left[:, 0:2]]).reshape(2, 8, COLS)
    corner_last = jnp.concatenate(
        [from_right[:, ROWS - 2 :], from_left[:, ROWS - 2 :]]
    ).reshape(2, 8, COLS)
    first = lax.dynamic_update_slice(first, corner_first, (EDGE_BLOCKS - 2, 0, 0))
    last = lax.dynamic_update_slice(last, corner_last, (EDGE_BLOCKS - 2, 0, 0))
    from_next = passed_along(first, "gx", -1)
    from_prev = passed_along(last, "gx", 1)

    e_out, h_out, spread = pl.pallas_call(
        field_kernel,
        out_shape=(
            f32(*e_field.shape),
            f32(*h_field.shape),
            f32(count_y, ROWS, 4 * each_q),
        ),
        in_specs=[hbm, hbm] + [vmem] * 6 + [smem, smem, vmem],
        out_specs=(hbm, hbm, vmem),
        scratch_shapes=[
            VMEM((2, 3, NZ + 1, EXT, COLS), jnp.float32),
            VMEM((2, 3, NZ + 1, EXT, COLS), jnp.float32),
            VMEM((NZ, EXT, COLS), jnp.float32),
            VMEM((13, EXT, COLS), jnp.float32),
            VMEM((2, 4, 2, EXT, COLS), jnp.float32),
            pltpu.SemaphoreType.DMA((2,)),
        ],
        compiler_params=pltpu.CompilerParams(vmem_limit_bytes=32 << 20),
        name="fields",
    )(
        e_field,
        h_field,
        coef,
        own,
        from_right,
        from_left,
        from_next,
        from_prev,
        rot,
        monitor_z,
        y_wave,
    )
    got = lax.all_to_all(spread, "gy", 0, 0, tiled=True)
    partial = pl.pallas_call(
        x_kernel,
        out_shape=f32(count_x, each_p, 4 * each_q),
        in_specs=[vmem, vmem],
        out_specs=vmem,
        name="x_section",
    )(got, x_wave)
    got = lax.all_to_all(partial, "gx", 0, 0, tiled=True)
    orders = pl.pallas_call(
        sum_kernel,
        out_shape=f32(2, 2, each_p, each_q),
        in_specs=[vmem],
        out_specs=vmem,
        name="order_sum",
    )(got)
    return e_out, h_out, orders


def solution(mesh):
    grid = P(None, None, None, "gx", "gy")
    cells = P(None, "gx", "gy")
    return jax.shard_map(
        shards,
        mesh=mesh,
        in_specs=(grid, grid, cells, cells, P(), P(), P(), P(), P()),
        out_specs=(grid, grid, P(None, None, "gx", "gy")),
        check_vma=False,
    )
```

time: 306 us -> 87.2 us (0.28)
  waiting for transfers between devices: 192 us -> 5.23 us
  local copies, waits for them, and re-layouts: 47.9 us -> 15.4 us
  blocking collectives: 0 us -> 21.4 us
  other arithmetic: 25.4 us -> 6.41 us
  Pallas kernels: 0 us -> 18.5 us
  between operations: 18.3 us -> 4.31 us
  matrix products: 4.12 us -> 0 us
    reduce_scatter x1 -> x0, waiting for transfers between devices: 114 us -> none  [shards(): lax.psum_scatter(x_section(spread, xcos, xsin), 'gx', scatter_dimension=0...]
    unnamed x3 -> x0, waiting for transfers between devices: 74.2 us -> none
    all_to_all x0 -> x1, blocking collectives: none -> 21.4 us  [shards(): got = lax.all_to_all(partial, 'gx', 0, 0, tiled=True)]
    pallas_call x0 -> x4, Pallas kernels: none -> 18.5 us  [the longest x1 11.4 us: shards(): pl.pallas_call(field_kernel, out_shape=(f32(*e_field.shape), f32(*h_field...]
    slice x21 -> x3, local copies, waits for them, and re-layouts: 15.6 us -> 0.6 us  [the longest x1 0.58 us: shards(): cos_y, sin_y = (jnp.cos(bloch_phase[1]), jnp.sin(bloch_phase[1]))]
    another operation x19 -> x0, other arithmetic: 10.8 us -> none  [the longest x6 7.68 us: pair_xz(): return jnp.stack([values[:, 0], values[:, 2]], axis=1)]
    ppermute x8 -> x4, starting transfers between devices: 17 us -> 8.89 us  [passed_along(): return lax.ppermute(block, axis, route)]
    all_to_all x0 -> x1, starting transfers between devices: none -> 6.47 us  [shards(): got = lax.all_to_all(spread, 'gy', 0, 0, tiled=True)]
  transfers between devices with their start and end apart: 10 -> 5, of which waited for: 4 -> 1; matrix products, arithmetic and copies ran while one was open for 12% -> 11% of each run, Pallas kernels for 0% -> 0%
where the time goes in v1:
time: 87.2 us; the launch traced here: 86.5 us
  blocking collectives  21.4 us (25%)
  Pallas kernels  18.5 us (21%)
  local copies, waits for them, and re-layouts  15.4 us (18%)
  starting transfers between devices  15.4 us (18%)
  other arithmetic  6.41 us (7%)
  waiting for transfers between devices  5.23 us (6%)
  between operations  4.31 us (5%)
    all_to_all x1, blocking collectives, shards(): got = lax.all_to_all(partial, 'gx', 0, 0, tiled=True)  21.4 us
    unnamed x34, local copies, waits for them, and re-layouts  12 us
    pallas_call x1, Pallas kernels, shards(): pl.pallas_call(field_kernel, out_shape=(f32(*e_field.shape), f32(*h_field...  11.4 us
    ppermute x4, starting transfers between devices, passed_along(): return lax.ppermute(block, axis, route)  8.89 us
    all_to_all x1, starting transfers between devices, shards(): got = lax.all_to_all(spread, 'gy', 0, 0, tiled=True)  6.47 us
    all_to_all x1, waiting for transfers between devices, shards(): got = lax.all_to_all(spread, 'gy', 0, 0, tiled=True)  5.22 us
    pallas_call x1, Pallas kernels, shards(): pl.pallas_call(pack_kernel, out_shape=(f32(NZ, ROWS, COLS), f32(13, ROWS,...  3.51 us
    cos x1, other arithmetic, shards(): x_wave = jnp.concatenate([jnp.cos(x_angle), jnp.sin(x_angle)], axis=1)  2.08 us
  transfers between devices with their start and end apart: 5, of which 1 were waited for; matrix products, arithmetic and copies ran while one was open for 11% of the time, Pallas kernels for 0%

profile of v1, /device:TPU:1, one launch (start us, length us, event | category | flops | bytes accessed | tf_op | source)
XLA Modules:
  0.0 86.5 jit_solution(1655682705711394013)
XLA Ops:
  0.6 0.0 copy-start
  0.6 1.4 %copy-done = f32[2,3,16,32,128]{4,3,2,1,0:T(8,128)S(1)} copy-done((f32[2,3,16,32,128]{4,3,2,1,0:T(8,128)S(1)}, f32[2,3,16,32,128]{4,3,2,1,0:T(8,128)}, u32[]{:S(2)}) %copy-start) | copy-done | bytes 1572888
  2.0 0.0 copy-start.2
  2.0 1.4 %copy-done.2 = f32[2,3,16,32,128]{4,3,2,1,0:T(8,128)S(1)} copy-done((f32[2,3,16,32,128]{4,3,2,1,0:T(8,128)S(1)}, f32[2,3,16,32,128]{4,3,2,1,0:T(8,128)}, u32[]{:S(2)}) %copy-start.2) | copy-done | bytes 1572888
  3.5 0.0 copy-start.6
  3.5 0.9 %copy-done.6 = s32[16,32,128]{2,1,0:T(8,128)S(1)} copy-done((s32[16,32,128]{2,1,0:T(8,128)S(1)}, s32[16,32,128]{2,1,0:T(8,128)}, u32[]{:S(2)}) %copy-start.6) | copy-done | bytes 262168
  4.4 0.0 copy-start.7
  4.4 0.9 %copy-done.7 = s32[16,32,128]{2,1,0:T(8,128)S(1)} copy-done((s32[16,32,128]{2,1,0:T(8,128)S(1)}, s32[16,32,128]{2,1,0:T(8,128)}, u32[]{:S(2)}) %copy-start.7) | copy-done | bytes 262168
  5.4 0.7 copy-done.10
  6.0 0.7 copy-done.11
  6.7 0.7 copy-done.12
  7.4 3.5 %pack.1 = (f32[16,32,128]{2,1,0:T(8,128)S(1)}, f32[13,32,128]{2,1,0:T(8,128)S(1)}, f32[4,32,128]{2,1,0:T(8,128)}, f32[4,32,128]{2,1,0:T(8,128)}, f32[58,8,128]{2,1,0:T(8,128)S(1)}, /*index=5*/f32[58,8,128]{2,1,0:T(8,128)S(1)}) custom-call(f32[2,3,16,32,128]{4,3,2,1,0:T(8,128)S(1)} %copy-done, f32[2,3,16,32,128]{4,3,2,1,0:T(8,128)S(1)} %copy-done.2, ...), custom_call_target="tpu_custom_call" | custom-call | tf_op jit(solution)/shard_map/pack/pallas_call | solution.py:459
  10.9 0.7 copy-done.4
  11.6 0.7 copy-done.8
  12.3 0.7 copy-done.13
  12.9 0.7 copy-done.14
  13.6 2.1 %collective-permute-start = (f32[4,32,128]{2,1,0:T(8,128)}, f32[4,32,128]{2,1,0:T(8,128)S(1)}, u32[]{:S(2)}, u32[]{:S(2)}) collective-permute-start(f32[4,32,128]{2,1,0:T(8,128)} %get-tuple-element.14), channel_id=1, source_target_pairs={{7,0},{0,1},{1,2},{2,3},{3,4},{4,5},{5,6},{6,7},{15,8},{8,9},{9,10... | collective-permute-start | bytes 196616 | tf_op jit(solution)/shard_map/ppermute | solution.py:26
  15.8 3.9 %collective-permute-start.1 = (f32[4,32,128]{2,1,0:T(8,128)}, f32[4,32,128]{2,1,0:T(8,128)S(1)}, u32[]{:S(2)}, u32[]{:S(2)}) collective-permute-start(f32[4,32,128]{2,1,0:T(8,128)} %get-tuple-element.15), channel_id=1, source_target_pairs={{1,0},{2,1},{3,2},{4,3},{5,4},{6,5},{7,6},{0,7},{9,8},{10,9},{11,1... | collective-permute-start | bytes 196616 | tf_op jit(solution)/shard_map/ppermute | solution.py:26
  19.7 0.0 copy-done.16
  19.7 0.6 fusion.13
  20.3 0.6 convert_multiply_fusion.1
  20.9 0.7 fusion.9
  21.6 0.6 fusion.8
  22.2 0.0 collective-permute-done.right_ref
  22.3 0.0 collective-permute-done.1.left_ref
  22.3 0.6 bitcast_dynamic-update-slice_fusion
  22.9 2.6 %collective-permute-start.3 = (f32[58,8,128]{2,1,0:T(8,128)}, f32[58,8,128]{2,1,0:T(8,128)}, u32[]{:S(2)}, u32[]{:S(2)}) collective-permute-start(f32[58,8,128]{2,1,0:T(8,128)} %bitcast_dynamic-update-slice_fusion), channel_id=1, source_target_pairs={{248,0},{0,8},{8,16},{16,24},{24,32},{32,40},{40,48},{48,56},{56,6... | collective-permute-start | bytes 712712 | tf_op jit(solution)/shard_map/ppermute | solution.py:26
  25.6 0.6 bitcast_dynamic-update-slice_fusion.1
  26.2 0.2 collective-permute-start.2
  26.4 0.6 convert_multiply_fusion
  30.6 1.5 %copy.12 = f32[256,32]{1,0:T(8,128)} copy(f32[256,32]{0,1:T(8,128)} %fusion.9) | data formatting | bytes 65536 | tf_op jit(solution)/shard_map/convert_element_type | solution.py:410
  32.1 0.1 stack.35.rot_ref
  32.2 2.1 %fusion.6 = (f32[256,32]{1,0:T(8,128)}, f32[256,32]{1,0:T(8,128)}) fusion(f32[256,32]{1,0:T(8,128)} %copy.12, f32[32]{0:T(128)S(1)} %convert_multiply_fusion), kind=kLoop, calls=%fused_computation.14 | loop fusion | flops 24576 | bytes 98432 | tf_op jit(solution)/shard_map/cos | solution.py:457
  34.2 0.0 collective-permute-done.3.prev_ref
  34.2 0.0 collective-permute-done.2.next_ref
  34.2 0.0 copy-done.3
  34.2 0.0 copy-done.1
  34.3 0.0 copy-start.5
  34.3 0.9 %copy-done.5 = f32[16,32,128]{2,1,0:T(8,128)S(1)} copy-done((f32[16,32,128]{2,1,0:T(8,128)S(1)}, f32[16,32,128]{2,1,0:T(8,128)}, u32[]{:S(2)}) %copy-start.5) | copy-done | bytes 262168
  35.2 0.9 %copy-done.9 = f32[13,32,128]{2,1,0:T(8,128)S(1)} copy-done((f32[13,32,128]{2,1,0:T(8,128)S(1)}, f32[13,32,128]{2,1,0:T(8,128)}, u32[]{:S(2)}) %copy-start.9) | copy-done | bytes 213016
  36.1 11.4 %fields.1 = (f32[2,3,16,32,128]{4,3,2,1,0:T(8,128)}, f32[2,3,16,32,128]{4,3,2,1,0:T(8,128)}, f32[8,32,128]{2,1,0:T(8,128)}) custom-call(f32[2,3,16,32,128]{4,3,2,1,0:T(8,128)S(1)} %copy-done.1, f32[2,3,16,32,128]{4,3,2,1,0:T(8,128)S(1)} %copy-done.3, f32[16,32,128]{2,1,0:T(8,128)S(1)} %copy-done.5, f32[13,32,128]{2,1,0:T(8,128)S(1)} %copy-done.9, ...), custom_call_target="tpu_custom_call" | custom-call | tf_op jit(solution)/shard_map/fields/pallas_call | solution.py:485
  47.5 6.5 %all-to-all-start = ((f32[8,32,128]{2,1,0:T(8,128)}), f32[8,32,128]{2,1,0:T(8,128)S(1)}, u32[]{:S(2)}, u32[]{:S(2)}) async-start(f32[8,32,128]{2,1,0:T(8,128)} %get-tuple-element.20), calls=%async_computation | async-start | bytes 262144 | tf_op jit(solution)/shard_map/all_to_all | solution.py:517
  54.0 1.7 %pad_maximum_fusion.wave_ref = f32[256,64]{1,0:T(8,128)} fusion(f32[256,32]{1,0:T(8,128)} %get-tuple-element.22, f32[256,32]{1,0:T(8,128)} %get-tuple-element.21), kind=kLoop, calls=%fused_computation.11 | loop fusion | flops 16384 | bytes 131072 | tf_op jit(solution)/shard_map/concatenate | solution.py:457
  55.7 5.2 %all-to-all-done.got_ref = f32[8,32,128]{2,1,0:T(8,128)S(1)} async-done(((f32[8,32,128]{2,1,0:T(8,128)}), f32[8,32,128]{2,1,0:T(8,128)S(1)}, u32[]{:S(2)}, u32[]{:S(2)}) %all-to-all-start) | async-done | bytes 131104 | tf_op jit(solution)/shard_map/all_to_all | solution.py:517
  61.0 0.6 copy-done.15
  61.6 1.9 %x_section.1 = f32[32,8,128]{2,1,0:T(8,128)} custom-call(f32[8,32,128]{2,1,0:T(8,128)} %copy-done.15, f32[256,64]{1,0:T(8,128)} %pad_maximum_fusion.wave_ref), custom_call_target="tpu_custom_call" | custom-call | tf_op jit(solution)/shard_map/x_section/pallas_call | solution.py:518
  63.5 21.4 %all_to_all.10.got_ref = f32[32,8,128]{2,1,0:T(8,128)} all-to-all(f32[32,8,128]{2,1,0:T(8,128)} %x_section.1), channel_id=1, replica_groups=mesh['gx'=32,'gy'=8] {'gx'}, dimensions={0} | all-to-all | bytes 262144 | tf_op jit(solution)/shard_map/all_to_all | solution.py:525
  84.9 1.6 %order_sum.1 = f32[2,2,8,32]{3,2,1,0:T(8,128)} custom-call(f32[32,8,128]{2,1,0:T(8,128)} %all_to_all.10.got_ref), custom_call_target="tpu_custom_call" | custom-call | tf_op jit(solution)/shard_map/order_sum/pallas_call | solution.py:526
  (20 shorter events, 0.1 us)
Async XLA Ops:
  0.6 1.4 %copy-start = (f32[2,3,16,32,128]{4,3,2,1,0:T(8,128)S(1)}, f32[2,3,16,32,128]{4,3,2,1,0:T(8,128)}, u32[]{:S(2)}) copy-start(f32[2,3,16,32,128]{4,3,2,1,0:T(8,128)} %e_hbm.1) | copy-start | bytes 4718596
  2.0 1.4 %copy-start.2 = (f32[2,3,16,32,128]{4,3,2,1,0:T(8,128)S(1)}, f32[2,3,16,32,128]{4,3,2,1,0:T(8,128)}, u32[]{:S(2)}) copy-start(f32[2,3,16,32,128]{4,3,2,1,0:T(8,128)} %h_hbm.1) | copy-start | bytes 4718596
  3.5 0.9 %copy-start.6 = (s32[16,32,128]{2,1,0:T(8,128)S(1)}, s32[16,32,128]{2,1,0:T(8,128)}, u32[]{:S(2)}) copy-start(s32[16,32,128]{2,1,0:T(8,128)} %material_ref.1) | copy-start | bytes 786436
  4.4 0.9 %copy-start.7 = (s32[16,32,128]{2,1,0:T(8,128)S(1)}, s32[16,32,128]{2,1,0:T(8,128)}, u32[]{:S(2)}) copy-start(s32[16,32,128]{2,1,0:T(8,128)} %pattern_ref.1) | copy-start | bytes 786436
  5.4 0.7 copy-start.10
  6.0 0.7 copy-start.11
  6.7 0.7 copy-start.12
  7.3 12.3 %copy-start.16 = (f32[2]{0:T(128)S(1)}, f32[2]{0:T(128)}, u32[]{:S(2)}) copy-start(f32[2]{0:T(128)} %param.16) | copy-start | bytes 28
  7.3 26.9 %copy-start.3 = (f32[2,3,16,32,128]{4,3,2,1,0:T(8,128)S(1)}, f32[2,3,16,32,128]{4,3,2,1,0:T(8,128)}, u32[]{:S(2)}) copy-start(f32[2,3,16,32,128]{4,3,2,1,0:T(8,128)} %h_hbm.1) | copy-start | bytes 4718596
  10.9 0.7 copy-start.4
  11.6 0.7 copy-start.8
  12.3 0.7 copy-start.13
  12.9 0.7 copy-start.14
  13.6 20.6 %copy-start.1 = (f32[2,3,16,32,128]{4,3,2,1,0:T(8,128)S(1)}, f32[2,3,16,32,128]{4,3,2,1,0:T(8,128)}, u32[]{:S(2)}) copy-start(f32[2,3,16,32,128]{4,3,2,1,0:T(8,128)} %e_hbm.1) | copy-start | bytes 4718596
  13.6 8.6 %collective-permute-start = (f32[4,32,128]{2,1,0:T(8,128)}, f32[4,32,128]{2,1,0:T(8,128)S(1)}, u32[]{:S(2)}, u32[]{:S(2)}) collective-permute-start(f32[4,32,128]{2,1,0:T(8,128)} %get-tuple-element.14), channel_id=1, source_target_pairs={{7,0},{0,1},{1,2},{2,3},{3,4},{4,5},{5,6},{6,7},{15,8},{8,9},{9,10... | collective-permute-start | bytes 196616 | tf_op jit(solution)/shard_map/ppermute | solution.py:26
  15.8 6.5 %collective-permute-start.1 = (f32[4,32,128]{2,1,0:T(8,128)}, f32[4,32,128]{2,1,0:T(8,128)S(1)}, u32[]{:S(2)}, u32[]{:S(2)}) collective-permute-start(f32[4,32,128]{2,1,0:T(8,128)} %get-tuple-element.15), channel_id=1, source_target_pairs={{1,0},{2,1},{3,2},{4,3},{5,4},{6,5},{7,6},{0,7},{9,8},{10,9},{11,1... | collective-permute-start | bytes 196616 | tf_op jit(solution)/shard_map/ppermute | solution.py:26
  22.9 11.3 %collective-permute-start.3 = (f32[58,8,128]{2,1,0:T(8,128)}, f32[58,8,128]{2,1,0:T(8,128)}, u32[]{:S(2)}, u32[]{:S(2)}) collective-permute-start(f32[58,8,128]{2,1,0:T(8,128)} %bitcast_dynamic-update-slice_fusion), channel_id=1, source_target_pairs={{248,0},{0,8},{8,16},{16,24},{24,32},{32,40},{40,48},{48,56},{56,6... | collective-permute-start | bytes 712712 | tf_op jit(solution)/shard_map/ppermute | solution.py:26
  26.2 8.1 %collective-permute-start.2 = (f32[58,8,128]{2,1,0:T(8,128)}, f32[58,8,128]{2,1,0:T(8,128)}, u32[]{:S(2)}, u32[]{:S(2)}) collective-permute-start(f32[58,8,128]{2,1,0:T(8,128)} %bitcast_dynamic-update-slice_fusion.1), channel_id=1, source_target_pairs={{8,0},{16,8},{24,16},{32,24},{40,32},{48,40},{56,48},{64,56},{72,6... | collective-permute-start | bytes 712712 | tf_op jit(solution)/shard_map/ppermute | solution.py:26
  34.3 1.0 %copy-start.5 = (f32[16,32,128]{2,1,0:T(8,128)S(1)}, f32[16,32,128]{2,1,0:T(8,128)}, u32[]{:S(2)}) copy-start(f32[16,32,128]{2,1,0:T(8,128)} %copy-done.4) | copy-start | bytes 786436
  35.2 0.9 %copy-start.9 = (f32[13,32,128]{2,1,0:T(8,128)S(1)}, f32[13,32,128]{2,1,0:T(8,128)}, u32[]{:S(2)}) copy-start(f32[13,32,128]{2,1,0:T(8,128)} %copy-done.8) | copy-start | bytes 638980
  47.5 13.4 %all-to-all-start = ((f32[8,32,128]{2,1,0:T(8,128)}), f32[8,32,128]{2,1,0:T(8,128)S(1)}, u32[]{:S(2)}, u32[]{:S(2)}) async-start(f32[8,32,128]{2,1,0:T(8,128)} %get-tuple-element.20), calls=%async_computation | async-start | bytes 262144 | tf_op jit(solution)/shard_map/all_to_all | solution.py:517
  61.0 0.6 copy-start.15

commit v2 on v1

v2 whole, which is shorter than its diff:
```python
import functools
import math

import jax
import jax.numpy as jnp
from jax import lax
from jax.experimental import pallas as pl
from jax.experimental.pallas import tpu as pltpu
from jax.sharding import PartitionSpec as P

STEP_DT = 0.5
ORD_X = 256
ORD_Y = 256
NZ = 16
ROWS = 32
COLS = 128
EXT = 40
MAIN_BLOCKS = 52
VMEM = pltpu.VMEM
SMEM = pltpu.SMEM


def passed_along(block, axis, distance):
    devices = range(lax.axis_size(axis))
    route = [((i - distance) % len(devices), i) for i in devices]
    return lax.ppermute(block, axis, route)


def roll(values, shift, axis):
    size = values.shape[axis]
    if isinstance(shift, int):
        shift = shift % size
        if shift == 0:
            return values
    return pltpu.roll(values, shift, axis)


def lanes_of(shape):
    return lax.broadcasted_iota(jnp.int32, shape, len(shape) - 1)


def coef_table(base_ref, mode_ref, node_ref):
    lane = lanes_of((8, 128))
    material = lane // 16
    pattern = lane % 16
    base = jnp.zeros((8, 128), jnp.float32)
    for m in range(8):
        base = jnp.where(material == m, base_ref[m], base)
    change = jnp.zeros((8, 128), jnp.float32)
    for k in range(4):
        mode = jnp.zeros((8, 128), jnp.float32)
        for p in range(16):
            mode = jnp.where(pattern == p, mode_ref[k, p], mode)
        change = change + node_ref[k] * mode
    return STEP_DT / (base * (1.0 + change))


def look_up(table, pair):
    rows = [
        jnp.take_along_axis(table, pair[8 * r : 8 * r + 8], axis=1)
        for r in range(pair.shape[0] // 8)
    ]
    return jnp.concatenate(rows, axis=0)


def fetched(pairs, sem):
    copies = [
        pltpu.make_async_copy(source, target, sem.at[k])
        for k, (source, target) in enumerate(pairs)
    ]
    for copy in copies:
        copy.start()
    for copy in copies:
        copy.wait()


def plane_of(e_ref, h_ref, n, z):
    ref = e_ref if n < 6 else h_ref
    return ref[(n % 6) // 3, n % 3, z]


def rows_kernel(
    e_hbm,
    h_hbm,
    material_hbm,
    pattern_hbm,
    base_hbm,
    mode_hbm,
    node_hbm,
    monitor_hbm,
    after_hbm,
    plane_ref,
    coef_ref,
    own_ref,
    first_ref,
    last_ref,
    e_ref,
    h_ref,
    material_ref,
    pattern_ref,
    base_ref,
    mode_ref,
    node_ref,
    monitor_ref,
    sem,
):
    fetched(
        [
            (e_hbm, e_ref),
            (h_hbm, h_ref),
            (material_hbm, material_ref),
            (pattern_hbm, pattern_ref),
            (base_hbm, base_ref),
            (mode_hbm, mode_ref),
            (node_hbm, node_ref),
            (monitor_hbm, monitor_ref),
        ],
        sem,
    )
    table = coef_table(base_ref, mode_ref, node_ref)

    def coef_plane(z, carry):
        coef_ref[z] = look_up(table, material_ref[z] * 16 + pattern_ref[z])
        return carry

    lax.fori_loop(0, NZ, coef_plane, 0)
    group = lanes_of((ROWS, COLS)) // 8
    for n in range(13):
        packed = jnp.zeros((ROWS, COLS), jnp.float32)
        for z in range(NZ):
            values = coef_ref[z] if n == 12 else plane_of(e_ref, h_ref, n, z)
            packed = jnp.where(group == z, roll(values, 8 * z + 6, 1), packed)
        own_ref[n] = packed
        for quad in range(NZ // 4):
            planes = [
                coef_ref[z] if n == 12 else plane_of(e_ref, h_ref, n, z)
                for z in range(4 * quad, 4 * quad + 4)
            ]
            first_ref[NEAR_BLOCKS + 4 * n + quad] = jnp.concatenate(
                [values[0:2] for values in planes], axis=0
            )
            last_ref[4 * n + quad] = jnp.concatenate(
                [values[ROWS - 2 : ROWS] for values in planes], axis=0
            )
    level = monitor_ref[0]
    for n in range(COUNT):
        if n < 2 * HALF:
            field, c, k = NEAR[n % HALF]
            z = level - 2 + k
            inside = z >= 0 if field else z < NZ
            ref = h_ref if field else e_ref
            values = jnp.where(inside, ref[n // HALF, c, jnp.clip(z, 0, NZ - 1)], 0.0)
        else:
            values = coef_ref[jnp.clip(level - 1 + n - 2 * HALF, 0, NZ - 1)]
        plane_ref[n] = values
        start = 4 * (n % 2)
        first_ref[n // 2, start : start + 4, :] = values[0:4]
    first_ref[NEAR_BLOCKS - 1, 4:8, :] = jnp.zeros((4, COLS), jnp.float32)
    for k in range(2):
        first_ref[NEAR_BLOCKS + MAIN_BLOCKS + k] = jnp.zeros((8, COLS), jnp.float32)


def pack_kernel(
    own_ref, next_ref, prev_ref, rot_ref, after_ref, tail_ref, right_ref, left_ref
):
    rot = [rot_ref[k : k + 1, :] for k in range(8)]
    group = lanes_of((2, COLS)) // 8
    place = lanes_of((EXT, COLS)) % 8

    tail_ref[...] = jnp.zeros_like(tail_ref)
    for ref, start, row, cos, sin in (
        (next_ref, NEAR_BLOCKS, 32, rot[0], rot[1]),
        (prev_ref, 0, 38, rot[2], rot[3]),
    ):
        for n in (0, 1, 2, 6, 7, 8, 12):
            parts = 1 if n == 12 else 2
            packed = [jnp.zeros((2, COLS), jnp.float32) for _ in range(parts)]
            for quad in range(NZ // 4):
                values = [ref[start + 4 * (n + 3 * part) + quad] for part in range(parts)]
                if parts == 2:
                    values = turned(values[0], values[1], cos, sin)
                for k in range(4):
                    z = 4 * quad + k
                    for part in range(parts):
                        packed[part] = jnp.where(
                            group == z,
                            roll(values[part][2 * k : 2 * k + 2], 8 * z + 6, 1),
                            packed[part],
                        )
            for part in range(parts):
                tail_ref[n + 3 * part, row - ROWS : row - ROWS + 2, :] = packed[part]
    def column(n):
        return jnp.concatenate([own_ref[n], tail_ref[n]], axis=0)

    for c in range(3):
        e_re, e_im, h_re, h_im = (column(3 * k + c) for k in range(4))
        right_ref[c] = jnp.where(
            place < 4,
            jnp.where(place < 2, roll(h_re, -4, 1), roll(h_im, -2, 1)),
            jnp.where(place < 6, e_re, roll(e_im, 2, 1)),
        )
        left_ref[c] = jnp.where(
            place < 4,
            jnp.where(place < 2, roll(h_im, -6, 1), roll(h_re, -4, 1)),
            jnp.where(place < 6, roll(e_im, -2, 1), e_re),
        )
    right_ref[3] = column(12)
    left_ref[3] = column(12)


def turned(re, im, cos, sin):
    return re * cos - im * sin, im * cos + re * sin


def strip_of(own, right, left, rot):
    place = lanes_of(own[0].shape) % 8

    def joined(index, from_right, from_left):
        return jnp.where(
            place < 4,
            jnp.where(place < 2, roll(own[index], -4, 1), from_left),
            jnp.where(place < 6, from_right, own[index]),
        )

    strip = [None] * 13
    for c in range(3):
        r = right[c]
        l = left[c]
        e_right = turned(r, roll(r, -2, 1), rot[4], rot[5])
        h_right = turned(roll(r, 4, 1), roll(r, 2, 1), rot[4], rot[5])
        e_left = turned(roll(l, -4, 1), roll(l, -2, 1), rot[6], rot[7])
        h_left = turned(l, roll(l, 2, 1), rot[6], rot[7])
        for part in range(2):
            strip[3 * part + c] = joined(3 * part + c, e_right[part], e_left[part])
            strip[6 + 3 * part + c] = joined(6 + 3 * part + c, h_right[part], h_left[part])
    strip[12] = joined(12, right[3], roll(left[3], -4, 1))
    return strip


def next_row(values):
    return roll(values, -1, 0)


def prev_row(values):
    return roll(values, 1, 0)


def h_new(h, e, e_up, e_xn, e_yn):
    return (
        h[0] - STEP_DT * (e_yn[1] - e[2] - (e_up[1] - e[1])),
        h[1] - STEP_DT * (e_up[0] - e[0] - (e_xn[1] - e[2])),
        h[2] - STEP_DT * (e_xn[0] - e[1] - (e_yn[0] - e[0])),
    )


def e_new(e, h, h_down, h_xp, h_yp, coef):
    return (
        e[0] + coef * (h[2] - h_yp[1] - (h[1] - h_down[1])),
        e[1] + coef * (h[0] - h_down[0] - (h[2] - h_xp[1])),
        e[2] + coef * (h[1] - h_xp[0] - (h[0] - h_yp[0])),
    )


def strip_h(h, e):
    up = lanes_of((EXT, COLS)) < 8 * (NZ - 1)
    above = [jnp.where(up, roll(e[c], -8, 1), 0.0) for c in range(2)]
    return h_new(
        h,
        e,
        above,
        (next_row(e[1]), next_row(e[2])),
        (roll(e[0], -1, 1), roll(e[2], -1, 1)),
    )


def strip_e(e, h, coef):
    up = lanes_of((EXT, COLS)) >= 8
    below = [jnp.where(up, roll(h[c], 8, 1), 0.0) for c in range(2)]
    return e_new(
        e,
        h,
        below,
        (prev_row(h[1]), prev_row(h[2])),
        (roll(h[0], 1, 1), roll(h[2], 1, 1)),
        coef,
    )


def field_kernel(
    e_hbm,
    h_hbm,
    coef_hbm,
    own_hbm,
    tail_hbm,
    right_hbm,
    left_hbm,
    next_hbm,
    prev_hbm,
    rot_hbm,
    after_hbm,
    e_out,
    h_out,
    e_all,
    h_all,
    coef_all,
    own_ref,
    right_ref,
    left_ref,
    next_ref,
    prev_ref,
    rot_ref,
    edge_ref,
    sem,
):
    load_e = pltpu.make_async_copy(e_hbm, e_all.at[:, :, 0:NZ, 0:ROWS, :], sem.at[0])
    load_h = pltpu.make_async_copy(h_hbm, h_all.at[:, :, 1 : NZ + 1, 0:ROWS, :], sem.at[1])
    small = [
        pltpu.make_async_copy(source, target, sem.at[4 + k])
        for k, (source, target) in enumerate(
            [
                (rot_hbm, rot_ref),
                (own_hbm, own_ref.at[:, 0:ROWS]),
                (tail_hbm, own_ref.at[:, ROWS:EXT]),
                (right_hbm, right_ref),
                (left_hbm, left_ref),
                (next_hbm, next_ref),
                (prev_hbm, prev_ref),
                (coef_hbm, coef_all.at[:, 0:ROWS]),
            ]
        )
    ]
    for copy in small:
        copy.start()
    load_e.start()
    load_h.start()
    for copy in small:
        copy.wait()
    rot = [rot_ref[k : k + 1, :] for k in range(8)]

    for part in range(2):
        for c in range(3):
            e_all[part, c, NZ] = jnp.zeros((EXT, COLS), jnp.float32)
            h_all[part, c, 0] = jnp.zeros((EXT, COLS), jnp.float32)
    for ref, start, row, cos, sin in (
        (next_ref, NEAR_BLOCKS, 32, rot[0], rot[1]),
        (prev_ref, 0, 38, rot[2], rot[3]),
    ):
        for field in range(2):
            for c in range(3):
                for quad in range(4):
                    re = ref[start + (6 * field + c) * 4 + quad]
                    im = ref[start + (6 * field + 3 + c) * 4 + quad]
                    for part, values in enumerate(turned(re, im, cos, sin)):
                        for k in range(4):
                            dest = h_all if field else e_all
                            z = 4 * quad + k + field
                            dest[part, c, z, row : row + 2, :] = values[2 * k : 2 * k + 2]
        for quad in range(4):
            values = ref[start + 48 + quad]
            for k in range(4):
                coef_all[4 * quad + k, row : row + 2, :] = values[2 * k : 2 * k + 2]
    strip = strip_of(
        [own_ref[a] for a in range(13)],
        [right_ref[a] for a in range(4)],
        [left_ref[a] for a in range(4)],
        rot,
    )
    for part in range(2):
        e = tuple(strip[3 * part + c] for c in range(3))
        h = tuple(strip[6 + 3 * part + c] for c in range(3))
        for step in range(2):
            edge_ref[part, 2 * step, 0] = e[0]
            edge_ref[part, 2 * step, 1] = e[2]
            h = strip_h(h, e)
            edge_ref[part, 2 * step + 1, 0] = h[0]
            edge_ref[part, 2 * step + 1, 1] = h[2]
            if step == 0:
                e = strip_e(e, h, strip[12])

    lane = lanes_of((EXT, COLS))

    def next_col(values, edge, z):
        arrived = roll(edge, lax.rem(COLS + 125 - 8 * z, COLS), 1)
        return jnp.where(lane == COLS - 1, arrived, roll(values, -1, 1))

    def prev_col(values, edge, z):
        arrived = roll(edge, lax.rem(COLS + 123 - 8 * z, COLS), 1)
        return jnp.where(lane == 0, arrived, roll(values, 1, 1))

    def do_h(step, z):
        for part in range(2):
            e = tuple(e_all[part, c, z] for c in range(3))
            h = tuple(h_all[part, c, z + 1] for c in range(3))
            e_up = (e_all[part, 0, z + 1], e_all[part, 1, z + 1])
            e_yn = (
                next_col(e[0], edge_ref[part, 2 * step, 0], z),
                next_col(e[2], edge_ref[part, 2 * step, 1], z),
            )
            new = h_new(h, e, e_up, (next_row(e[1]), next_row(e[2])), e_yn)
            for c in range(3):
                h_all[part, c, z + 1] = new[c]

    def do_e(step, z):
        coef = coef_all[z]
        for part in range(2):
            e = tuple(e_all[part, c, z] for c in range(3))
            h = tuple(h_all[part, c, z + 1] for c in range(3))
            h_down = (h_all[part, 0, z], h_all[part, 1, z])
            h_yp = (
                prev_col(h[0], edge_ref[part, 2 * step + 1, 0], z),
                prev_col(h[2], edge_ref[part, 2 * step + 1, 1], z),
            )
            new = e_new(e, h, h_down, (prev_row(h[1]), prev_row(h[2])), h_yp, coef)
            for c in range(3):
                e_all[part, c, z] = new[c]

    load_e.wait()
    load_h.wait()

    def store(z):
        pltpu.make_async_copy(
            e_all.at[:, :, z, 0:ROWS, :], e_out.at[:, :, z], sem.at[2]
        ).start()
        pltpu.make_async_copy(
            h_all.at[:, :, z + 1, 0:ROWS, :], h_out.at[:, :, z], sem.at[3]
        ).start()

    do_h(0, 0)
    do_e(0, 0)

    def layer(z, carry):
        do_h(0, z)
        do_e(0, z)
        do_h(1, z - 1)
        do_e(1, z - 1)
        store(z - 1)
        return carry

    lax.fori_loop(1, NZ, layer, 0)
    do_h(1, NZ - 1)
    do_e(1, NZ - 1)
    store(NZ - 1)
    pltpu.make_async_copy(e_all.at[:, :, 0:NZ, 0:ROWS, :], e_out, sem.at[2]).wait()
    pltpu.make_async_copy(h_all.at[:, :, 1 : NZ + 1, 0:ROWS, :], h_out, sem.at[3]).wait()


def y_section(re, im, wave_ref, spread_ref):
    wave = wave_ref[...]
    owners, _, lanes = spread_ref.shape
    each = lanes // 4
    out = [
        jnp.dot(
            jnp.concatenate(pair, axis=1),
            wave,
            precision=lax.Precision.HIGHEST,
            preferred_element_type=jnp.float32,
        )
        for pair in ((re, im), (im, -re))
    ]
    for owner in range(owners):
        pieces = [
            out[part][c * ROWS : (c + 1) * ROWS, owner * each : (owner + 1) * each]
            for part in range(2)
            for c in range(2)
        ]
        spread_ref[owner] = jnp.concatenate(pieces, axis=1)


def x_kernel(got_ref, wave_ref, part_ref):
    total = got_ref[0]
    for source in range(1, got_ref.shape[0]):
        total = total + got_ref[source]
    half = total.shape[1] // 2
    other = roll(total, half, 1)
    other = jnp.where(lanes_of(other.shape) < half, other, -other)
    result = jnp.dot(
        wave_ref[...],
        jnp.concatenate([total, other], axis=0),
        precision=lax.Precision.HIGHEST,
        preferred_element_type=jnp.float32,
    )
    part_ref[...] = result.reshape(part_ref.shape)


def sum_kernel(got_ref, out_ref):
    total = got_ref[0]
    for source in range(1, got_ref.shape[0]):
        total = total + got_ref[source]
    each = total.shape[1] // 4
    for c in range(2):
        for part in range(2):
            start = (2 * part + c) * each
            out_ref[c, part] = total[:, start : start + each]


NEAR = (
    [(0, 0, k) for k in range(0, 5)]
    + [(0, 1, k) for k in range(0, 5)]
    + [(0, 2, k) for k in range(0, 4)]
    + [(1, 0, k) for k in range(0, 4)]
    + [(1, 1, k) for k in range(0, 4)]
    + [(1, 2, k) for k in range(1, 4)]
)
HALF = len(NEAR)
COUNT = 2 * HALF + 3
NEAR_BLOCKS = (COUNT + 1) // 2
CORNER = NEAR_BLOCKS + MAIN_BLOCKS
WIDE = 2 * COLS


def near_kernel(
    e_hbm,
    h_hbm,
    material_hbm,
    pattern_hbm,
    base_hbm,
    mode_hbm,
    node_hbm,
    monitor_hbm,
    cols_ref,
    e_ref,
    h_ref,
    material_ref,
    pattern_ref,
    base_ref,
    mode_ref,
    node_ref,
    monitor_ref,
    sem,
):
    fetched(
        [
            (e_hbm, e_ref),
            (h_hbm, h_ref),
            (material_hbm, material_ref),
            (pattern_hbm, pattern_ref),
            (base_hbm, base_ref),
            (mode_hbm, mode_ref),
            (node_hbm, node_ref),
            (monitor_hbm, monitor_ref),
        ],
        sem,
    )
    level = monitor_ref[0]
    table = coef_table(base_ref, mode_ref, node_ref)
    slot = lanes_of((ROWS, COLS)) // 4
    packed = [jnp.zeros((ROWS, COLS), jnp.float32) for _ in range(2)]
    for n in range(COUNT):
        if n < 2 * HALF:
            field, c, k = NEAR[n % HALF]
            z = level - 2 + k
            inside = z >= 0 if field else z < NZ
            ref = h_ref if field else e_ref
            values = ref[n // HALF, c, jnp.clip(z, 0, NZ - 1)]
            values = jnp.where(inside, values, 0.0)
        else:
            z = jnp.clip(level - 1 + n - 2 * HALF, 0, NZ - 1)
            values = look_up(table, material_ref[z] * 16 + pattern_ref[z])
        packed[n // 32] = jnp.where(
            slot == n % 32, roll(values, 4 * (n % 32), 1), packed[n // 32]
        )
    for k in range(2):
        cols_ref[k] = packed[k]


def plane_kernel(
    plane_ref, cols_ref, rows_ref, rot_ref, wave_ref, monitor_ref, spread_ref, all_ref
):
    rot = [rot_ref[k : k + 1, :] for k in range(8)]
    level = monitor_ref[0]

    def put(n, rows, main, side):
        all_ref[n, rows, 0:COLS] = main
        all_ref[n, rows, COLS:WIDE] = side

    def side_of(n):
        return roll(cols_ref[n // 32], -4 * (n % 32), 1)

    def foot_of(n):
        start = 4 * (n % 2)
        return rows_ref[n // 2, start : start + 4, :]

    def corner_of(n):
        return roll(rows_ref[CORNER + n // 32, 0:4, :], -4 * (n % 32), 1)

    body = slice(0, ROWS)
    foot = slice(ROWS, ROWS + 4)
    for n in range(HALF):
        m = n + HALF
        sides = turned(side_of(n), side_of(m), rot[6], rot[7])
        feet = turned(foot_of(n), foot_of(m), rot[0], rot[1])
        corners = turned(corner_of(n), corner_of(m), rot[6], rot[7])
        corners = turned(*corners, rot[0], rot[1])
        for part, at in enumerate((n, m)):
            put(at, body, plane_ref[at], sides[part])
            put(at, foot, feet[part], corners[part])
    for n in range(2 * HALF, COUNT):
        put(n, body, plane_ref[n], side_of(n))
        put(n, foot, foot_of(n), corner_of(n))

    def where(field, c, k, part):
        return NEAR.index((field, c, k)) + part * HALF

    def e_at(c, k, part):
        return all_ref[where(0, c, k, part)]

    def h_at(c, k, part):
        return all_ref[where(1, c, k, part)]

    def next_col(values):
        return roll(values, -1, 1)

    def prev_col(values):
        return roll(values, 1, 1)

    def update_h(k, part, wanted):
        above = level - 2 + k >= 0
        new = {}
        if 0 in wanted:
            ez, ey = e_at(2, k, part), e_at(1, k, part)
            new[0] = h_at(0, k, part) - STEP_DT * (
                next_col(ez) - ez - (e_at(1, k + 1, part) - ey)
            )
        if 1 in wanted:
            ez, ex = e_at(2, k, part), e_at(0, k, part)
            new[1] = h_at(1, k, part) - STEP_DT * (
                e_at(0, k + 1, part) - ex - (next_row(ez) - ez)
            )
        if 2 in wanted:
            ex, ey = e_at(0, k, part), e_at(1, k, part)
            new[2] = h_at(2, k, part) - STEP_DT * (
                next_row(ey) - ey - (next_col(ex) - ex)
            )
        for c, values in new.items():
            if k < 2:
                values = jnp.where(above, values, 0.0)
            all_ref[where(1, c, k, part)] = values

    def update_e(k, part, wanted):
        below = level - 2 + k < NZ
        coef = all_ref[2 * HALF + k - 1]
        hx, hy, hz = (h_at(c, k, part) for c in range(3)) if 2 not in wanted else (
            h_at(0, k, part),
            h_at(1, k, part),
            h_at(2, k, part) if k > 0 else None,
        )
        new = {}
        if 0 in wanted:
            new[0] = e_at(0, k, part) + coef * (
                hz - prev_col(hz) - (hy - h_at(1, k - 1, part))
            )
        if 1 in wanted:
            new[1] = e_at(1, k, part) + coef * (
                hx - h_at(0, k - 1, part) - (hz - prev_row(hz))
            )
        if 2 in wanted:
            new[2] = e_at(2, k, part) + coef * (
                hy - prev_row(hy) - (hx - prev_col(hx))
            )
        for c, values in new.items():
            if k > 2:
                values = jnp.where(below, values, 0.0)
            all_ref[where(0, c, k, part)] = values

    for part in range(2):
        for k in range(4):
            update_h(k, part, (0, 1, 2) if k > 0 else (0, 1))
        for k in range(1, 4):
            update_e(k, part, (0, 1, 2) if k < 3 else (0, 1))
        update_h(1, part, (0, 1))
        update_h(2, part, (0, 1, 2))
        update_e(2, part, (0, 1))

    def cells(c, part):
        values = all_ref[where(0, c, 2, part), 2 : ROWS + 2, :]
        return roll(values, -2, 1)[:, 0:COLS]

    re = jnp.concatenate([cells(c, 0) for c in range(2)], axis=0)
    im = jnp.concatenate([cells(c, 1) for c in range(2)], axis=0)
    y_section(re, im, wave_ref, spread_ref)


def table_kernel(
    count_x, count_y, phase_hbm, place_ref, after_hbm, rot_ref, y_ref, x_ref, phase_ref, sem
):
    fetched([(phase_hbm, phase_ref)], sem)
    index_x, index_y = place_ref[0], place_ref[1]
    theta_x, theta_y = phase_ref[0], phase_ref[1]
    total_x, total_y = ROWS * count_x, COLS * count_y
    row = lax.broadcasted_iota(jnp.int32, (8, COLS), 0)
    angle = jnp.where(row < 4, theta_x, theta_y)
    flags = [
        jnp.where(flag, 1, 0)
        for flag in (index_x == count_x - 1, index_x == 0, index_y == 0, index_y == count_y - 1)
    ]
    here = jnp.where(
        row < 4,
        jnp.where(row < 2, flags[0], flags[1]),
        jnp.where(row < 6, flags[2], flags[3]),
    )
    angle = jnp.where(here == 1, angle, 0.0)
    angle = jnp.where(row // 2 == 1, -angle, jnp.where(row // 2 == 2, -angle, angle))
    rot_ref[...] = jnp.where(row % 2 == 0, jnp.cos(angle), jnp.sin(angle))

    def angles(order, place, total, theta):
        product = (order * place) & (total - 1)
        return (
            2.0 * math.pi * product.astype(jnp.float32) + theta * place.astype(jnp.float32)
        ) / total

    scale = 1.0 / math.sqrt(total_x * total_y)
    shape = (COLS, ORD_Y)
    place = index_y * COLS + 2 + lax.broadcasted_iota(jnp.int32, shape, 0)
    order = lax.broadcasted_iota(jnp.int32, shape, 1) - ORD_Y // 2
    angle = angles(order, place, total_y, theta_y)
    y_ref[0:COLS, :] = jnp.cos(angle) * scale
    y_ref[COLS:, :] = jnp.sin(angle) * scale
    shape = (ORD_X, 2 * ROWS)
    lane = lax.broadcasted_iota(jnp.int32, shape, 1)
    place = index_x * ROWS + 2 + lane % ROWS
    order = lax.broadcasted_iota(jnp.int32, shape, 0) - ORD_X // 2
    angle = angles(order, place, total_x, theta_x)
    x_ref[...] = jnp.where(lane < ROWS, jnp.cos(angle), jnp.sin(angle))


def params(mebibytes):
    return pltpu.CompilerParams(vmem_limit_bytes=mebibytes << 20)


def cost(microseconds):
    return pl.CostEstimate(
        flops=0, bytes_accessed=microseconds * 3_000_000, transcendentals=0
    )


def f32(*shape):
    return jax.ShapeDtypeStruct(shape, jnp.float32)


def shards(
    e_field, h_field, material, pattern, base_eps, mode_table, nodes, bloch_phase, monitor_z
):
    count_x = lax.axis_size("gx")
    count_y = lax.axis_size("gy")
    index_x = lax.axis_index("gx")
    index_y = lax.axis_index("gy")
    each_p = ORD_X // count_x
    each_q = ORD_Y // count_y
    vmem = pl.BlockSpec(memory_space=VMEM)
    smem = pl.BlockSpec(memory_space=SMEM)
    hbm = pl.BlockSpec(memory_space=pltpu.HBM)
    f32_vmem = lambda *shape: VMEM(shape, jnp.float32)
    tables = [
        SMEM(base_eps.shape, jnp.float32),
        SMEM(mode_table.shape, jnp.float32),
        SMEM(nodes.shape, jnp.float32),
    ]

    cols = pl.pallas_call(
        near_kernel,
        out_shape=f32(2, ROWS, COLS),
        in_specs=[hbm] * 8,
        out_specs=vmem,
        scratch_shapes=[
            f32_vmem(*e_field.shape),
            f32_vmem(*h_field.shape),
            VMEM(material.shape, jnp.int32),
            VMEM(pattern.shape, jnp.int32),
            *tables,
            SMEM((1,), jnp.int32),
            pltpu.SemaphoreType.DMA((8,)),
        ],
        compiler_params=params(60),
        name="near",
    )(e_field, h_field, material, pattern, base_eps, mode_table, nodes, monitor_z)
    near_cols = passed_along(cols, "gy", -1)

    planes, coef, own, first, last = pl.pallas_call(
        rows_kernel,
        out_shape=(
            f32(COUNT, ROWS, COLS),
            f32(NZ, ROWS, COLS),
            f32(13, ROWS, COLS),
            f32(CORNER + 2, 8, COLS),
            f32(MAIN_BLOCKS, 8, COLS),
        ),
        in_specs=[hbm] * 9,
        out_specs=(vmem,) * 5,
        scratch_shapes=[
            f32_vmem(*e_field.shape),
            f32_vmem(*h_field.shape),
            VMEM(material.shape, jnp.int32),
            VMEM(pattern.shape, jnp.int32),
            *tables,
            SMEM((1,), jnp.int32),
            pltpu.SemaphoreType.DMA((8,)),
        ],
        compiler_params=params(60),
        cost_estimate=cost(0),
        name="rows",
    )(e_field, h_field, material, pattern, base_eps, mode_table, nodes, monitor_z, cols)
    first = lax.dynamic_update_slice(first, near_cols[:, 0:8], (CORNER, 0, 0))
    from_next = passed_along(first, "gx", -1)
    from_prev = passed_along(last, "gx", 1)
    rot, y_wave, x_wave = pl.pallas_call(
        functools.partial(table_kernel, count_x, count_y),
        out_shape=(f32(8, COLS), f32(2 * COLS, ORD_Y), f32(ORD_X, 2 * ROWS)),
        in_specs=[hbm, smem, hbm],
        out_specs=(vmem,) * 3,
        scratch_shapes=[SMEM((2,), jnp.float32), pltpu.SemaphoreType.DMA((1,))],
        compiler_params=params(8),
        cost_estimate=cost(0),
        name="tables",
    )(bloch_phase, jnp.stack([index_x, index_y]), near_cols)
    spread = pl.pallas_call(
        plane_kernel,
        out_shape=f32(count_y, ROWS, 4 * each_q),
        in_specs=[vmem] * 5 + [smem],
        out_specs=vmem,
        scratch_shapes=[f32_vmem(COUNT, EXT, WIDE)],
        compiler_params=params(12),
        cost_estimate=cost(0),
        name="plane",
    )(planes, near_cols, from_next, rot, y_wave, monitor_z)
    tail, right, left = pl.pallas_call(
        pack_kernel,
        out_shape=(f32(13, 8, COLS), f32(4, EXT, COLS), f32(4, EXT, COLS)),
        in_specs=[vmem] * 5,
        out_specs=(vmem,) * 3,
        compiler_params=params(8),
        cost_estimate=cost(0),
        name="pack",
    )(own, from_next, from_prev, rot, spread)
    from_right = passed_along(right, "gy", 1)
    from_left = passed_along(left, "gy", -1)
    got = lax.all_to_all(spread, "gy", 0, 0, tiled=True)
    partial = pl.pallas_call(
        x_kernel,
        out_shape=f32(count_x, each_p, 4 * each_q),
        in_specs=[vmem, vmem],
        out_specs=vmem,
        compiler_params=params(8),
        cost_estimate=cost(0),
        name="x_section",
    )(got, x_wave)
    got = lax.all_to_all(partial, "gx", 0, 0, tiled=True)
    e_out, h_out = pl.pallas_call(
        field_kernel,
        out_shape=(f32(*e_field.shape), f32(*h_field.shape)),
        in_specs=[hbm] * 11,
        out_specs=(hbm, hbm),
        scratch_shapes=[
            f32_vmem(2, 3, NZ + 1, EXT, COLS),
            f32_vmem(2, 3, NZ + 1, EXT, COLS),
            f32_vmem(NZ, EXT, COLS),
            f32_vmem(13, EXT, COLS),
            f32_vmem(4, EXT, COLS),
            f32_vmem(4, EXT, COLS),
            f32_vmem(CORNER + 2, 8, COLS),
            f32_vmem(MAIN_BLOCKS, 8, COLS),
            f32_vmem(8, COLS),
            f32_vmem(2, 4, 2, EXT, COLS),
            pltpu.SemaphoreType.DMA((12,)),
        ],
        compiler_params=params(60),
        cost_estimate=cost(0),
        name="fields",
    )(
        e_field,
        h_field,
        coef,
        own,
        tail,
        from_right,
        from_left,
        from_next,
        from_prev,
        rot,
        partial,
    )
    orders = pl.pallas_call(
        sum_kernel,
        out_shape=f32(2, 2, each_p, each_q),
        in_specs=[vmem],
        out_specs=vmem,
        compiler_params=params(8),
        cost_estimate=cost(0),
        name="order_sum",
    )(got)
    return e_out, h_out, orders


def solution(mesh):
    grid = P(None, None, None, "gx", "gy")
    cells = P(None, "gx", "gy")
    return jax.shard_map(
        shards,
        mesh=mesh,
        in_specs=(grid, grid, cells, cells, P(), P(), P(), P(), P()),
        out_specs=(grid, grid, P(None, None, "gx", "gy")),
        check_vma=False,
    )
```

time: 87.2 us -> 68.8 us (0.79)
  blocking collectives: 21.4 us -> 0 us
  local copies, waits for them, and re-layouts: 15.4 us -> 3.16 us
  starting transfers between devices: 15.4 us -> 24.4 us
  waiting for transfers between devices: 5.23 us -> 13.5 us
  Pallas kernels: 18.5 us -> 25.3 us
  other arithmetic: 6.41 us -> 0.07 us
  between operations: 4.31 us -> 1.44 us
    all_to_all x1 -> x0, blocking collectives: 21.4 us -> none  [shards(): got = lax.all_to_all(partial, 'gx', 0, 0, tiled=True)]
    pallas_call x1 -> x5, Pallas kernels: 3.51 us -> 14.5 us  [the longest x1 5.52 us: shards(): pl.pallas_call(rows_kernel, out_shape=(f32(COUNT, ROWS, COLS), f32(NZ, RO...]
    unnamed x34 -> x20, local copies, waits for them, and re-layouts: 12 us -> 2.56 us
    all_to_all x0 -> x1, starting transfers between devices: none -> 8.8 us  [shards(): got = lax.all_to_all(partial, 'gx', 0, 0, tiled=True)]
    ppermute x4 -> x5, waiting for transfers between devices: 0.01 us -> 6.78 us  [passed_along(): return lax.ppermute(block, axis, route)]
    ppermute x4 -> x5, starting transfers between devices: 8.89 us -> 12.2 us  [passed_along(): return lax.ppermute(block, axis, route)]
    all_to_all x1, starting transfers between devices: 6.47 us -> 3.37 us  [shards(): got = lax.all_to_all(spread, 'gy', 0, 0, tiled=True)]
    cos x2 -> x0, other arithmetic: 2.68 us -> none  [the longest x1 2.08 us: shards(): x_wave = jnp.concatenate([jnp.cos(x_angle), jnp.sin(x_angle)], axis=1)]
  transfers between devices with their start and end apart: 5 -> 7, of which waited for: 1 -> 3; matrix products, arithmetic and copies ran while one was open for 11% -> 0% of each run, Pallas kernels for 0% -> 28%
where the time goes in v2:
time: 68.8 us; the launch traced here: 67.9 us
  Pallas kernels  25.3 us (37%)
  starting transfers between devices  24.4 us (35%)
  waiting for transfers between devices  13.5 us (20%)
  local copies, waits for them, and re-layouts  3.16 us (5%)
  between operations  1.44 us (2%)
    ppermute x5, starting transfers between devices, passed_along(): return lax.ppermute(block, axis, route)  12.2 us
    pallas_call x1, Pallas kernels, shards(): pl.pallas_call(field_kernel, out_shape=(f32(*e_field.shape), f32(*h_field...  9.13 us
    all_to_all x1, starting transfers between devices, shards(): got = lax.all_to_all(partial, 'gx', 0, 0, tiled=True)  8.8 us
    ppermute x5, waiting for transfers between devices, passed_along(): return lax.ppermute(block, axis, route)  6.78 us
    all_to_all x1, waiting for transfers between devices, shards(): got = lax.all_to_all(spread, 'gy', 0, 0, tiled=True)  6.75 us
    pallas_call x1, Pallas kernels, shards(): pl.pallas_call(rows_kernel, out_shape=(f32(COUNT, ROWS, COLS), f32(NZ, RO...  5.52 us
    all_to_all x1, starting transfers between devices, shards(): got = lax.all_to_all(spread, 'gy', 0, 0, tiled=True)  3.37 us
    pallas_call x1, Pallas kernels, shards(): pl.pallas_call(near_kernel, out_shape=f32(2, ROWS, COLS), in_specs=[hbm]...  3.05 us
  transfers between devices with their start and end apart: 7, of which 3 were waited for; matrix products, arithmetic and copies ran while one was open for 0% of the time, Pallas kernels for 28%

profile of v2, /device:TPU:1, one launch (start us, length us, event | category | flops | bytes accessed | tf_op | source)
XLA Modules:
  0.0 67.9 jit_solution(14013512310957919202)
XLA Ops:
  1.3 3.1 %near.1.after_hbm = f32[2,32,128]{2,1,0:T(8,128)} custom-call(f32[2,3,16,32,128]{4,3,2,1,0:T(8,128)} %e_hbm.5, f32[2,3,16,32,128]{4,3,2,1,0:T(8,128)} %h_hbm.5, s32[16,32,128]{2,1,0:T(8,128)} %material_hbm.3, s32[16,32,128]{2,1,0:T(8,128)} %pattern_hbm.3, f32[8]{0:T(128)} %base_hbm.3, f32[4,16]{1,0:T(4,128)} %mode_hbm.3, f32[4]{0:T(128)} %node_hbm.3, ...), custom_call_target="tpu_custom_call" | custom-call | tf_op jit(solution)/shard_map/near/pallas_call | solution.py:759
  4.3 0.0 copy-start.6
  4.3 6.1 %collective-permute-start = (f32[2,32,128]{2,1,0:T(8,128)}, f32[2,32,128]{2,1,0:T(8,128)S(1)}, u32[]{:S(2)}, u32[]{:S(2)}) collective-permute-start(f32[2,32,128]{2,1,0:T(8,128)} %near.1.after_hbm), channel_id=1, source_target_pairs={{1,0},{2,1},{3,2},{4,3},{5,4},{6,5},{7,6},{0,7},{9,8},{10,9},{11,1... | collective-permute-start | bytes 98312 | tf_op jit(solution)/shard_map/ppermute | solution.py:26
  10.4 5.5 %rows.1 = (f32[53,32,128]{2,1,0:T(8,128)}, f32[16,32,128]{2,1,0:T(8,128)}, f32[13,32,128]{2,1,0:T(8,128)}, f32[81,8,128]{2,1,0:T(8,128)}, f32[52,8,128]{2,1,0:T(8,128)}) custom-call(f32[2,3,16,32,128]{4,3,2,1,0:T(8,128)} %e_hbm.5, f32[2,3,16,32,128]{4,3,2,1,0:T(8,128)} %h_hbm.5, s32[16,32,128]{2,1,0:T(8,128)} %material_hbm.3, s32[16,32,128]{2,1,0:T(8,128)} %pattern_hbm.3, ...), custom_call_target="tpu_custom_call" | custom-call | tf_op jit(solution)/shard_map/rows/pallas_call | solution.py:778
  16.0 0.0 collective-permute-done.after_hbm.cols_ref
  16.0 0.6 slice_dynamic-update-slice_fusion
  16.6 1.0 %collective-permute-start.1 = (f32[81,8,128]{2,1,0:T(8,128)}, f32[81,8,128]{2,1,0:T(8,128)S(1)}, u32[]{:S(2)}, u32[]{:S(2)}) collective-permute-start(f32[81,8,128]{2,1,0:T(8,128)} %slice_dynamic-update-slice_fusion), channel_id=1, source_target_pairs={{8,0},{16,8},{24,16},{32,24},{40,32},{48,40},{56,48},{64,56},{72,6... | collective-permute-start | bytes 995336 | tf_op jit(solution)/shard_map/ppermute | solution.py:26
  17.5 0.1 pad_add_fusion.place_ref
  17.6 0.0 copy-done.6
  17.6 2.1 %tables.1 = (f32[8,128]{1,0:T(8,128)S(1)}, f32[256,256]{1,0:T(8,128)S(1)}, f32[256,64]{1,0:T(8,128)S(1)}) custom-call(f32[2]{0:T(128)S(1)} %copy-done.6, s32[2]{0:T(128)S(1)} %pad_add_fusion.place_ref, f32[2,32,128]{2,1,0:T(8,128)S(1)} %collective-permute-done.after_hbm.cols_ref), custom_call_target="tpu_custom_call" | custom-call | tf_op jit(solution)/shard_map/tables/pallas_call | solution.py:805
  19.8 0.0 copy-start.5
  19.8 4.3 %collective-permute-done.1.rows_ref.next_ref.next_hbm = f32[81,8,128]{2,1,0:T(8,128)S(1)} collective-permute-done((f32[81,8,128]{2,1,0:T(8,128)}, f32[81,8,128]{2,1,0:T(8,128)S(1)}, u32[]{:S(2)}, u32[]{:S(2)}) %collective-permute-start.1) | collective-permute-done | bytes 331808 | tf_op jit(solution)/shard_map/ppermute | solution.py:26
  24.1 0.0 copy-start
  24.1 0.0 copy-start.1
  24.1 1.3 %copy-done.1 = f32[53,32,128]{2,1,0:T(8,128)S(1)} copy-done((f32[53,32,128]{2,1,0:T(8,128)S(1)}, f32[53,32,128]{2,1,0:T(8,128)}, u32[]{:S(2)}) %copy-start.1) | copy-done | bytes 868376
  25.4 0.0 copy-start.9
  25.4 0.0 copy-start.2
  25.4 2.2 %plane.1.after_ref = f32[8,32,128]{2,1,0:T(8,128)} custom-call(f32[53,32,128]{2,1,0:T(8,128)S(1)} %copy-done.1, f32[2,32,128]{2,1,0:T(8,128)S(1)} %collective-permute-done.after_hbm.cols_ref, f32[81,8,128]{2,1,0:T(8,128)S(1)} %collective-permute-done.1.rows_ref.next_ref.next_hbm, f32[8,128]{1,0:T(8,128)S(1)} %get-tuple-element.20.rot_ref.rot_hbm, ...), custom_call_target="tpu_custom_call" | custom-call | tf_op jit(solution)/shard_map/plane/pallas_call | solution.py:815
  27.6 3.4 %all-to-all-start = ((f32[8,32,128]{2,1,0:T(8,128)}), f32[8,32,128]{2,1,0:T(8,128)S(1)}, u32[]{:S(2)}, u32[]{:S(2)}) async-start(f32[8,32,128]{2,1,0:T(8,128)} %plane.1.after_ref), calls=%async_computation | async-start | bytes 262144 | tf_op jit(solution)/shard_map/all_to_all | solution.py:836
  30.9 0.0 copy-done.9
  30.9 0.1 collective-permute-start.2
  31.1 6.8 %all-to-all-done.got_ref = f32[8,32,128]{2,1,0:T(8,128)S(1)} async-done(((f32[8,32,128]{2,1,0:T(8,128)}), f32[8,32,128]{2,1,0:T(8,128)S(1)}, u32[]{:S(2)}, u32[]{:S(2)}) %all-to-all-start) | async-done | bytes 131104 | tf_op jit(solution)/shard_map/all_to_all | solution.py:836
  37.8 1.0 %x_section.1.after_hbm = f32[32,8,128]{2,1,0:T(8,128)} custom-call(f32[8,32,128]{2,1,0:T(8,128)S(1)} %all-to-all-done.got_ref, f32[256,64]{1,0:T(8,128)S(1)} %get-tuple-element.26.wave_ref), custom_call_target="tpu_custom_call" | custom-call | tf_op jit(solution)/shard_map/x_section/pallas_call | solution.py:837
  38.8 8.8 %all-to-all-start.1 = ((f32[32,8,128]{2,1,0:T(8,128)}), f32[32,8,128]{2,1,0:T(8,128)S(1)}, u32[]{:S(2)}, u32[]{:S(2)}) async-start(f32[32,8,128]{2,1,0:T(8,128)} %x_section.1.after_hbm), calls=%async_computation.1 | async-start | bytes 262144 | tf_op jit(solution)/shard_map/all_to_all | solution.py:846
  47.6 0.0 collective-permute-done.2.prev_ref.prev_hbm
  47.6 0.0 copy-start.3
  47.6 0.0 copy-done.2
  47.6 1.6 %pack.1 = (f32[13,8,128]{2,1,0:T(8,128)S(1)}, f32[4,40,128]{2,1,0:T(8,128)S(1)}, f32[4,40,128]{2,1,0:T(8,128)S(1)}) custom-call(f32[13,32,128]{2,1,0:T(8,128)S(1)} %copy-done.2, f32[81,8,128]{2,1,0:T(8,128)S(1)} %collective-permute-done.1.rows_ref.next_ref.next_hbm, f32[52,8,128]{2,1,0:T(8,128)S(1)} %collective-permute-done.2.prev_ref.prev_hbm, ...), custom_call_target="tpu_custom_call" | custom-call | tf_op jit(solution)/shard_map/pack/pallas_call | solution.py:825
  49.2 0.0 copy-done.5
  49.2 0.0 copy-done
  49.2 0.0 copy-start.4
  49.2 0.6 copy-done.4
  49.8 0.2 collective-permute-start.3
  50.1 4.9 %collective-permute-start.4 = (f32[4,40,128]{2,1,0:T(8,128)S(1)}, f32[4,40,128]{2,1,0:T(8,128)S(1)}, u32[]{:S(2)}, u32[]{:S(2)}) collective-permute-start(f32[4,40,128]{2,1,0:T(8,128)S(1)} %get-tuple-element.25), channel_id=1, source_target_pairs={{1,0},{2,1},{3,2},{4,3},{5,4},{6,5},{7,6},{0,7},{9,8},{10,9},{11,1... | collective-permute-start | bytes 245768 | tf_op jit(solution)/shard_map/ppermute | solution.py:26
  54.9 2.5 %collective-permute-done.3.right_hbm = f32[4,40,128]{2,1,0:T(8,128)S(1)} collective-permute-done((f32[4,40,128]{2,1,0:T(8,128)S(1)}, f32[4,40,128]{2,1,0:T(8,128)S(1)}, u32[]{:S(2)}, u32[]{:S(2)}) %collective-permute-start.3) | collective-permute-done | bytes 81952 | tf_op jit(solution)/shard_map/ppermute | solution.py:26
  57.4 0.0 copy-start.7
  57.4 0.0 collective-permute-done.4.left_hbm
  57.4 0.0 copy-start.8
  57.4 0.0 copy-done.3
  57.4 0.6 copy-done.7
  58.0 0.0 copy-done.8
  58.1 9.1 %fields.1 = (f32[2,3,16,32,128]{4,3,2,1,0:T(8,128)}, f32[2,3,16,32,128]{4,3,2,1,0:T(8,128)}) custom-call(f32[2,3,16,32,128]{4,3,2,1,0:T(8,128)} %e_hbm.5, f32[2,3,16,32,128]{4,3,2,1,0:T(8,128)} %h_hbm.5, f32[16,32,128]{2,1,0:T(8,128)} %get-tuple-element.16.coef_hbm, f32[13,32,128]{2,1,0:T(8,128)} %get-tuple-element.17.own_ref.own_hbm, ...), custom_call_target="tpu_custom_call" | custom-call | tf_op jit(solution)/shard_map/fields/pallas_call | solution.py:847
  67.2 0.0 all-to-all-done.1.got_ref
  67.2 0.7 %order_sum.1 = f32[2,2,8,32]{3,2,1,0:T(8,128)} custom-call(f32[32,8,128]{2,1,0:T(8,128)S(1)} %all-to-all-done.1.got_ref), custom_call_target="tpu_custom_call" | custom-call | tf_op jit(solution)/shard_map/order_sum/pallas_call | solution.py:881
Async XLA Ops:
  4.3 13.3 %copy-start.6 = (f32[2]{0:T(128)S(1)}, f32[2]{0:T(128)}, u32[]{:S(2)}) copy-start(f32[2]{0:T(128)} %phase_hbm.1) | copy-start | bytes 28
  4.3 11.6 %collective-permute-start = (f32[2,32,128]{2,1,0:T(8,128)}, f32[2,32,128]{2,1,0:T(8,128)S(1)}, u32[]{:S(2)}, u32[]{:S(2)}) collective-permute-start(f32[2,32,128]{2,1,0:T(8,128)} %near.1.after_hbm), channel_id=1, source_target_pairs={{1,0},{2,1},{3,2},{4,3},{5,4},{6,5},{7,6},{0,7},{9,8},{10,9},{11,1... | collective-permute-start | bytes 98312 | tf_op jit(solution)/shard_map/ppermute | solution.py:26
  16.6 7.5 %collective-permute-start.1 = (f32[81,8,128]{2,1,0:T(8,128)}, f32[81,8,128]{2,1,0:T(8,128)S(1)}, u32[]{:S(2)}, u32[]{:S(2)}) collective-permute-start(f32[81,8,128]{2,1,0:T(8,128)} %slice_dynamic-update-slice_fusion), channel_id=1, source_target_pairs={{8,0},{16,8},{24,16},{32,24},{40,32},{48,40},{56,48},{64,56},{72,6... | collective-permute-start | bytes 995336 | tf_op jit(solution)/shard_map/ppermute | solution.py:26
  19.8 29.4 %copy-start.5 = (f32[8,128]{1,0:T(8,128)}, f32[8,128]{1,0:T(8,128)S(1)}, u32[]{:S(2)}) copy-start(f32[8,128]{1,0:T(8,128)S(1)} %get-tuple-element.20.rot_ref.rot_hbm) | copy-start | bytes 12292
  24.1 25.1 %copy-start = (f32[81,8,128]{2,1,0:T(8,128)}, f32[81,8,128]{2,1,0:T(8,128)S(1)}, u32[]{:S(2)}) copy-start(f32[81,8,128]{2,1,0:T(8,128)S(1)} %collective-permute-done.1.rows_ref.next_ref.next_hbm) | copy-start | bytes 995332
  24.1 1.3 %copy-start.1 = (f32[53,32,128]{2,1,0:T(8,128)S(1)}, f32[53,32,128]{2,1,0:T(8,128)}, u32[]{:S(2)}) copy-start(f32[53,32,128]{2,1,0:T(8,128)} %get-tuple-element.21.plane_ref) | copy-start | bytes 2605060
  25.4 5.6 %copy-start.9 = (f32[52,8,128]{2,1,0:T(8,128)S(1)}, f32[52,8,128]{2,1,0:T(8,128)}, u32[]{:S(2)}) copy-start(f32[52,8,128]{2,1,0:T(8,128)} %get-tuple-element.19) | copy-start | bytes 638980
  25.4 22.3 %copy-start.2 = (f32[13,32,128]{2,1,0:T(8,128)S(1)}, f32[13,32,128]{2,1,0:T(8,128)}, u32[]{:S(2)}) copy-start(f32[13,32,128]{2,1,0:T(8,128)} %get-tuple-element.17.own_ref.own_hbm) | copy-start | bytes 638980
  27.6 10.3 %all-to-all-start = ((f32[8,32,128]{2,1,0:T(8,128)}), f32[8,32,128]{2,1,0:T(8,128)S(1)}, u32[]{:S(2)}, u32[]{:S(2)}) async-start(f32[8,32,128]{2,1,0:T(8,128)} %plane.1.after_ref), calls=%async_computation | async-start | bytes 262144 | tf_op jit(solution)/shard_map/all_to_all | solution.py:836
  30.9 16.7 %collective-permute-start.2 = (f32[52,8,128]{2,1,0:T(8,128)S(1)}, f32[52,8,128]{2,1,0:T(8,128)S(1)}, u32[]{:S(2)}, u32[]{:S(2)}) collective-permute-start(f32[52,8,128]{2,1,0:T(8,128)S(1)} %copy-done.9), channel_id=1, source_target_pairs={{248,0},{0,8},{8,16},{16,24},{24,32},{32,40},{40,48},{48,56},{56,6... | collective-permute-start | bytes 638984 | tf_op jit(solution)/shard_map/ppermute | solution.py:26
  38.8 28.4 %all-to-all-start.1 = ((f32[32,8,128]{2,1,0:T(8,128)}), f32[32,8,128]{2,1,0:T(8,128)S(1)}, u32[]{:S(2)}, u32[]{:S(2)}) async-start(f32[32,8,128]{2,1,0:T(8,128)} %x_section.1.after_hbm), calls=%async_computation.1 | async-start | bytes 262144 | tf_op jit(solution)/shard_map/all_to_all | solution.py:846
  47.6 9.8 %copy-start.3 = (f32[52,8,128]{2,1,0:T(8,128)}, f32[52,8,128]{2,1,0:T(8,128)S(1)}, u32[]{:S(2)}) copy-start(f32[52,8,128]{2,1,0:T(8,128)S(1)} %collective-permute-done.2.prev_ref.prev_hbm) | copy-start | bytes 638980
  49.2 0.6 copy-start.4
  49.8 7.6 %collective-permute-start.3 = (f32[4,40,128]{2,1,0:T(8,128)S(1)}, f32[4,40,128]{2,1,0:T(8,128)S(1)}, u32[]{:S(2)}, u32[]{:S(2)}) collective-permute-start(f32[4,40,128]{2,1,0:T(8,128)S(1)} %get-tuple-element.24), channel_id=1, source_target_pairs={{7,0},{0,1},{1,2},{2,3},{3,4},{4,5},{5,6},{6,7},{15,8},{8,9},{9,10... | collective-permute-start | bytes 245768 | tf_op jit(solution)/shard_map/ppermute | solution.py:26
  50.1 7.3 %collective-permute-start.4 = (f32[4,40,128]{2,1,0:T(8,128)S(1)}, f32[4,40,128]{2,1,0:T(8,128)S(1)}, u32[]{:S(2)}, u32[]{:S(2)}) collective-permute-start(f32[4,40,128]{2,1,0:T(8,128)S(1)} %get-tuple-element.25), channel_id=1, source_target_pairs={{1,0},{2,1},{3,2},{4,3},{5,4},{6,5},{7,6},{0,7},{9,8},{10,9},{11,1... | collective-permute-start | bytes 245768 | tf_op jit(solution)/shard_map/ppermute | solution.py:26
  57.4 0.6 copy-start.7
  57.4 0.6 copy-start.8

commit v3 on v1

v3 whole, which is shorter than its diff:
```python
import functools
import math

import jax
import jax.numpy as jnp
from jax import lax
from jax.experimental import pallas as pl
from jax.experimental.pallas import tpu as pltpu
from jax.sharding import PartitionSpec as P

STEP_DT = 0.5
ORD_X = 256
ORD_Y = 256
NZ = 16
ROWS = 32
COLS = 128
EXT = 40
MAIN_BLOCKS = 52
VMEM = pltpu.VMEM
SMEM = pltpu.SMEM


def swapped(block, axis, first):
    count = lax.axis_size(axis)
    route = []
    for i in range(count):
        ahead = (i % 2 == 0) == first
        route.append((i, (i + 1) % count if ahead else (i - 1) % count))
    return lax.ppermute(block, axis, route)


def roll(values, shift, axis):
    size = values.shape[axis]
    if isinstance(shift, int):
        shift = shift % size
        if shift == 0:
            return values
    return pltpu.roll(values, shift, axis)


def lanes_of(shape):
    return lax.broadcasted_iota(jnp.int32, shape, len(shape) - 1)


def coef_table(base_ref, mode_ref, node_ref):
    lane = lanes_of((8, 128))
    material = lane // 16
    pattern = lane % 16
    base = jnp.zeros((8, 128), jnp.float32)
    for m in range(8):
        base = jnp.where(material == m, base_ref[m], base)
    change = jnp.zeros((8, 128), jnp.float32)
    for k in range(4):
        mode = jnp.zeros((8, 128), jnp.float32)
        for p in range(16):
            mode = jnp.where(pattern == p, mode_ref[k, p], mode)
        change = change + node_ref[k] * mode
    return STEP_DT / (base * (1.0 + change))


def look_up(table, pair):
    rows = [
        jnp.take_along_axis(table, pair[8 * r : 8 * r + 8], axis=1)
        for r in range(pair.shape[0] // 8)
    ]
    return jnp.concatenate(rows, axis=0)


def fetch(pairs, sem, first=0):
    copies = [
        pltpu.make_async_copy(source, target, sem.at[first + k])
        for k, (source, target) in enumerate(pairs)
    ]
    for copy in copies:
        copy.start()
    return copies


def arrived(copies):
    for copy in copies:
        copy.wait()


def is_even(axis):
    return lax.rem(lax.axis_index(axis), 2) == 0


def fetch_swapped(got, ahead_ref, behind_ref, even, sem, first):
    @pl.when(even)
    def _():
        fetch(((got[0], ahead_ref), (got[1], behind_ref)), sem, first)

    @pl.when(jnp.logical_not(even))
    def _():
        fetch(((got[1], ahead_ref), (got[0], behind_ref)), sem, first)

    return [
        pltpu.make_async_copy(got[k], ref, sem.at[first + k])
        for k, ref in enumerate((ahead_ref, behind_ref))
    ]


def plane_of(e_ref, h_ref, n, z):
    ref = e_ref if n < 6 else h_ref
    return ref[(n % 6) // 3, n % 3, z]


def rows_kernel(
    e_hbm,
    h_hbm,
    material_hbm,
    pattern_hbm,
    base_hbm,
    mode_hbm,
    node_hbm,
    table_ref,
    first_swap_ref,
    second_swap_ref,
    e_ref,
    h_ref,
    material_ref,
    pattern_ref,
    base_ref,
    mode_ref,
    node_ref,
    sem,
):
    small = fetch([(base_hbm, base_ref), (mode_hbm, mode_ref), (node_hbm, node_ref)], sem)
    ends = (slice(0, 8), slice(ROWS - 8, ROWS))
    large = fetch(
        [
            (source.at[..., end, :], target.at[k])
            for source, target in (
                (e_hbm, e_ref),
                (h_hbm, h_ref),
                (material_hbm, material_ref),
                (pattern_hbm, pattern_ref),
            )
            for k, end in enumerate(ends)
        ],
        sem,
        3,
    )
    even = is_even("gx")
    arrived(small)
    table = coef_table(base_ref, mode_ref, node_ref)
    table_ref[...] = table
    arrived(large)
    for n in range(13):
        for quad in range(NZ // 4):
            blocks = []
            for k in range(2):
                pieces = []
                for z in range(4 * quad, 4 * quad + 4):
                    if n == 12:
                        values = look_up(table, material_ref[k, z] * 16 + pattern_ref[k, z])
                    else:
                        ref = e_ref if n < 6 else h_ref
                        values = ref[k, (n % 6) // 3, n % 3, z]
                    pieces.append(values[6 * k : 6 * k + 2])
                blocks.append(jnp.concatenate(pieces, axis=0))
            first_swap_ref[4 * n + quad] = jnp.where(even, blocks[1], blocks[0])
            second_swap_ref[4 * n + quad] = jnp.where(even, blocks[0], blocks[1])


def own_kernel(
    e_hbm,
    h_hbm,
    material_hbm,
    pattern_hbm,
    table_hbm,
    own_ref,
    coef_ref,
    e_ref,
    h_ref,
    material_ref,
    pattern_ref,
    table_ref,
    sem,
):
    small = fetch(
        [(material_hbm, material_ref), (pattern_hbm, pattern_ref), (table_hbm, table_ref)], sem
    )
    large = fetch([(e_hbm, e_ref), (h_hbm, h_ref)], sem, 3)
    arrived(small)
    table = table_ref[...]
    for z in range(NZ):
        coef_ref[z] = look_up(table, material_ref[z] * 16 + pattern_ref[z])
    arrived(large)
    group = lanes_of((ROWS, COLS)) // 8
    for n in range(13):
        packed = jnp.zeros((ROWS, COLS), jnp.float32)
        for z in range(NZ):
            values = coef_ref[z] if n == 12 else plane_of(e_ref, h_ref, n, z)
            packed = jnp.where(group == z, roll(values, 8 * z + 6, 1), packed)
        own_ref[n] = packed


def bloch_factors(theta_x, theta_y):
    count_x, count_y = lax.axis_size("gx"), lax.axis_size("gy")
    index_x, index_y = lax.axis_index("gx"), lax.axis_index("gy")
    row = lax.broadcasted_iota(jnp.int32, (8, COLS), 0)
    angle = jnp.where(row < 4, theta_x, theta_y)
    flags = [
        jnp.where(flag, 1, 0)
        for flag in (index_x == count_x - 1, index_x == 0, index_y == 0, index_y == count_y - 1)
    ]
    here = jnp.where(
        row < 4,
        jnp.where(row < 2, flags[0], flags[1]),
        jnp.where(row < 6, flags[2], flags[3]),
    )
    angle = jnp.where(here == 1, angle, 0.0)
    angle = jnp.where(row // 2 == 1, -angle, jnp.where(row // 2 == 2, -angle, angle))
    return jnp.where(row % 2 == 0, jnp.cos(angle), jnp.sin(angle))


def pack_kernel(
    own_hbm,
    rows_a_hbm,
    rows_b_hbm,
    phase_hbm,
    all_ref,
    first_swap_ref,
    second_swap_ref,
    rot_ref,
    own_ref,
    next_ref,
    prev_ref,
    phase_ref,
    sem,
):
    small = fetch([(phase_hbm, phase_ref)], sem)
    copies = fetch([(own_hbm, own_ref)], sem, 1)
    copies += fetch_swapped(
        (rows_a_hbm, rows_b_hbm), next_ref, prev_ref, is_even("gx"), sem, 2
    )
    even = is_even("gy")
    arrived(small)
    rot_ref[...] = bloch_factors(phase_ref[0], phase_ref[1])
    arrived(copies)
    rot = [rot_ref[k : k + 1, :] for k in range(8)]
    group = lanes_of((2, COLS)) // 8
    place = lanes_of((EXT, COLS)) % 8
    for n in range(13):
        all_ref[n, 0:ROWS, :] = own_ref[n]
        all_ref[n, ROWS:EXT, :] = jnp.zeros((EXT - ROWS, COLS), jnp.float32)
    for ref, row, cos, sin in ((next_ref, 32, rot[0], rot[1]), (prev_ref, 38, rot[2], rot[3])):
        for n in (0, 1, 2, 6, 7, 8, 12):
            parts = 1 if n == 12 else 2
            packed = [jnp.zeros((2, COLS), jnp.float32) for _ in range(parts)]
            for quad in range(NZ // 4):
                values = [ref[4 * (n + 3 * part) + quad] for part in range(parts)]
                if parts == 2:
                    values = turned(values[0], values[1], cos, sin)
                for k in range(4):
                    z = 4 * quad + k
                    for part in range(parts):
                        packed[part] = jnp.where(
                            group == z,
                            roll(values[part][2 * k : 2 * k + 2], 8 * z + 6, 1),
                            packed[part],
                        )
            for part in range(parts):
                all_ref[n + 3 * part, row : row + 2, :] = packed[part]
    for c in range(4):
        if c == 3:
            right = left = all_ref[12]
        else:
            e_re, e_im, h_re, h_im = (all_ref[3 * k + c] for k in range(4))
            right = jnp.where(
                place < 4,
                jnp.where(place < 2, roll(h_re, -4, 1), roll(h_im, -2, 1)),
                jnp.where(place < 6, e_re, roll(e_im, 2, 1)),
            )
            left = jnp.where(
                place < 4,
                jnp.where(place < 2, roll(h_im, -6, 1), roll(h_re, -4, 1)),
                jnp.where(place < 6, roll(e_im, -2, 1), e_re),
            )
        first_swap_ref[c] = jnp.where(even, right, left)
        second_swap_ref[c] = jnp.where(even, left, right)


def turned(re, im, cos, sin):
    return re * cos - im * sin, im * cos + re * sin


def strip_of(own, right, left, rot):
    place = lanes_of(own[0].shape) % 8

    def joined(index, from_right, from_left):
        return jnp.where(
            place < 4,
            jnp.where(place < 2, roll(own[index], -4, 1), from_left),
            jnp.where(place < 6, from_right, own[index]),
        )

    strip = [None] * 13
    for c in range(3):
        r = right[c]
        l = left[c]
        e_right = turned(r, roll(r, -2, 1), rot[4], rot[5])
        h_right = turned(roll(r, 4, 1), roll(r, 2, 1), rot[4], rot[5])
        e_left = turned(roll(l, -4, 1), roll(l, -2, 1), rot[6], rot[7])
        h_left = turned(l, roll(l, 2, 1), rot[6], rot[7])
        for part in range(2):
            strip[3 * part + c] = joined(3 * part + c, e_right[part], e_left[part])
            strip[6 + 3 * part + c] = joined(6 + 3 * part + c, h_right[part], h_left[part])
    strip[12] = joined(12, right[3], roll(left[3], -4, 1))
    return strip


def next_row(values):
    return roll(values, -1, 0)


def prev_row(values):
    return roll(values, 1, 0)


def h_new(h, e, e_up, e_xn, e_yn):
    return (
        h[0] - STEP_DT * (e_yn[1] - e[2] - (e_up[1] - e[1])),
        h[1] - STEP_DT * (e_up[0] - e[0] - (e_xn[1] - e[2])),
        h[2] - STEP_DT * (e_xn[0] - e[1] - (e_yn[0] - e[0])),
    )


def e_new(e, h, h_down, h_xp, h_yp, coef):
    return (
        e[0] + coef * (h[2] - h_yp[1] - (h[1] - h_down[1])),
        e[1] + coef * (h[0] - h_down[0] - (h[2] - h_xp[1])),
        e[2] + coef * (h[1] - h_xp[0] - (h[0] - h_yp[0])),
    )


def strip_h(h, e):
    up = lanes_of((EXT, COLS)) < 8 * (NZ - 1)
    above = [jnp.where(up, roll(e[c], -8, 1), 0.0) for c in range(2)]
    return h_new(
        h,
        e,
        above,
        (next_row(e[1]), next_row(e[2])),
        (roll(e[0], -1, 1), roll(e[2], -1, 1)),
    )


def strip_e(e, h, coef):
    up = lanes_of((EXT, COLS)) >= 8
    below = [jnp.where(up, roll(h[c], 8, 1), 0.0) for c in range(2)]
    return e_new(
        e,
        h,
        below,
        (prev_row(h[1]), prev_row(h[2])),
        (roll(h[0], 1, 1), roll(h[2], 1, 1)),
        coef,
    )


def fetch_edges(own_hbm, rows_hbm, cols_hbm, rot_hbm, edges, sem, first):
    own_ref, next_ref, prev_ref, right_ref, left_ref, rot_ref = edges
    copies = fetch([(own_hbm, own_ref), (rot_hbm, rot_ref)], sem, first)
    copies += fetch_swapped(rows_hbm, next_ref, prev_ref, is_even("gx"), sem, first + 2)
    copies += fetch_swapped(cols_hbm, left_ref, right_ref, is_even("gy"), sem, first + 4)
    return copies


def edge_scratch():
    return [
        VMEM(shape, jnp.float32)
        for shape in (
            (13, EXT, COLS),
            (MAIN_BLOCKS, 8, COLS),
            (MAIN_BLOCKS, 8, COLS),
            (4, EXT, COLS),
            (4, EXT, COLS),
            (8, COLS),
        )
    ]


def block_scratch(parts):
    return [
        VMEM((parts, 3, NZ + 1, EXT, COLS), jnp.float32),
        VMEM((parts, 3, NZ + 1, EXT, COLS), jnp.float32),
        VMEM((NZ, EXT, COLS), jnp.float32),
        VMEM((parts, 4, 2, EXT, COLS), jnp.float32),
    ]


def fill_edges(edges, block, parts):
    own_ref, next_ref, prev_ref, right_ref, left_ref, rot_ref = edges
    e_all, h_all, coef_all, edge_ref = block
    rot = [rot_ref[k : k + 1, :] for k in range(8)]
    for at in range(len(parts)):
        for c in range(3):
            e_all[at, c, NZ] = jnp.zeros((EXT, COLS), jnp.float32)
            h_all[at, c, 0] = jnp.zeros((EXT, COLS), jnp.float32)
    for ref, row, cos, sin in ((next_ref, 32, rot[0], rot[1]), (prev_ref, 38, rot[2], rot[3])):
        for field in range(2):
            dest = h_all if field else e_all
            for c in range(3):
                for quad in range(4):
                    re = ref[(6 * field + c) * 4 + quad]
                    im = ref[(6 * field + 3 + c) * 4 + quad]
                    both = turned(re, im, cos, sin)
                    for at, part in enumerate(parts):
                        for k in range(4):
                            z = 4 * quad + k + field
                            dest[at, c, z, row : row + 2, :] = both[part][2 * k : 2 * k + 2]
        for quad in range(4):
            values = ref[48 + quad]
            for k in range(4):
                coef_all[4 * quad + k, row : row + 2, :] = values[2 * k : 2 * k + 2]
    strip = strip_of(
        [own_ref[a] for a in range(13)],
        [right_ref[a] for a in range(4)],
        [left_ref[a] for a in range(4)],
        rot,
    )
    for at, part in enumerate(parts):
        e = tuple(strip[3 * part + c] for c in range(3))
        h = tuple(strip[6 + 3 * part + c] for c in range(3))
        for step in range(2):
            edge_ref[at, 2 * step, 0] = e[0]
            edge_ref[at, 2 * step, 1] = e[2]
            h = strip_h(h, e)
            edge_ref[at, 2 * step + 1, 0] = h[0]
            edge_ref[at, 2 * step + 1, 1] = h[2]
            if step == 0:
                e = strip_e(e, h, strip[12])


def updates(block, parts):
    e_all, h_all, coef_all, edge_ref = block
    lane = lanes_of((EXT, COLS))

    def next_col(values, edge, z):
        edge = roll(edge, lax.rem(COLS + 125 - 8 * z, COLS), 1)
        return jnp.where(lane == COLS - 1, edge, roll(values, -1, 1))

    def prev_col(values, edge, z):
        edge = roll(edge, lax.rem(COLS + 123 - 8 * z, COLS), 1)
        return jnp.where(lane == 0, edge, roll(values, 1, 1))

    def do_h(step, layers):
        new = []
        for at in range(parts):
            for z in layers:
                e = tuple(e_all[at, c, z] for c in range(3))
                h = tuple(h_all[at, c, z + 1] for c in range(3))
                e_up = (e_all[at, 0, z + 1], e_all[at, 1, z + 1])
                e_yn = (
                    next_col(e[0], edge_ref[at, 2 * step, 0], z),
                    next_col(e[2], edge_ref[at, 2 * step, 1], z),
                )
                values = h_new(h, e, e_up, (next_row(e[1]), next_row(e[2])), e_yn)
                new.append((at, z, values))
        for at, z, values in new:
            for c in range(3):
                h_all[at, c, z + 1] = values[c]

    def do_e(step, layers):
        new = []
        for at in range(parts):
            for z in layers:
                e = tuple(e_all[at, c, z] for c in range(3))
                h = tuple(h_all[at, c, z + 1] for c in range(3))
                h_down = (h_all[at, 0, z], h_all[at, 1, z])
                h_yp = (
                    prev_col(h[0], edge_ref[at, 2 * step + 1, 0], z),
                    prev_col(h[2], edge_ref[at, 2 * step + 1, 1], z),
                )
                values = e_new(
                    e, h, h_down, (prev_row(h[1]), prev_row(h[2])), h_yp, coef_all[z]
                )
                new.append((at, z, values))
        for at, z, values in new:
            for c in range(3):
                e_all[at, c, z] = values[c]

    return do_h, do_e


def plane_kernel(
    e_hbm,
    h_hbm,
    coef_hbm,
    own_hbm,
    rows_a_hbm,
    rows_b_hbm,
    cols_a_hbm,
    cols_b_hbm,
    rot_hbm,
    wave_hbm,
    monitor_hbm,
    spread_ref,
    *scratch,
):
    edges, block = scratch[0:6], scratch[6:10]
    wave_ref, monitor_ref, sem = scratch[10:13]
    e_all, h_all, coef_all, edge_ref = block
    scalar = fetch([(monitor_hbm, monitor_ref)], sem)
    copies = fetch_edges(
        own_hbm,
        (rows_a_hbm, rows_b_hbm),
        (cols_a_hbm, cols_b_hbm),
        rot_hbm,
            edges,
        sem,
        1,
    )
    arrived(scalar)
    level = monitor_ref[0]
    low = jnp.clip(level - 2, 0, NZ - 5)
    large = fetch(
        [
            (e_hbm.at[:, :, pl.ds(low, 5)], e_all.at[:, :, pl.ds(low, 5), 0:ROWS, :]),
            (h_hbm.at[:, :, pl.ds(low, 5)], h_all.at[:, :, pl.ds(low + 1, 5), 0:ROWS, :]),
            (coef_hbm.at[pl.ds(low, 5)], coef_all.at[pl.ds(low, 5), 0:ROWS, :]),
            (wave_hbm, wave_ref),
        ],
        sem,
        7,
    )
    arrived(copies)
    fill_edges(edges, block, (0, 1))
    arrived(large)
    near = {}
    for k in range(-2, 3):
        z = jnp.clip(level + k, 0, NZ - 1)
        for part in range(2):
            for c in range(3):
                if c < 2 or k < 2:
                    e = e_all[part, c, z]
                    near["e", part, c, k] = jnp.where(level + k < NZ, e, 0.0) if k > 0 else e
                if k < 2 and (c < 2 or k > -2):
                    h = h_all[part, c, z + 1]
                    near["h", part, c, k] = jnp.where(level + k >= 0, h, 0.0) if k < 0 else h
    lane = lanes_of((EXT, COLS))

    def next_col(values, edge, z):
        edge = roll(edge, lax.rem(COLS + 125 - 8 * z, COLS), 1)
        return jnp.where(lane == COLS - 1, edge, roll(values, -1, 1))

    def prev_col(values, edge, z):
        edge = roll(edge, lax.rem(COLS + 123 - 8 * z, COLS), 1)
        return jnp.where(lane == 0, edge, roll(values, 1, 1))

    def update_h(step, part, k, wanted):
        z = jnp.clip(level + k, 0, NZ - 1)
        ex, ey, ez = (near["e", part, c, k] for c in range(3))
        edge = edge_ref.at[part, 2 * step]
        new = {}
        if 0 in wanted:
            new[0] = next_col(ez, edge[1], z) - ez - (near["e", part, 1, k + 1] - ey)
        if 1 in wanted:
            new[1] = near["e", part, 0, k + 1] - ex - (next_row(ez) - ez)
        if 2 in wanted:
            new[2] = next_row(ey) - ey - (next_col(ex, edge[0], z) - ex)
        for c, curl in new.items():
            values = near["h", part, c, k] - STEP_DT * curl
            near["h", part, c, k] = jnp.where(level + k >= 0, values, 0.0) if k < 0 else values

    def update_e(step, part, k, wanted):
        z = jnp.clip(level + k, 0, NZ - 1)
        hx, hy, hz = (near["h", part, c, k] for c in range(3))
        edge = edge_ref.at[part, 2 * step + 1]
        coef = coef_all[z]
        new = {}
        if 0 in wanted:
            new[0] = hz - prev_col(hz, edge[1], z) - (hy - near["h", part, 1, k - 1])
        if 1 in wanted:
            new[1] = hx - near["h", part, 0, k - 1] - (hz - prev_row(hz))
        if 2 in wanted:
            new[2] = hy - prev_row(hy) - (hx - prev_col(hx, edge[0], z))
        for c, curl in new.items():
            values = near["e", part, c, k] + coef * curl
            near["e", part, c, k] = jnp.where(level + k < NZ, values, 0.0) if k > 0 else values

    for part in range(2):
        for k in range(-2, 2):
            update_h(0, part, k, (0, 1, 2) if k > -2 else (0, 1))
        for k in range(-1, 2):
            update_e(0, part, k, (0, 1, 2) if k < 1 else (0, 1))
        update_h(1, part, -1, (0, 1))
        update_h(1, part, 0, (0, 1, 2))
        update_e(1, part, 0, (0, 1))
    re, im = (
        jnp.concatenate([near["e", part, c, 0][0:ROWS] for c in range(2)], axis=0)
        for part in range(2)
    )
    y_section(re, im, wave_ref, spread_ref)


def field_kernel(parts, inputs, *refs):
    (
        e_hbm,
        h_hbm,
        coef_hbm,
        own_hbm,
        rows_a_hbm,
        rows_b_hbm,
        cols_a_hbm,
        cols_b_hbm,
        rot_hbm,
        ) = refs[0:9]
    e_out, h_out = refs[inputs : inputs + 2]
    scratch = refs[inputs + 2 :]
    edges, block, sem = scratch[0:6], scratch[6:10], scratch[10]
    e_all, h_all, coef_all, _ = block
    copies = fetch_edges(
        own_hbm,
        (rows_a_hbm, rows_b_hbm),
        (cols_a_hbm, cols_b_hbm),
        rot_hbm,
            edges,
        sem,
        0,
    )
    large = fetch(
        [
            (coef_hbm, coef_all.at[:, 0:ROWS, :]),
            (e_hbm.at[parts[0] : parts[-1] + 1], e_all.at[:, :, 0:NZ, 0:ROWS, :]),
            (h_hbm.at[parts[0] : parts[-1] + 1], h_all.at[:, :, 1 : NZ + 1, 0:ROWS, :]),
        ],
        sem,
        6,
    )
    arrived(copies)
    fill_edges(edges, block, parts)
    arrived(large)
    do_h, do_e = updates(block, len(parts))

    def sweep(update, step, store=None):
        def layers(quad, carry):
            start = 4 * quad
            update(step, [start + k for k in range(4)])
            if store is not None:
                store(start)
            return carry

        lax.fori_loop(0, NZ // 4, layers, 0)

    def store_h(start):
        fetch(
            [
                (
                    h_all.at[at, :, pl.ds(start + 1, 4), 0:ROWS, :],
                    h_out.at[part, :, pl.ds(start, 4)],
                )
                for at, part in enumerate(parts)
            ],
            sem,
            10,
        )

    def store_e(start):
        fetch(
            [
                (
                    e_all.at[at, :, pl.ds(start, 4), 0:ROWS, :],
                    e_out.at[part, :, pl.ds(start, 4)],
                )
                for at, part in enumerate(parts)
            ],
            sem,
            12,
        )

    sweep(do_h, 0)
    sweep(do_e, 0)
    sweep(do_h, 1, store_h)
    sweep(do_e, 1, store_e)
    for at, part in enumerate(parts):
        pltpu.make_async_copy(
            h_all.at[at, :, 1 : NZ + 1, 0:ROWS, :], h_out.at[part], sem.at[10 + at]
        ).wait()
        pltpu.make_async_copy(
            e_all.at[at, :, 0:NZ, 0:ROWS, :], e_out.at[part], sem.at[12 + at]
        ).wait()


def y_section(re, im, wave_ref, spread_ref):
    wave = wave_ref[...]
    owners, _, lanes = spread_ref.shape
    each = lanes // 4
    out = [
        jnp.dot(
            jnp.concatenate(pair, axis=1),
            wave,
            precision=lax.Precision.HIGHEST,
            preferred_element_type=jnp.float32,
        )
        for pair in ((re, im), (im, -re))
    ]
    for owner in range(owners):
        pieces = [
            out[part][c * ROWS : (c + 1) * ROWS, owner * each : (owner + 1) * each]
            for part in range(2)
            for c in range(2)
        ]
        spread_ref[owner] = jnp.concatenate(pieces, axis=1)


def x_kernel(got_ref, wave_ref, part_ref):
    total = got_ref[0]
    for source in range(1, got_ref.shape[0]):
        total = total + got_ref[source]
    half = total.shape[1] // 2
    other = roll(total, half, 1)
    other = jnp.where(lanes_of(other.shape) < half, other, -other)
    result = jnp.dot(
        wave_ref[...],
        jnp.concatenate([total, other], axis=0),
        precision=lax.Precision.HIGHEST,
        preferred_element_type=jnp.float32,
    )
    part_ref[...] = result.reshape(part_ref.shape)


def sum_kernel(got_ref, out_ref):
    total = got_ref[0]
    for source in range(1, got_ref.shape[0]):
        total = total + got_ref[source]
    each = total.shape[1] // 4
    for c in range(2):
        for part in range(2):
            start = (2 * part + c) * each
            out_ref[c, part] = total[:, start : start + each]


def table_kernel(
    count_x, count_y, phase_hbm, after_hbm, y_ref, x_ref, phase_ref, sem
):
    arrived(fetch([(phase_hbm, phase_ref)], sem))
    index_x, index_y = lax.axis_index("gx"), lax.axis_index("gy")
    theta_x, theta_y = phase_ref[0], phase_ref[1]
    total_x, total_y = ROWS * count_x, COLS * count_y

    def waves(product, place, total, theta):
        angle = (
            2.0 * math.pi * (product & (total - 1)).astype(jnp.float32)
            + theta * place.astype(jnp.float32)
        ) / total
        return jnp.cos(angle), jnp.sin(angle)

    def joined(a, b):
        return a[0] * b[0] - a[1] * b[1], a[1] * b[0] + a[0] * b[1]

    scale = 1.0 / math.sqrt(total_x * total_y)
    blocks = COLS // 8
    start = index_y * COLS
    order = lax.broadcasted_iota(jnp.int32, (blocks, ORD_Y), 1) - ORD_Y // 2
    place = start + 8 * lax.broadcasted_iota(jnp.int32, (blocks, ORD_Y), 0)
    coarse = waves(order * place, place, total_y, theta_y)
    place = lax.broadcasted_iota(jnp.int32, (8, ORD_Y), 0)
    fine = waves(order[0:8] * place, place, total_y, theta_y)
    fine = (fine[0] * scale, fine[1] * scale)
    for block in range(blocks):
        part = tuple(values[block : block + 1] for values in coarse)
        cos, sin = joined(part, fine)
        y_ref[8 * block : 8 * block + 8, :] = cos
        y_ref[COLS + 8 * block : COLS + 8 * block + 8, :] = sin
    blocks = ORD_X // 8
    shape = (blocks, 2 * ROWS)
    place = index_x * ROWS + lax.broadcasted_iota(jnp.int32, shape, 1) % ROWS
    order = 8 * lax.broadcasted_iota(jnp.int32, shape, 0) - ORD_X // 2
    coarse = waves(order * place, place, total_x, theta_x)
    order = lax.broadcasted_iota(jnp.int32, (8, 2 * ROWS), 0)
    fine = waves(order * place[0:8], place[0:8], total_x, 0.0)
    lane = lax.broadcasted_iota(jnp.int32, (8, 2 * ROWS), 1)
    for block in range(blocks):
        part = tuple(values[block : block + 1] for values in coarse)
        cos, sin = joined(part, fine)
        x_ref[8 * block : 8 * block + 8, :] = jnp.where(lane < ROWS, cos, sin)


def params(mebibytes):
    return pltpu.CompilerParams(vmem_limit_bytes=mebibytes << 20)


def cost(microseconds):
    return pl.CostEstimate(
        flops=0, bytes_accessed=microseconds * 3_000_000, transcendentals=0
    )


def f32(*shape):
    return jax.ShapeDtypeStruct(shape, jnp.float32)


def shards(
    e_field, h_field, material, pattern, base_eps, mode_table, nodes, bloch_phase, monitor_z
):
    count_x = lax.axis_size("gx")
    count_y = lax.axis_size("gy")
    each_p = ORD_X // count_x
    each_q = ORD_Y // count_y
    vmem = pl.BlockSpec(memory_space=VMEM)
    hbm = pl.BlockSpec(memory_space=pltpu.HBM)
    f32_vmem = lambda *shape: VMEM(shape, jnp.float32)
    dma = pltpu.SemaphoreType.DMA

    table, rows_a, rows_b = pl.pallas_call(
        rows_kernel,
        out_shape=(
            f32(8, COLS),
            f32(MAIN_BLOCKS, 8, COLS),
            f32(MAIN_BLOCKS, 8, COLS),
        ),
        in_specs=[hbm] * 7,
        out_specs=(vmem,) * 3,
        scratch_shapes=[
            f32_vmem(2, 2, 3, NZ, 8, COLS),
            f32_vmem(2, 2, 3, NZ, 8, COLS),
            VMEM((2, NZ, 8, COLS), jnp.int32),
            VMEM((2, NZ, 8, COLS), jnp.int32),
            SMEM(base_eps.shape, jnp.float32),
            SMEM(mode_table.shape, jnp.float32),
            SMEM(nodes.shape, jnp.float32),
            dma((11,)),
        ],
        compiler_params=params(60),
        cost_estimate=cost(3),
        name="rows",
    )(e_field, h_field, material, pattern, base_eps, mode_table, nodes)
    rows_a = swapped(rows_a, "gx", True)
    rows_b = swapped(rows_b, "gx", False)
    own, coef = pl.pallas_call(
        own_kernel,
        out_shape=(f32(13, ROWS, COLS), f32(NZ, ROWS, COLS)),
        in_specs=[hbm] * 5,
        out_specs=(vmem,) * 2,
        scratch_shapes=[
            f32_vmem(*e_field.shape),
            f32_vmem(*h_field.shape),
            VMEM(material.shape, jnp.int32),
            VMEM(pattern.shape, jnp.int32),
            f32_vmem(8, COLS),
            dma((5,)),
        ],
        compiler_params=params(60),
        cost_estimate=cost(4),
        name="own",
    )(e_field, h_field, material, pattern, table)
    own, cols_a, cols_b, rot = pl.pallas_call(
        pack_kernel,
        out_shape=(
            f32(13, EXT, COLS),
            f32(4, EXT, COLS),
            f32(4, EXT, COLS),
            f32(8, COLS),
        ),
        in_specs=[hbm] * 4,
        out_specs=(vmem,) * 4,
        scratch_shapes=[
            f32_vmem(*own.shape),
            f32_vmem(MAIN_BLOCKS, 8, COLS),
            f32_vmem(MAIN_BLOCKS, 8, COLS),
            SMEM((2,), jnp.float32),
            dma((4,)),
        ],
        compiler_params=params(60),
        cost_estimate=cost(2),
        name="pack",
    )(own, rows_a, rows_b, bloch_phase)
    y_wave, x_wave = pl.pallas_call(
        functools.partial(table_kernel, count_x, count_y),
        out_shape=(f32(2 * COLS, ORD_Y), f32(ORD_X, 2 * ROWS)),
        in_specs=[hbm, hbm],
        out_specs=(vmem,) * 2,
        scratch_shapes=[SMEM((2,), jnp.float32), dma((1,))],
        compiler_params=params(60),
        cost_estimate=cost(2),
        name="tables",
    )(bloch_phase, rot)
    cols_b = swapped(cols_b, "gy", False)
    cols_a = swapped(cols_a, "gy", True)
    around = (e_field, h_field, coef, own, rows_a, rows_b, cols_a, cols_b, rot)
    spread = pl.pallas_call(
        plane_kernel,
        out_shape=f32(count_y, ROWS, 4 * each_q),
        in_specs=[hbm] * 11,
        out_specs=vmem,
        scratch_shapes=[
            *edge_scratch(),
            *block_scratch(2),
            f32_vmem(*y_wave.shape),
            SMEM((1,), jnp.int32),
            dma((11,)),
        ],
        compiler_params=params(60),
        cost_estimate=cost(3),
        name="plane",
    )(*around, y_wave, monitor_z)

    def fields(parts, after, before=()):
        return pl.pallas_call(
            functools.partial(field_kernel, parts, 10 + len(before)),
            out_shape=(f32(*e_field.shape), f32(*h_field.shape)),
            in_specs=[hbm] * (10 + len(before)),
            out_specs=(hbm, hbm),
            scratch_shapes=[*edge_scratch(), *block_scratch(len(parts)), dma((14,))],
            input_output_aliases={10 + k: k for k in range(len(before))},
            compiler_params=params(60),
            cost_estimate=cost(6),
            name="fields",
        )(*around, after, *before)

    got = lax.all_to_all(spread, "gy", 0, 0, tiled=True)
    partial = pl.pallas_call(
        x_kernel,
        out_shape=f32(count_x, each_p, 4 * each_q),
        in_specs=[vmem, vmem],
        out_specs=vmem,
        compiler_params=params(8),
        cost_estimate=cost(1),
        name="x_section",
    )(got, x_wave)
    got = lax.all_to_all(partial, "gx", 0, 0, tiled=True)
    e_out, h_out = fields((0, 1), partial)
    orders = pl.pallas_call(
        sum_kernel,
        out_shape=f32(2, 2, each_p, each_q),
        in_specs=[vmem],
        out_specs=vmem,
        compiler_params=params(8),
        cost_estimate=cost(1),
        name="order_sum",
    )(got)
    return e_out, h_out, orders


def solution(mesh):
    grid = P(None, None, None, "gx", "gy")
    cells = P(None, "gx", "gy")
    return jax.shard_map(
        shards,
        mesh=mesh,
        in_specs=(grid, grid, cells, cells, P(), P(), P(), P(), P()),
        out_specs=(grid, grid, P(None, None, "gx", "gy")),
        check_vma=False,
    )
```

time: 87.2 us -> 62.6 us (0.72)
  local copies, waits for them, and re-layouts: 15.4 us -> 1.32 us
  blocking collectives: 21.4 us -> 12 us
  other arithmetic: 6.41 us -> 0 us
  starting transfers between devices: 15.4 us -> 20.1 us
  Pallas kernels: 18.5 us -> 22.8 us
  between operations: 4.31 us -> 1.39 us
    unnamed x34 -> x10, local copies, waits for them, and re-layouts: 12 us -> 1.32 us
    all_to_all x1, blocking collectives: 21.4 us -> 12 us  [shards(): got = lax.all_to_all(spread, 'gy', 0, 0, tiled=True)]
    all_to_all x1, starting transfers between devices: 6.47 us -> 12.8 us  [shards(): got = lax.all_to_all(partial, 'gx', 0, 0, tiled=True)]
    pallas_call x2 -> x6, Pallas kernels: 14.9 us -> 21.2 us  [the longest x1 7.3 us: fields(): pl.pallas_call(functools.partial(field_kernel, parts, 10 + len(before)),...]
    all_to_all x1, waiting for transfers between devices: 5.22 us -> 1.76 us  [shards(): got = lax.all_to_all(partial, 'gx', 0, 0, tiled=True)]
    ppermute x4, waiting for transfers between devices: 0.01 us -> 2.73 us  [swapped(): return lax.ppermute(block, axis, route)]
    cos x2 -> x0, other arithmetic: 2.68 us -> none  [the longest x1 2.08 us: shards(): x_wave = jnp.concatenate([jnp.cos(x_angle), jnp.sin(x_angle)], axis=1)]
    concatenate x3 -> x0, other arithmetic: 1.73 us -> none  [the longest x1 1.72 us: shards(): x_wave = jnp.concatenate([jnp.cos(x_angle), jnp.sin(x_angle)], axis=1)]
  transfers between devices with their start and end apart: 5 -> 5, of which waited for: 1 -> 3; matrix products, arithmetic and copies ran while one was open for 11% -> 0% of each run, Pallas kernels for 0% -> 20%
where the time goes in v3:
time: 62.6 us; the launch traced here: 62.2 us
  Pallas kernels  22.8 us (36%)
  starting transfers between devices  20.1 us (32%)
  blocking collectives  12 us (19%)
  waiting for transfers between devices  4.48 us (7%)
  between operations  1.39 us (2%)
  local copies, waits for them, and re-layouts  1.32 us (2%)
    all_to_all x1, starting transfers between devices, shards(): got = lax.all_to_all(partial, 'gx', 0, 0, tiled=True)  12.8 us
    all_to_all x1, blocking collectives, shards(): got = lax.all_to_all(spread, 'gy', 0, 0, tiled=True)  12 us
    ppermute x4, starting transfers between devices, swapped(): return lax.ppermute(block, axis, route)  7.33 us
    pallas_call x1, Pallas kernels, fields(): pl.pallas_call(functools.partial(field_kernel, parts, 10 + len(before)),...  7.3 us
    pallas_call x1, Pallas kernels, shards(): pl.pallas_call(own_kernel, out_shape=(f32(13, ROWS, COLS), f32(NZ, ROWS,...  3.75 us
    pallas_call x1, Pallas kernels, shards(): pl.pallas_call(plane_kernel, out_shape=f32(count_y, ROWS, 4 * each_q), in...  3.62 us
    ppermute x4, waiting for transfers between devices, swapped(): return lax.ppermute(block, axis, route)  2.73 us
    pallas_call x1, Pallas kernels, shards(): pl.pallas_call(rows_kernel, out_shape=(f32(8, COLS), f32(MAIN_BLOCKS, 8,...  2.45 us
  transfers between devices with their start and end apart: 5, of which 3 were waited for; matrix products, arithmetic and copies ran while one was open for 0% of the time, Pallas kernels for 20%

profile of v3, /device:TPU:1, one launch (start us, length us, event | category | flops | bytes accessed | tf_op | source)
XLA Modules:
  0.0 62.2 jit_solution(13815518361391013155)
XLA Ops:
  0.6 2.5 %rows.1 = (f32[8,128]{1,0:T(8,128)}, f32[52,8,128]{2,1,0:T(8,128)}, f32[52,8,128]{2,1,0:T(8,128)}) custom-call(f32[2,3,16,32,128]{4,3,2,1,0:T(8,128)} %refs_0_.1, f32[2,3,16,32,128]{4,3,2,1,0:T(8,128)} %refs_1_.1, s32[16,32,128]{2,1,0:T(8,128)} %material_hbm.3, s32[16,32,128]{2,1,0:T(8,128)} %pattern_hbm.3, f32[8]{0:T(128)} %base_hbm.1, f32[4,16]{1,0:T(4,128)} %mode_hbm.1, ...), custom_call_target="tpu_custom_call" | custom-call | bytes 9000000 | tf_op jit(solution)/shard_map/rows/pallas_call | solution.py:808
  3.1 3.3 %collective-permute-start = (f32[52,8,128]{2,1,0:T(8,128)}, f32[52,8,128]{2,1,0:T(8,128)S(1)}, u32[]{:S(2)}, u32[]{:S(2)}) collective-permute-start(f32[52,8,128]{2,1,0:T(8,128)} %get-tuple-element.19), channel_id=1, source_target_pairs={{0,8},{8,0},{16,24},{24,16},{32,40},{40,32},{48,56},{56,48},{64,72... | collective-permute-start | bytes 638984 | tf_op jit(solution)/shard_map/ppermute | solution.py:29
  6.4 0.0 collective-permute-start.1
  6.4 3.7 %own.1 = (f32[13,32,128]{2,1,0:T(8,128)}, f32[16,32,128]{2,1,0:T(8,128)}) custom-call(f32[2,3,16,32,128]{4,3,2,1,0:T(8,128)} %refs_0_.1, f32[2,3,16,32,128]{4,3,2,1,0:T(8,128)} %refs_1_.1, s32[16,32,128]{2,1,0:T(8,128)} %material_hbm.3, s32[16,32,128]{2,1,0:T(8,128)} %pattern_hbm.3, f32[8,128]{1,0:T(8,128)} %get-tuple-element.16.table_hbm), custom_call_target="tpu_custom_call" | custom-call | bytes 12000000 | tf_op jit(solution)/shard_map/own/pallas_call | solution.py:833
  10.2 0.0 collective-permute-done.rows_a_hbm.refs_4_
  10.2 0.0 copy-start.1
  10.2 1.7 %collective-permute-done.1.rows_b_hbm.refs_5_ = f32[52,8,128]{2,1,0:T(8,128)S(1)} collective-permute-done((f32[52,8,128]{2,1,0:T(8,128)}, f32[52,8,128]{2,1,0:T(8,128)S(1)}, u32[]{:S(2)}, u32[]{:S(2)}) %collective-permute-start.1) | collective-permute-done | bytes 213024 | tf_op jit(solution)/shard_map/ppermute | solution.py:29
  11.9 0.0 copy-start.2
  11.9 0.0 copy-done.1
  11.9 0.7 %copy-done.2 = f32[52,8,128]{2,1,0:T(8,128)} copy-done((f32[52,8,128]{2,1,0:T(8,128)}, f32[52,8,128]{2,1,0:T(8,128)S(1)}, u32[]{:S(2)}) %copy-start.2) | copy-done | bytes 213016
  12.6 2.4 %pack.1 = (f32[13,40,128]{2,1,0:T(8,128)}, f32[4,40,128]{2,1,0:T(8,128)}, f32[4,40,128]{2,1,0:T(8,128)}, f32[8,128]{1,0:T(8,128)}) custom-call(f32[13,32,128]{2,1,0:T(8,128)} %get-tuple-element.18.own_hbm, f32[52,8,128]{2,1,0:T(8,128)} %copy-done.1, f32[52,8,128]{2,1,0:T(8,128)} %copy-done.2, f32[2]{0:T(128)} %phase_hbm.3), custom_call_target="tpu_custom_call" | custom-call | bytes 6000000 | tf_op jit(solution)/shard_map/pack/pallas_call | solution.py:850
  15.0 0.1 collective-permute-start.2
  15.1 3.9 %collective-permute-start.3 = (f32[4,40,128]{2,1,0:T(8,128)}, f32[4,40,128]{2,1,0:T(8,128)S(1)}, u32[]{:S(2)}, u32[]{:S(2)}) collective-permute-start(f32[4,40,128]{2,1,0:T(8,128)} %get-tuple-element.23), channel_id=1, source_target_pairs={{0,7},{1,2},{2,1},{3,4},{4,3},{5,6},{6,5},{7,0},{8,15},{9,10},{10,... | collective-permute-start | bytes 245768 | tf_op jit(solution)/shard_map/ppermute | solution.py:29
  19.7 1.6 %tables.1 = (f32[256,256]{1,0:T(8,128)}, f32[256,64]{1,0:T(8,128)}) custom-call(f32[2]{0:T(128)} %phase_hbm.3, f32[8,128]{1,0:T(8,128)} %get-tuple-element.24.after_hbm.rot_hbm.refs_8_), custom_call_target="tpu_custom_call" | custom-call | bytes 6000000 | tf_op jit(solution)/shard_map/tables/pallas_call | solution.py:871
  21.3 0.0 collective-permute-done.2.cols_a_hbm.refs_6_
  21.3 0.0 copy-start.3
  21.3 1.0 %collective-permute-done.3.cols_b_hbm.refs_7_ = f32[4,40,128]{2,1,0:T(8,128)S(1)} collective-permute-done((f32[4,40,128]{2,1,0:T(8,128)}, f32[4,40,128]{2,1,0:T(8,128)S(1)}, u32[]{:S(2)}, u32[]{:S(2)}) %collective-permute-start.3) | collective-permute-done | bytes 81952 | tf_op jit(solution)/shard_map/ppermute | solution.py:29
  22.3 0.0 copy-start.4
  22.3 0.0 copy-done.3
  22.3 0.6 %copy-done.4 = f32[4,40,128]{2,1,0:T(8,128)} copy-done((f32[4,40,128]{2,1,0:T(8,128)}, f32[4,40,128]{2,1,0:T(8,128)S(1)}, u32[]{:S(2)}) %copy-start.4) | copy-done | bytes 81944
  23.0 0.0 copy-start
  23.0 3.6 %plane.1 = f32[8,32,128]{2,1,0:T(8,128)} custom-call(f32[2,3,16,32,128]{4,3,2,1,0:T(8,128)} %refs_0_.1, f32[2,3,16,32,128]{4,3,2,1,0:T(8,128)} %refs_1_.1, f32[16,32,128]{2,1,0:T(8,128)} %get-tuple-element.17.coef_hbm.refs_2_, f32[13,40,128]{2,1,0:T(8,128)} %get-tuple-element.21.own_hbm.refs_3_, f32[52,8,128]{2,1,0:T(8,128)} %copy-done.1, ...), custom_call_target="tpu_custom_call" | custom-call | bytes 9000000 | tf_op jit(solution)/shard_map/plane/pallas_call | solution.py:884
  26.6 12.0 %all_to_all.10.got_ref = f32[8,32,128]{2,1,0:T(8,128)S(1)} all-to-all(f32[8,32,128]{2,1,0:T(8,128)} %plane.1), channel_id=1, replica_groups=mesh['gx'=32,'gy'=8] {'gy'}, dimensions={0} | all-to-all | bytes 262144 | tf_op jit(solution)/shard_map/all_to_all | solution.py:914
  38.6 0.0 copy-done
  38.6 1.0 %x_section.1.refs_9_ = f32[32,8,128]{2,1,0:T(8,128)} custom-call(f32[8,32,128]{2,1,0:T(8,128)S(1)} %all_to_all.10.got_ref, f32[256,64]{1,0:T(8,128)S(1)} %copy-done), custom_call_target="tpu_custom_call" | custom-call | bytes 3000000 | tf_op jit(solution)/shard_map/x_section/pallas_call | solution.py:915
  39.6 12.8 %all-to-all-start.1 = ((f32[32,8,128]{2,1,0:T(8,128)}), f32[32,8,128]{2,1,0:T(8,128)S(1)}, u32[]{:S(2)}, u32[]{:S(2)}) async-start(f32[32,8,128]{2,1,0:T(8,128)} %x_section.1.refs_9_), calls=%async_computation.1 | async-start | bytes 262144 | tf_op jit(solution)/shard_map/all_to_all | solution.py:924
  52.5 7.3 %fields.1 = (f32[2,3,16,32,128]{4,3,2,1,0:T(8,128)}, f32[2,3,16,32,128]{4,3,2,1,0:T(8,128)}) custom-call(f32[2,3,16,32,128]{4,3,2,1,0:T(8,128)} %refs_0_.1, f32[2,3,16,32,128]{4,3,2,1,0:T(8,128)} %refs_1_.1, f32[16,32,128]{2,1,0:T(8,128)} %get-tuple-element.17.coef_hbm.refs_2_, f32[13,40,128]{2,1,0:T(8,128)} %get-tuple-element.21.own_hbm.refs_3_, ...), custom_call_target="tpu_custom_call" | custom-call | bytes 18000000 | tf_op jit(solution)/shard_map/fields/pallas_call | solution.py:902
  59.8 1.8 %all-to-all-done.1.got_ref = f32[32,8,128]{2,1,0:T(8,128)S(1)} async-done(((f32[32,8,128]{2,1,0:T(8,128)}), f32[32,8,128]{2,1,0:T(8,128)S(1)}, u32[]{:S(2)}, u32[]{:S(2)}) %all-to-all-start.1) | async-done | bytes 131104 | tf_op jit(solution)/shard_map/all_to_all | solution.py:924
  61.5 0.7 %order_sum.1 = f32[2,2,8,32]{3,2,1,0:T(8,128)} custom-call(f32[32,8,128]{2,1,0:T(8,128)S(1)} %all-to-all-done.1.got_ref), custom_call_target="tpu_custom_call" | custom-call | bytes 3000000 | tf_op jit(solution)/shard_map/order_sum/pallas_call | solution.py:926
Async XLA Ops:
  3.1 7.1 %collective-permute-start = (f32[52,8,128]{2,1,0:T(8,128)}, f32[52,8,128]{2,1,0:T(8,128)S(1)}, u32[]{:S(2)}, u32[]{:S(2)}) collective-permute-start(f32[52,8,128]{2,1,0:T(8,128)} %get-tuple-element.19), channel_id=1, source_target_pairs={{0,8},{8,0},{16,24},{24,16},{32,40},{40,32},{48,56},{56,48},{64,72... | collective-permute-start | bytes 638984 | tf_op jit(solution)/shard_map/ppermute | solution.py:29
  6.4 5.5 %collective-permute-start.1 = (f32[52,8,128]{2,1,0:T(8,128)}, f32[52,8,128]{2,1,0:T(8,128)S(1)}, u32[]{:S(2)}, u32[]{:S(2)}) collective-permute-start(f32[52,8,128]{2,1,0:T(8,128)} %get-tuple-element.20), channel_id=1, source_target_pairs={{0,248},{8,16},{16,8},{24,32},{32,24},{40,48},{48,40},{56,64},{64,... | collective-permute-start | bytes 638984 | tf_op jit(solution)/shard_map/ppermute | solution.py:29
  10.2 1.7 %copy-start.1 = (f32[52,8,128]{2,1,0:T(8,128)}, f32[52,8,128]{2,1,0:T(8,128)S(1)}, u32[]{:S(2)}) copy-start(f32[52,8,128]{2,1,0:T(8,128)S(1)} %collective-permute-done.rows_a_hbm.refs_4_) | copy-start | bytes 638980
  11.9 0.7 %copy-start.2 = (f32[52,8,128]{2,1,0:T(8,128)}, f32[52,8,128]{2,1,0:T(8,128)S(1)}, u32[]{:S(2)}) copy-start(f32[52,8,128]{2,1,0:T(8,128)S(1)} %collective-permute-done.1.rows_b_hbm.refs_5_) | copy-start | bytes 638980
  15.0 6.3 %collective-permute-start.2 = (f32[4,40,128]{2,1,0:T(8,128)}, f32[4,40,128]{2,1,0:T(8,128)S(1)}, u32[]{:S(2)}, u32[]{:S(2)}) collective-permute-start(f32[4,40,128]{2,1,0:T(8,128)} %get-tuple-element.22), channel_id=1, source_target_pairs={{0,1},{1,0},{2,3},{3,2},{4,5},{5,4},{6,7},{7,6},{8,9},{9,8},{10,11... | collective-permute-start | bytes 245768 | tf_op jit(solution)/shard_map/ppermute | solution.py:29
  15.1 7.2 %collective-permute-start.3 = (f32[4,40,128]{2,1,0:T(8,128)}, f32[4,40,128]{2,1,0:T(8,128)S(1)}, u32[]{:S(2)}, u32[]{:S(2)}) collective-permute-start(f32[4,40,128]{2,1,0:T(8,128)} %get-tuple-element.23), channel_id=1, source_target_pairs={{0,7},{1,2},{2,1},{3,4},{4,3},{5,6},{6,5},{7,0},{8,15},{9,10},{10,... | collective-permute-start | bytes 245768 | tf_op jit(solution)/shard_map/ppermute | solution.py:29
  21.3 1.0 %copy-start.3 = (f32[4,40,128]{2,1,0:T(8,128)}, f32[4,40,128]{2,1,0:T(8,128)S(1)}, u32[]{:S(2)}) copy-start(f32[4,40,128]{2,1,0:T(8,128)S(1)} %collective-permute-done.2.cols_a_hbm.refs_6_) | copy-start | bytes 245764
  22.3 0.6 %copy-start.4 = (f32[4,40,128]{2,1,0:T(8,128)}, f32[4,40,128]{2,1,0:T(8,128)S(1)}, u32[]{:S(2)}) copy-start(f32[4,40,128]{2,1,0:T(8,128)S(1)} %collective-permute-done.3.cols_b_hbm.refs_7_) | copy-start | bytes 245764
  23.0 15.7 %copy-start = (f32[256,64]{1,0:T(8,128)S(1)}, f32[256,64]{1,0:T(8,128)}, u32[]{:S(2)}) copy-start(f32[256,64]{1,0:T(8,128)} %get-tuple-element.26.wave_ref) | copy-start | bytes 196612
  39.6 21.9 %all-to-all-start.1 = ((f32[32,8,128]{2,1,0:T(8,128)}), f32[32,8,128]{2,1,0:T(8,128)S(1)}, u32[]{:S(2)}, u32[]{:S(2)}) async-start(f32[32,8,128]{2,1,0:T(8,128)} %x_section.1.refs_9_), calls=%async_computation.1 | async-start | bytes 262144 | tf_op jit(solution)/shard_map/all_to_all | solution.py:924

commit v4 on v3

--- a/solution.py
+++ b/solution.py
@@ -163,6 +163,28 @@
             second_swap_ref[4 * n + quad] = jnp.where(even, blocks[0], blocks[1])
 
 
+def messages(own_ref, rows, first_swap_ref, second_swap_ref):
+    even = is_even("gy")
+    place = lanes_of((rows.stop - rows.start, COLS)) % 8
+    for c in range(4):
+        if c == 3:
+            right = left = own_ref[12, rows, :]
+        else:
+            e_re, e_im, h_re, h_im = (own_ref[3 * k + c, rows, :] for k in range(4))
+            right = jnp.where(
+                place < 4,
+                jnp.where(place < 2, roll(h_re, -4, 1), roll(h_im, -2, 1)),
+                jnp.where(place < 6, e_re, roll(e_im, 2, 1)),
+            )
+            left = jnp.where(
+                place < 4,
+                jnp.where(place < 2, roll(h_im, -6, 1), roll(h_re, -4, 1)),
+                jnp.where(place < 6, roll(e_im, -2, 1), e_re),
+            )
+        first_swap_ref[c, rows, :] = jnp.where(even, right, left)
+        second_swap_ref[c, rows, :] = jnp.where(even, left, right)
+
+
 def own_kernel(
     e_hbm,
     h_hbm,
@@ -170,6 +192,8 @@
     pattern_hbm,
     table_hbm,
     own_ref,
+    first_swap_ref,
+    second_swap_ref,
     coef_ref,
     e_ref,
     h_ref,
@@ -194,6 +218,7 @@
             values = coef_ref[z] if n == 12 else plane_of(e_ref, h_ref, n, z)
             packed = jnp.where(group == z, roll(values, 8 * z + 6, 1), packed)
         own_ref[n] = packed
+    messages(own_ref, slice(0, ROWS), first_swap_ref, second_swap_ref)
 
 
 def bloch_factors(theta_x, theta_y):
@@ -217,69 +242,62 @@
 
 def pack_kernel(
     own_hbm,
+    main_a_hbm,
+    main_b_hbm,
+    rows_b_hbm,
     rows_a_hbm,
-    rows_b_hbm,
     phase_hbm,
     all_ref,
     first_swap_ref,
     second_swap_ref,
     rot_ref,
-    own_ref,
     next_ref,
     prev_ref,
     phase_ref,
     sem,
 ):
     small = fetch([(phase_hbm, phase_ref)], sem)
-    copies = fetch([(own_hbm, own_ref)], sem, 1)
-    copies += fetch_swapped(
-        (rows_a_hbm, rows_b_hbm), next_ref, prev_ref, is_even("gx"), sem, 2
-    )
-    even = is_even("gy")
+    copies = fetch_swapped((rows_a_hbm, rows_b_hbm), next_ref, prev_ref, is_even("gx"), sem, 1)
+    mains = fetch(
+        [
+            (own_hbm, all_ref.at[:, 0:ROWS]),
+            (main_a_hbm, first_swap_ref.at[:, 0:ROWS]),
+            (main_b_hbm, second_swap_ref.at[:, 0:ROWS]),
+        ],
+        sem,
+        3,
+    )
     arrived(small)
     rot_ref[...] = bloch_factors(phase_ref[0], phase_ref[1])
     arrived(copies)
     rot = [rot_ref[k : k + 1, :] for k in range(8)]
     group = lanes_of((2, COLS)) // 8
-    place = lanes_of((EXT, COLS)) % 8
-    for n in range(13):
-        all_ref[n, 0:ROWS, :] = own_ref[n]
-        all_ref[n, ROWS:EXT, :] = jnp.zeros((EXT - ROWS, COLS), jnp.float32)
-    for ref, row, cos, sin in ((next_ref, 32, rot[0], rot[1]), (prev_ref, 38, rot[2], rot[3])):
-        for n in (0, 1, 2, 6, 7, 8, 12):
-            parts = 1 if n == 12 else 2
-            packed = [jnp.zeros((2, COLS), jnp.float32) for _ in range(parts)]
-            for quad in range(NZ // 4):
-                values = [ref[4 * (n + 3 * part) + quad] for part in range(parts)]
-                if parts == 2:
-                    values = turned(values[0], values[1], cos, sin)
-                for k in range(4):
-                    z = 4 * quad + k
-                    for part in range(parts):
-                        packed[part] = jnp.where(
-                            group == z,
-                            roll(values[part][2 * k : 2 * k + 2], 8 * z + 6, 1),
-                            packed[part],
-                        )
-            for part in range(parts):
-                all_ref[n + 3 * part, row : row + 2, :] = packed[part]
-    for c in range(4):
-        if c == 3:
-            right = left = all_ref[12]
-        else:
-            e_re, e_im, h_re, h_im = (all_ref[3 * k + c] for k in range(4))
-            right = jnp.where(
-                place < 4,
-                jnp.where(place < 2, roll(h_re, -4, 1), roll(h_im, -2, 1)),
-                jnp.where(place < 6, e_re, roll(e_im, 2, 1)),
+    row = lax.broadcasted_iota(jnp.int32, (8, COLS), 0)
+    lane = lanes_of((8, COLS))
+    group = (lane + COLS + 2 - 4 * (row % 2)) % COLS // 8
+
+    def packed(blocks):
+        total = jnp.zeros((8, COLS), jnp.float32)
+        for quad, values in enumerate(blocks):
+            moved = pltpu.roll(values, 32 * quad, 1, stride=4, stride_axis=0)
+            total = jnp.where(group == 4 * quad + row // 2, moved, total)
+        total = jnp.where(row % 2 == 1, roll(total, 2, 1), roll(total, 6, 1))
+        total = total + roll(total, 2, 0)
+        return total + roll(total, 4, 0)
+
+    quads = range(NZ // 4)
+    for n in (0, 1, 2, 6, 7, 8, 12):
+        parts = 1 if n == 12 else 2
+        sides = []
+        for ref, cos, sin in ((next_ref, rot[0], rot[1]), (prev_ref, rot[2], rot[3])):
+            found = [packed([ref[4 * (n + 3 * part) + quad] for quad in quads]) for part in range(parts)]
+            sides.append(turned(found[0], found[1], cos, sin) if parts == 2 else found)
+        for part in range(parts):
+            all_ref[n + 3 * part, ROWS:EXT, :] = jnp.where(
+                row < 2, sides[0][part], jnp.where(row < 6, 0.0, sides[1][part])
             )
-            left = jnp.where(
-                place < 4,
-                jnp.where(place < 2, roll(h_im, -6, 1), roll(h_re, -4, 1)),
-                jnp.where(place < 6, roll(e_im, -2, 1), e_re),
-            )
-        first_swap_ref[c] = jnp.where(even, right, left)
-        second_swap_ref[c] = jnp.where(even, left, right)
+    messages(all_ref, slice(ROWS, EXT), first_swap_ref, second_swap_ref)
+    arrived(mains)
 
 
 def turned(re, im, cos, sin):
@@ -360,11 +378,40 @@
     )
 
 
-def fetch_edges(own_hbm, rows_hbm, cols_hbm, rot_hbm, edges, sem, first):
-    own_ref, next_ref, prev_ref, right_ref, left_ref, rot_ref = edges
+def feet_kernel(
+    rows_b_hbm, rows_a_hbm, rot_hbm, e_ref, h_ref, coef_ref, next_ref, prev_ref, rot_ref, sem
+):
+    copies = fetch([(rot_hbm, rot_ref)], sem)
+    copies += fetch_swapped((rows_a_hbm, rows_b_hbm), next_ref, prev_ref, is_even("gx"), sem, 1)
+    arrived(copies)
+    rot = [rot_ref[k : k + 1, :] for k in range(8)]
+    row = lax.broadcasted_iota(jnp.int32, (8, COLS), 0)
+
+    def foot(ahead, behind, k):
+        return jnp.where(
+            row < 2,
+            roll(ahead, -2 * k, 0),
+            jnp.where(row < 6, 0.0, roll(behind, 6 - 2 * k, 0)),
+        )
+
+    for quad in range(NZ // 4):
+        for field, target in ((0, e_ref), (1, h_ref)):
+            for c in range(3):
+                n = (6 * field + c) * 4 + quad
+                m = n + 12
+                ahead = turned(next_ref[n], next_ref[m], rot[0], rot[1])
+                behind = turned(prev_ref[n], prev_ref[m], rot[2], rot[3])
+                for part in range(2):
+                    for k in range(4):
+                        target[part, c, 4 * quad + k] = foot(ahead[part], behind[part], k)
+        for k in range(4):
+            coef_ref[4 * quad + k] = foot(next_ref[48 + quad], prev_ref[48 + quad], k)
+
+
+def fetch_edges(own_hbm, cols_hbm, rot_hbm, edges, sem, first):
+    own_ref, right_ref, left_ref, rot_ref = edges
     copies = fetch([(own_hbm, own_ref), (rot_hbm, rot_ref)], sem, first)
-    copies += fetch_swapped(rows_hbm, next_ref, prev_ref, is_even("gx"), sem, first + 2)
-    copies += fetch_swapped(cols_hbm, left_ref, right_ref, is_even("gy"), sem, first + 4)
+    copies += fetch_swapped(cols_hbm, left_ref, right_ref, is_even("gy"), sem, first + 2)
     return copies
 
 
@@ -373,8 +420,6 @@
         VMEM(shape, jnp.float32)
         for shape in (
             (13, EXT, COLS),
-            (MAIN_BLOCKS, 8, COLS),
-            (MAIN_BLOCKS, 8, COLS),
             (4, EXT, COLS),
             (4, EXT, COLS),
             (8, COLS),
@@ -392,29 +437,13 @@
 
 
 def fill_edges(edges, block, parts):
-    own_ref, next_ref, prev_ref, right_ref, left_ref, rot_ref = edges
+    own_ref, right_ref, left_ref, rot_ref = edges
     e_all, h_all, coef_all, edge_ref = block
     rot = [rot_ref[k : k + 1, :] for k in range(8)]
     for at in range(len(parts)):
         for c in range(3):
             e_all[at, c, NZ] = jnp.zeros((EXT, COLS), jnp.float32)
             h_all[at, c, 0] = jnp.zeros((EXT, COLS), jnp.float32)
-    for ref, row, cos, sin in ((next_ref, 32, rot[0], rot[1]), (prev_ref, 38, rot[2], rot[3])):
-        for field in range(2):
-            dest = h_all if field else e_all
-            for c in range(3):
-                for quad in range(4):
-                    re = ref[(6 * field + c) * 4 + quad]
-                    im = ref[(6 * field + 3 + c) * 4 + quad]
-                    both = turned(re, im, cos, sin)
-                    for at, part in enumerate(parts):
-                        for k in range(4):
-                            z = 4 * quad + k + field
-                            dest[at, c, z, row : row + 2, :] = both[part][2 * k : 2 * k + 2]
-        for quad in range(4):
-            values = ref[48 + quad]
-            for k in range(4):
-                coef_all[4 * quad + k, row : row + 2, :] = values[2 * k : 2 * k + 2]
     strip = strip_of(
         [own_ref[a] for a in range(13)],
         [right_ref[a] for a in range(4)],
@@ -434,17 +463,17 @@
                 e = strip_e(e, h, strip[12])
 
 
+def beside(edge, values, z, ahead):
+    shift = COLS + (125 if ahead else 123) - 8 * z
+    shift = shift % COLS if isinstance(z, int) else lax.rem(shift, COLS)
+    lane = lanes_of(values.shape)
+    if ahead:
+        return jnp.where(lane == COLS - 1, roll(edge, shift, 1), roll(values, -1, 1))
+    return jnp.where(lane == 0, roll(edge, shift, 1), roll(values, 1, 1))
+
+
 def updates(block, parts):
     e_all, h_all, coef_all, edge_ref = block
-    lane = lanes_of((EXT, COLS))
-
-    def next_col(values, edge, z):
-        edge = roll(edge, lax.rem(COLS + 125 - 8 * z, COLS), 1)
-        return jnp.where(lane == COLS - 1, edge, roll(values, -1, 1))
-
-    def prev_col(values, edge, z):
-        edge = roll(edge, lax.rem(COLS + 123 - 8 * z, COLS), 1)
-        return jnp.where(lane == 0, edge, roll(values, 1, 1))
 
     def do_h(step, layers):
         new = []
@@ -454,8 +483,8 @@
                 h = tuple(h_all[at, c, z + 1] for c in range(3))
                 e_up = (e_all[at, 0, z + 1], e_all[at, 1, z + 1])
                 e_yn = (
-                    next_col(e[0], edge_ref[at, 2 * step, 0], z),
-                    next_col(e[2], edge_ref[at, 2 * step, 1], z),
+                    beside(edge_ref[at, 2 * step, 0], e[0], z, True),
+                    beside(edge_ref[at, 2 * step, 1], e[2], z, True),
                 )
                 values = h_new(h, e, e_up, (next_row(e[1]), next_row(e[2])), e_yn)
                 new.append((at, z, values))
@@ -471,8 +500,8 @@
                 h = tuple(h_all[at, c, z + 1] for c in range(3))
                 h_down = (h_all[at, 0, z], h_all[at, 1, z])
                 h_yp = (
-                    prev_col(h[0], edge_ref[at, 2 * step + 1, 0], z),
-                    prev_col(h[2], edge_ref[at, 2 * step + 1, 1], z),
+                    beside(edge_ref[at, 2 * step + 1, 0], h[0], z, False),
+                    beside(edge_ref[at, 2 * step + 1, 1], h[2], z, False),
                 )
                 values = e_new(
                     e, h, h_down, (prev_row(h[1]), prev_row(h[2])), h_yp, coef_all[z]
@@ -489,42 +518,37 @@
     e_hbm,
     h_hbm,
     coef_hbm,
+    e_foot_hbm,
+    h_foot_hbm,
+    coef_foot_hbm,
     own_hbm,
-    rows_a_hbm,
-    rows_b_hbm,
+    cols_b_hbm,
     cols_a_hbm,
-    cols_b_hbm,
     rot_hbm,
     wave_hbm,
-    monitor_hbm,
+    monitor_ref,
     spread_ref,
     *scratch,
 ):
-    edges, block = scratch[0:6], scratch[6:10]
-    wave_ref, monitor_ref, sem = scratch[10:13]
+    edges, block = scratch[0:4], scratch[4:8]
+    wave_ref, sem = scratch[8:10]
     e_all, h_all, coef_all, edge_ref = block
-    scalar = fetch([(monitor_hbm, monitor_ref)], sem)
-    copies = fetch_edges(
-        own_hbm,
-        (rows_a_hbm, rows_b_hbm),
-        (cols_a_hbm, cols_b_hbm),
-        rot_hbm,
-            edges,
-        sem,
-        1,
-    )
-    arrived(scalar)
+    copies = fetch_edges(own_hbm, (cols_a_hbm, cols_b_hbm), rot_hbm, edges, sem, 0)
     level = monitor_ref[0]
     low = jnp.clip(level - 2, 0, NZ - 5)
+    here, there = pl.ds(low, 5), pl.ds(low + 1, 5)
     large = fetch(
         [
-            (e_hbm.at[:, :, pl.ds(low, 5)], e_all.at[:, :, pl.ds(low, 5), 0:ROWS, :]),
-            (h_hbm.at[:, :, pl.ds(low, 5)], h_all.at[:, :, pl.ds(low + 1, 5), 0:ROWS, :]),
-            (coef_hbm.at[pl.ds(low, 5)], coef_all.at[pl.ds(low, 5), 0:ROWS, :]),
+            (e_hbm.at[:, :, here], e_all.at[:, :, here, 0:ROWS, :]),
+            (h_hbm.at[:, :, here], h_all.at[:, :, there, 0:ROWS, :]),
+            (coef_hbm.at[here], coef_all.at[here, 0:ROWS, :]),
+            (e_foot_hbm.at[:, :, here], e_all.at[:, :, here, ROWS:EXT, :]),
+            (h_foot_hbm.at[:, :, here], h_all.at[:, :, there, ROWS:EXT, :]),
+            (coef_foot_hbm.at[here], coef_all.at[here, ROWS:EXT, :]),
             (wave_hbm, wave_ref),
         ],
         sem,
-        7,
+        4,
     )
     arrived(copies)
     fill_edges(edges, block, (0, 1))
@@ -540,27 +564,17 @@
                 if k < 2 and (c < 2 or k > -2):
                     h = h_all[part, c, z + 1]
                     near["h", part, c, k] = jnp.where(level + k >= 0, h, 0.0) if k < 0 else h
-    lane = lanes_of((EXT, COLS))
-
-    def next_col(values, edge, z):
-        edge = roll(edge, lax.rem(COLS + 125 - 8 * z, COLS), 1)
-        return jnp.where(lane == COLS - 1, edge, roll(values, -1, 1))
-
-    def prev_col(values, edge, z):
-        edge = roll(edge, lax.rem(COLS + 123 - 8 * z, COLS), 1)
-        return jnp.where(lane == 0, edge, roll(values, 1, 1))
-
     def update_h(step, part, k, wanted):
         z = jnp.clip(level + k, 0, NZ - 1)
         ex, ey, ez = (near["e", part, c, k] for c in range(3))
         edge = edge_ref.at[part, 2 * step]
         new = {}
         if 0 in wanted:
-            new[0] = next_col(ez, edge[1], z) - ez - (near["e", part, 1, k + 1] - ey)
+            new[0] = beside(edge[1], ez, z, True) - ez - (near["e", part, 1, k + 1] - ey)
         if 1 in wanted:
             new[1] = near["e", part, 0, k + 1] - ex - (next_row(ez) - ez)
         if 2 in wanted:
-            new[2] = next_row(ey) - ey - (next_col(ex, edge[0], z) - ex)
+            new[2] = next_row(ey) - ey - (beside(edge[0], ex, z, True) - ex)
         for c, curl in new.items():
             values = near["h", part, c, k] - STEP_DT * curl
             near["h", part, c, k] = jnp.where(level + k >= 0, values, 0.0) if k < 0 else values
@@ -572,11 +586,11 @@
         coef = coef_all[z]
         new = {}
         if 0 in wanted:
-            new[0] = hz - prev_col(hz, edge[1], z) - (hy - near["h", part, 1, k - 1])
+            new[0] = hz - beside(edge[1], hz, z, False) - (hy - near["h", part, 1, k - 1])
         if 1 in wanted:
             new[1] = hx - near["h", part, 0, k - 1] - (hz - prev_row(hz))
         if 2 in wanted:
-            new[2] = hy - prev_row(hy) - (hx - prev_col(hx, edge[0], z))
+            new[2] = hy - prev_row(hy) - (hx - beside(edge[0], hx, z, False))
         for c, curl in new.items():
             values = near["e", part, c, k] + coef * curl
             near["e", part, c, k] = jnp.where(level + k < NZ, values, 0.0) if k > 0 else values
@@ -601,92 +615,72 @@
         e_hbm,
         h_hbm,
         coef_hbm,
+        e_foot_hbm,
+        h_foot_hbm,
+        coef_foot_hbm,
         own_hbm,
-        rows_a_hbm,
-        rows_b_hbm,
+        cols_b_hbm,
         cols_a_hbm,
-        cols_b_hbm,
         rot_hbm,
-        ) = refs[0:9]
-    e_out, h_out = refs[inputs : inputs + 2]
-    scratch = refs[inputs + 2 :]
-    edges, block, sem = scratch[0:6], scratch[6:10], scratch[10]
+    ) = refs[0:10]
+    e_out, h_out, token_ref = refs[inputs : inputs + 3]
+    token_ref[...] = jnp.zeros_like(token_ref)
+    scratch = refs[inputs + 3 :]
+    edges, block, sem = scratch[0:4], scratch[4:8], scratch[8]
     e_all, h_all, coef_all, _ = block
-    copies = fetch_edges(
-        own_hbm,
-        (rows_a_hbm, rows_b_hbm),
-        (cols_a_hbm, cols_b_hbm),
-        rot_hbm,
-            edges,
-        sem,
-        0,
-    )
-    large = fetch(
-        [
-            (coef_hbm, coef_all.at[:, 0:ROWS, :]),
-            (e_hbm.at[parts[0] : parts[-1] + 1], e_all.at[:, :, 0:NZ, 0:ROWS, :]),
-            (h_hbm.at[parts[0] : parts[-1] + 1], h_all.at[:, :, 1 : NZ + 1, 0:ROWS, :]),
-        ],
-        sem,
-        6,
-    )
+    copies = fetch_edges(own_hbm, (cols_a_hbm, cols_b_hbm), rot_hbm, edges, sem, 0)
+    some = slice(parts[0], parts[-1] + 1)
+    quads = range(NZ // 4)
+    loads = []
+    for quad in quads:
+        here, there = pl.ds(4 * quad, 4), pl.ds(4 * quad + 1, 4)
+        loads.append(
+            fetch(
+                [
+                    (e_hbm.at[some, :, here], e_all.at[:, :, here, 0:ROWS, :]),
+                    (e_foot_hbm.at[some, :, here], e_all.at[:, :, here, ROWS:EXT, :]),
+                    (h_hbm.at[some, :, here], h_all.at[:, :, there, 0:ROWS, :]),
+                    (h_foot_hbm.at[some, :, here], h_all.at[:, :, there, ROWS:EXT, :]),
+                    (coef_hbm.at[here], coef_all.at[here, 0:ROWS, :]),
+                    (coef_foot_hbm.at[here], coef_all.at[here, ROWS:EXT, :]),
+                ],
+                sem,
+                6 + 6 * quad,
+            )
+        )
     arrived(copies)
     fill_edges(edges, block, parts)
-    arrived(large)
     do_h, do_e = updates(block, len(parts))
 
-    def sweep(update, step, store=None):
-        def layers(quad, carry):
-            start = 4 * quad
-            update(step, [start + k for k in range(4)])
-            if store is not None:
-                store(start)
-            return carry
-
-        lax.fori_loop(0, NZ // 4, layers, 0)
-
-    def store_h(start):
-        fetch(
-            [
-                (
-                    h_all.at[at, :, pl.ds(start + 1, 4), 0:ROWS, :],
-                    h_out.at[part, :, pl.ds(start, 4)],
-                )
-                for at, part in enumerate(parts)
-            ],
-            sem,
-            10,
-        )
-
-    def store_e(start):
-        fetch(
-            [
-                (
-                    e_all.at[at, :, pl.ds(start, 4), 0:ROWS, :],
-                    e_out.at[part, :, pl.ds(start, 4)],
-                )
-                for at, part in enumerate(parts)
-            ],
-            sem,
-            12,
-        )
-
-    sweep(do_h, 0)
-    sweep(do_e, 0)
-    sweep(do_h, 1, store_h)
-    sweep(do_e, 1, store_e)
-    for at, part in enumerate(parts):
-        pltpu.make_async_copy(
-            h_all.at[at, :, 1 : NZ + 1, 0:ROWS, :], h_out.at[part], sem.at[10 + at]
-        ).wait()
-        pltpu.make_async_copy(
-            e_all.at[at, :, 0:NZ, 0:ROWS, :], e_out.at[part], sem.at[12 + at]
-        ).wait()
+    def finish(quad):
+        layers = [4 * quad + k for k in range(4)]
+        here, there = pl.ds(4 * quad, 4), pl.ds(4 * quad + 1, 4)
+        do_h(1, layers)
+        fetch([(h_all.at[:, :, there, 0:ROWS, :], h_out.at[some, :, here])], sem, 4)
+        do_e(1, layers)
+        fetch([(e_all.at[:, :, here, 0:ROWS, :], e_out.at[some, :, here])], sem, 5)
+
+    arrived(loads[0])
+    for quad in quads:
+        if quad + 1 < len(quads):
+            arrived(loads[quad + 1])
+        layers = [4 * quad + k for k in range(4)]
+        do_h(0, layers)
+        do_e(0, layers)
+        if quad > 0:
+            finish(quad - 1)
+    finish(quads[-1])
+    stored = (
+        (h_all.at[:, :, 1 : NZ + 1, 0:ROWS, :], h_out.at[some]),
+        (e_all.at[:, :, 0:NZ, 0:ROWS, :], e_out.at[some]),
+    )
+    for k, (source, target) in enumerate(stored):
+        pltpu.make_async_copy(source, target, sem.at[4 + k]).wait()
 
 
 def y_section(re, im, wave_ref, spread_ref):
     wave = wave_ref[...]
-    owners, _, lanes = spread_ref.shape
+    _, owners, _, lanes = spread_ref.shape
     each = lanes // 4
     out = [
         jnp.dot(
@@ -703,13 +697,20 @@
             for part in range(2)
             for c in range(2)
         ]
-        spread_ref[owner] = jnp.concatenate(pieces, axis=1)
-
-
-def x_kernel(got_ref, wave_ref, part_ref):
-    total = got_ref[0]
-    for source in range(1, got_ref.shape[0]):
-        total = total + got_ref[source]
+        joined = jnp.concatenate(pieces, axis=1)
+        for half in range(2):
+            spread_ref[half, owner] = joined
+
+
+def x_kernel(got_ref, wave_ref, after_hbm, part_ref):
+    each = got_ref.shape[0] // 2
+    totals = []
+    for half in range(2):
+        total = got_ref[half * each]
+        for source in range(1, each):
+            total = total + got_ref[half * each + source]
+        totals.append(total)
+    total = jnp.concatenate(totals, axis=0)
     half = total.shape[1] // 2
     other = roll(total, half, 1)
     other = jnp.where(lanes_of(other.shape) < half, other, -other)
@@ -720,6 +721,21 @@
         preferred_element_type=jnp.float32,
     )
     part_ref[...] = result.reshape(part_ref.shape)
+
+
+def groups(mesh_shape):
+    count_x, count_y = mesh_shape
+    rest = count_x // 2
+    near = [
+        [(half * rest + r) * count_y + y for half in range(2) for y in range(count_y)]
+        for r in range(rest)
+    ]
+    far = [
+        [(half * rest + r) * count_y + y for r in range(rest)]
+        for half in range(2)
+        for y in range(count_y)
+    ]
+    return near, far
 
 
 def sum_kernel(got_ref, out_ref):
@@ -765,18 +781,21 @@
         cos, sin = joined(part, fine)
         y_ref[8 * block : 8 * block + 8, :] = cos
         y_ref[COLS + 8 * block : COLS + 8 * block + 8, :] = sin
-    blocks = ORD_X // 8
-    shape = (blocks, 2 * ROWS)
-    place = index_x * ROWS + lax.broadcasted_iota(jnp.int32, shape, 1) % ROWS
-    order = 8 * lax.broadcasted_iota(jnp.int32, shape, 0) - ORD_X // 2
+    blocks = ORD_X // 16
+    shape = (blocks, 4 * ROWS)
+    rest = count_x // 2
+    lane = lax.broadcasted_iota(jnp.int32, shape, 1)
+    block_x = lax.rem(index_x, rest) + rest * (lane // ROWS % 2)
+    place = block_x * ROWS + lane % ROWS
+    own_half = index_x // rest * (ORD_X // 2)
+    order = 8 * lax.broadcasted_iota(jnp.int32, shape, 0) + own_half - ORD_X // 2
     coarse = waves(order * place, place, total_x, theta_x)
-    order = lax.broadcasted_iota(jnp.int32, (8, 2 * ROWS), 0)
+    order = lax.broadcasted_iota(jnp.int32, (8, 4 * ROWS), 0)
     fine = waves(order * place[0:8], place[0:8], total_x, 0.0)
-    lane = lax.broadcasted_iota(jnp.int32, (8, 2 * ROWS), 1)
     for block in range(blocks):
         part = tuple(values[block : block + 1] for values in coarse)
         cos, sin = joined(part, fine)
-        x_ref[8 * block : 8 * block + 8, :] = jnp.where(lane < ROWS, cos, sin)
+        x_ref[8 * block : 8 * block + 8, :] = jnp.where(lane[0:8] < 2 * ROWS, cos, sin)
 
 
 def params(mebibytes):
@@ -824,17 +843,22 @@
             SMEM(nodes.shape, jnp.float32),
             dma((11,)),
         ],
-        compiler_params=params(60),
+        compiler_params=params(64),
         cost_estimate=cost(3),
         name="rows",
     )(e_field, h_field, material, pattern, base_eps, mode_table, nodes)
+    rows_b = swapped(rows_b, "gx", False)
     rows_a = swapped(rows_a, "gx", True)
-    rows_b = swapped(rows_b, "gx", False)
-    own, coef = pl.pallas_call(
+    own, cols_a, cols_b, coef = pl.pallas_call(
         own_kernel,
-        out_shape=(f32(13, ROWS, COLS), f32(NZ, ROWS, COLS)),
+        out_shape=(
+            f32(13, ROWS, COLS),
+            f32(4, ROWS, COLS),
+            f32(4, ROWS, COLS),
+            f32(NZ, ROWS, COLS),
+        ),
         in_specs=[hbm] * 5,
-        out_specs=(vmem,) * 2,
+        out_specs=(vmem,) * 4,
         scratch_shapes=[
             f32_vmem(*e_field.shape),
             f32_vmem(*h_field.shape),
@@ -843,7 +867,7 @@
             f32_vmem(8, COLS),
             dma((5,)),
         ],
-        compiler_params=params(60),
+        compiler_params=params(64),
         cost_estimate=cost(4),
         name="own",
     )(e_field, h_field, material, pattern, table)
@@ -855,42 +879,59 @@
             f32(4, EXT, COLS),
             f32(8, COLS),
         ),
-        in_specs=[hbm] * 4,
+        in_specs=[hbm] * 6,
         out_specs=(vmem,) * 4,
         scratch_shapes=[
-            f32_vmem(*own.shape),
             f32_vmem(MAIN_BLOCKS, 8, COLS),
             f32_vmem(MAIN_BLOCKS, 8, COLS),
             SMEM((2,), jnp.float32),
-            dma((4,)),
+            dma((6,)),
         ],
-        compiler_params=params(60),
+        compiler_params=params(64),
         cost_estimate=cost(2),
         name="pack",
-    )(own, rows_a, rows_b, bloch_phase)
+    )(own, cols_a, cols_b, rows_b, rows_a, bloch_phase)
     y_wave, x_wave = pl.pallas_call(
         functools.partial(table_kernel, count_x, count_y),
-        out_shape=(f32(2 * COLS, ORD_Y), f32(ORD_X, 2 * ROWS)),
+        out_shape=(f32(2 * COLS, ORD_Y), f32(ORD_X // 2, 4 * ROWS)),
         in_specs=[hbm, hbm],
         out_specs=(vmem,) * 2,
         scratch_shapes=[SMEM((2,), jnp.float32), dma((1,))],
-        compiler_params=params(60),
+        compiler_params=params(64),
         cost_estimate=cost(2),
         name="tables",
     )(bloch_phase, rot)
     cols_b = swapped(cols_b, "gy", False)
     cols_a = swapped(cols_a, "gy", True)
-    around = (e_field, h_field, coef, own, rows_a, rows_b, cols_a, cols_b, rot)
+    feet = pl.pallas_call(
+        feet_kernel,
+        out_shape=(
+            f32(2, 3, NZ, EXT - ROWS, COLS),
+            f32(2, 3, NZ, EXT - ROWS, COLS),
+            f32(NZ, EXT - ROWS, COLS),
+        ),
+        in_specs=[hbm] * 3,
+        out_specs=(vmem,) * 3,
+        scratch_shapes=[
+            f32_vmem(MAIN_BLOCKS, 8, COLS),
+            f32_vmem(MAIN_BLOCKS, 8, COLS),
+            f32_vmem(8, COLS),
+            dma((3,)),
+        ],
+        compiler_params=params(64),
+        cost_estimate=cost(2),
+        name="feet",
+    )(rows_b, rows_a, rot)
+    around = (e_field, h_field, coef, *feet, own, cols_b, cols_a, rot)
     spread = pl.pallas_call(
         plane_kernel,
-        out_shape=f32(count_y, ROWS, 4 * each_q),
-        in_specs=[hbm] * 11,
+        out_shape=f32(2, count_y, ROWS, 4 * each_q),
+        in_specs=[hbm] * 11 + [pl.BlockSpec(memory_space=SMEM)],
         out_specs=vmem,
         scratch_shapes=[
             *edge_scratch(),
             *block_scratch(2),
             f32_vmem(*y_wave.shape),
-            SMEM((1,), jnp.int32),
             dma((11,)),
         ],
         compiler_params=params(60),
@@ -898,31 +939,30 @@
         name="plane",
     )(*around, y_wave, monitor_z)
 
-    def fields(parts, after, before=()):
-        return pl.pallas_call(
-            functools.partial(field_kernel, parts, 10 + len(before)),
-            out_shape=(f32(*e_field.shape), f32(*h_field.shape)),
-            in_specs=[hbm] * (10 + len(before)),
-            out_specs=(hbm, hbm),
-            scratch_shapes=[*edge_scratch(), *block_scratch(len(parts)), dma((14,))],
-            input_output_aliases={10 + k: k for k in range(len(before))},
-            compiler_params=params(60),
-            cost_estimate=cost(6),
-            name="fields",
-        )(*around, after, *before)
-
-    got = lax.all_to_all(spread, "gy", 0, 0, tiled=True)
+    near, far = groups((count_x, count_y))
+    both = ("gx", "gy")
+    spread = spread.reshape(2 * count_y, ROWS, 4 * each_q)
+    got = lax.all_to_all(spread, both, 0, 0, tiled=True, axis_index_groups=near)
+    e_out, h_out, token = pl.pallas_call(
+        functools.partial(field_kernel, (0, 1), 11),
+        out_shape=(f32(*e_field.shape), f32(*h_field.shape), f32(8, COLS)),
+        in_specs=[hbm] * 11,
+        out_specs=(hbm, hbm, vmem),
+        scratch_shapes=[*edge_scratch(), *block_scratch(2), dma((30,))],
+        compiler_params=params(60),
+        cost_estimate=cost(6),
+        name="fields",
+    )(*around, spread)
     partial = pl.pallas_call(
         x_kernel,
-        out_shape=f32(count_x, each_p, 4 * each_q),
-        in_specs=[vmem, vmem],
+        out_shape=f32(count_x // 2, each_p, 4 * each_q),
+        in_specs=[vmem, vmem, hbm],
         out_specs=vmem,
         compiler_params=params(8),
         cost_estimate=cost(1),
         name="x_section",
-    )(got, x_wave)
-    got = lax.all_to_all(partial, "gx", 0, 0, tiled=True)
-    e_out, h_out = fields((0, 1), partial)
+    )(got, x_wave, token)
+    got = lax.all_to_all(partial, both, 0, 0, tiled=True, axis_index_groups=far)
     orders = pl.pallas_call(
         sum_kernel,
         out_shape=f32(2, 2, each_p, each_q),

time: 62.6 us -> 59 us (0.942)
  waiting for transfers between devices: 4.48 us -> 0.73 us
  blocking collectives: 12 us -> 14.7 us
  starting transfers between devices: 20.1 us -> 17.9 us
  local copies, waits for them, and re-layouts: 1.32 us -> 0.69 us
    all_to_all x1, starting transfers between devices: 12.8 us -> 5.1 us  [shards(): got = lax.all_to_all(spread, both, 0, 0, tiled=True, axis_index_groups=near)]
    ppermute x4, starting transfers between devices: 7.33 us -> 12.8 us  [swapped(): return lax.ppermute(block, axis, route)]
    ppermute x4, waiting for transfers between devices: 2.73 us -> 0.01 us  [swapped(): return lax.ppermute(block, axis, route)]
    all_to_all x1, blocking collectives: 12 us -> 14.7 us  [shards(): got = lax.all_to_all(partial, both, 0, 0, tiled=True, axis_index_groups=far)]
    all_to_all x1, waiting for transfers between devices: 1.76 us -> 0.72 us  [shards(): got = lax.all_to_all(spread, both, 0, 0, tiled=True, axis_index_groups=near)]
    unnamed x10 -> x4, local copies, waits for them, and re-layouts: 1.32 us -> 0.69 us
    pallas_call x4 -> x5, Pallas kernels: 15.6 us -> 16.2 us  [the longest x1 6.81 us: shards(): pl.pallas_call(functools.partial(field_kernel, (0, 1), 11), out_shape=(f3...]
  transfers between devices with their start and end apart: 5 -> 5, of which waited for: 3 -> 1; matrix products, arithmetic and copies ran while one was open for 0% -> 0% of each run, Pallas kernels for 20% -> 24%
where the time goes in v4:
time: 59 us; the launch traced here: 58.6 us
  Pallas kernels  23.2 us (39%)
  starting transfers between devices  17.9 us (30%)
  blocking collectives  14.7 us (25%)
  between operations  1.4 us (2%)
  waiting for transfers between devices  0.73 us (1%)
  local copies, waits for them, and re-layouts  0.69 us (1%)
    all_to_all x1, blocking collectives, shards(): got = lax.all_to_all(partial, both, 0, 0, tiled=True, axis_index_groups=far)  14.7 us
    ppermute x4, starting transfers between devices, swapped(): return lax.ppermute(block, axis, route)  12.8 us
    pallas_call x1, Pallas kernels, shards(): pl.pallas_call(functools.partial(field_kernel, (0, 1), 11), out_shape=(f3...  6.81 us
    all_to_all x1, starting transfers between devices, shards(): got = lax.all_to_all(spread, both, 0, 0, tiled=True, axis_index_groups=near)  5.1 us
    pallas_call x1, Pallas kernels, shards(): pl.pallas_call(own_kernel, out_shape=(f32(13, ROWS, COLS), f32(4, ROWS, C...  3.79 us
    pallas_call x1, Pallas kernels, shards(): pl.pallas_call(plane_kernel, out_shape=f32(2, count_y, ROWS, 4 * each_q),...  3.32 us
    pallas_call x1, Pallas kernels, shards(): pl.pallas_call(rows_kernel, out_shape=(f32(8, COLS), f32(MAIN_BLOCKS, 8,...  2.45 us
    pallas_call x1, Pallas kernels, shards(): pl.pallas_call(pack_kernel, out_shape=(f32(13, EXT, COLS), f32(4, EXT, CO...  2.27 us
  transfers between devices with their start and end apart: 5, of which 1 were waited for; matrix products, arithmetic and copies ran while one was open for 0% of the time, Pallas kernels for 24%

profile of v4, /device:TPU:1, one launch (start us, length us, event | category | flops | bytes accessed | tf_op | source)
XLA Modules:
  0.0 58.6 jit_solution(5247745294247314112)
XLA Ops:
  0.6 2.5 %rows.1 = (f32[8,128]{1,0:T(8,128)}, f32[52,8,128]{2,1,0:T(8,128)}, f32[52,8,128]{2,1,0:T(8,128)}) custom-call(f32[2,3,16,32,128]{4,3,2,1,0:T(8,128)} %refs_0_.1, f32[2,3,16,32,128]{4,3,2,1,0:T(8,128)} %refs_1_.1, s32[16,32,128]{2,1,0:T(8,128)} %material_hbm.3, s32[16,32,128]{2,1,0:T(8,128)} %pattern_hbm.3, f32[8]{0:T(128)} %base_hbm.1, f32[4,16]{1,0:T(4,128)} %mode_hbm.1, ...), custom_call_target="tpu_custom_call" | custom-call | bytes 9000000 | tf_op jit(solution)/shard_map/rows/pallas_call | solution.py:827
  3.1 3.1 %collective-permute-start = (f32[52,8,128]{2,1,0:T(8,128)}, f32[52,8,128]{2,1,0:T(8,128)}, u32[]{:S(2)}, u32[]{:S(2)}) collective-permute-start(f32[52,8,128]{2,1,0:T(8,128)} %get-tuple-element.24), channel_id=1, source_target_pairs={{0,248},{8,16},{16,8},{24,32},{32,24},{40,48},{48,40},{56,64},{64,... | collective-permute-start | bytes 638984 | tf_op jit(solution)/shard_map/ppermute | solution.py:29
  6.2 4.7 %collective-permute-start.1 = (f32[52,8,128]{2,1,0:T(8,128)}, f32[52,8,128]{2,1,0:T(8,128)}, u32[]{:S(2)}, u32[]{:S(2)}) collective-permute-start(f32[52,8,128]{2,1,0:T(8,128)} %get-tuple-element.25), channel_id=1, source_target_pairs={{0,8},{8,0},{16,24},{24,16},{32,40},{40,32},{48,56},{56,48},{64,72... | collective-permute-start | bytes 638984 | tf_op jit(solution)/shard_map/ppermute | solution.py:29
  10.9 3.8 %own.1 = (f32[13,32,128]{2,1,0:T(8,128)}, f32[4,32,128]{2,1,0:T(8,128)}, f32[4,32,128]{2,1,0:T(8,128)}, f32[16,32,128]{2,1,0:T(8,128)}) custom-call(f32[2,3,16,32,128]{4,3,2,1,0:T(8,128)} %refs_0_.1, f32[2,3,16,32,128]{4,3,2,1,0:T(8,128)} %refs_1_.1, s32[16,32,128]{2,1,0:T(8,128)} %material_hbm.3, s32[16,32,128]{2,1,0:T(8,128)} %pattern_hbm.3, ...), custom_call_target="tpu_custom_call" | custom-call | bytes 12000000 | tf_op jit(solution)/shard_map/own/pallas_call | solution.py:852
  14.7 0.0 collective-permute-done.rows_b_hbm
  14.7 0.0 collective-permute-done.1.rows_a_hbm
  14.7 2.3 %pack.1 = (f32[13,40,128]{2,1,0:T(8,128)}, f32[4,40,128]{2,1,0:T(8,128)}, f32[4,40,128]{2,1,0:T(8,128)}, f32[8,128]{1,0:T(8,128)}) custom-call(f32[13,32,128]{2,1,0:T(8,128)} %get-tuple-element.26.own_hbm, f32[4,32,128]{2,1,0:T(8,128)} %get-tuple-element.27.main_a_hbm, f32[4,32,128]{2,1,0:T(8,128)} %get-tuple-element.28.main_b_hbm, ...), custom_call_target="tpu_custom_call" | custom-call | bytes 6000000 | tf_op jit(solution)/shard_map/pack/pallas_call | solution.py:874
  17.0 5.0 %collective-permute-start.2 = (f32[4,40,128]{2,1,0:T(8,128)}, f32[4,40,128]{2,1,0:T(8,128)}, u32[]{:S(2)}, u32[]{:S(2)}) collective-permute-start(f32[4,40,128]{2,1,0:T(8,128)} %get-tuple-element.34), channel_id=1, source_target_pairs={{0,7},{1,2},{2,1},{3,4},{4,3},{5,6},{6,5},{7,0},{8,15},{9,10},{10,... | collective-permute-start | bytes 245768 | tf_op jit(solution)/shard_map/ppermute | solution.py:29
  22.0 0.0 collective-permute-start.3
  22.6 1.5 %tables.1 = (f32[256,256]{1,0:T(8,128)}, f32[128,128]{1,0:T(8,128)}) custom-call(f32[2]{0:T(128)} %phase_hbm.3, f32[8,128]{1,0:T(8,128)} %get-tuple-element.29.rot_hbm.after_hbm.refs_9_), custom_call_target="tpu_custom_call" | custom-call | bytes 6000000 | tf_op jit(solution)/shard_map/tables/pallas_call | solution.py:894
  24.2 2.1 %feet.1 = (f32[2,3,16,8,128]{4,3,2,1,0:T(8,128)}, f32[2,3,16,8,128]{4,3,2,1,0:T(8,128)}, f32[16,8,128]{2,1,0:T(8,128)}) custom-call(f32[52,8,128]{2,1,0:T(8,128)} %collective-permute-done.rows_b_hbm, f32[52,8,128]{2,1,0:T(8,128)} %collective-permute-done.1.rows_a_hbm, f32[8,128]{1,0:T(8,128)} %get-tuple-element.29.rot_hbm.after_hbm.refs_9_), custom_call_target="tpu_custom_call" | custom-call | bytes 6000000 | tf_op jit(solution)/shard_map/feet/pallas_call | solution.py:906
  26.2 0.0 collective-permute-done.2.cols_b_hbm.refs_7_
  26.3 0.0 collective-permute-done.3.cols_a_hbm.refs_8_
  26.3 3.3 %plane.1 = f32[2,8,32,128]{3,2,1,0:T(8,128)} custom-call(f32[2,3,16,32,128]{4,3,2,1,0:T(8,128)} %refs_0_.1, f32[2,3,16,32,128]{4,3,2,1,0:T(8,128)} %refs_1_.1, f32[16,32,128]{2,1,0:T(8,128)} %get-tuple-element.23.coef_hbm.refs_2_, f32[2,3,16,8,128]{4,3,2,1,0:T(8,128)} %get-tuple-element.30.e_foot_hbm.refs_3_, ...), custom_call_target="tpu_custom_call" | custom-call | bytes 9000000 | tf_op jit(solution)/shard_map/plane/pallas_call | solution.py:926
  29.6 5.1 %all-to-all-start = ((f32[16,32,128]{2,1,0:T(8,128)}), f32[16,32,128]{2,1,0:T(8,128)S(1)}, u32[]{:S(2)}, u32[]{:S(2)}) async-start(f32[16,32,128]{2,1,0:T(8,128)} %bitcast.1), calls=%async_computation | async-start | bytes 524288 | tf_op jit(solution)/shard_map/all_to_all | solution.py:945
  34.7 0.0 copy-start
  34.7 6.8 %fields.1 = (f32[2,3,16,32,128]{4,3,2,1,0:T(8,128)}, f32[2,3,16,32,128]{4,3,2,1,0:T(8,128)}, f32[8,128]{1,0:T(8,128)}) custom-call(f32[2,3,16,32,128]{4,3,2,1,0:T(8,128)} %refs_0_.1, f32[2,3,16,32,128]{4,3,2,1,0:T(8,128)} %refs_1_.1, f32[16,32,128]{2,1,0:T(8,128)} %get-tuple-element.23.coef_hbm.refs_2_, ...), custom_call_target="tpu_custom_call" | custom-call | bytes 18000000 | tf_op jit(solution)/shard_map/fields/pallas_call | solution.py:946
  41.5 0.7 %all-to-all-done.got_ref = f32[16,32,128]{2,1,0:T(8,128)S(1)} async-done(((f32[16,32,128]{2,1,0:T(8,128)}), f32[16,32,128]{2,1,0:T(8,128)S(1)}, u32[]{:S(2)}, u32[]{:S(2)}) %all-to-all-start) | async-done | bytes 262176 | tf_op jit(solution)/shard_map/all_to_all | solution.py:945
  42.2 0.0 copy-done
  42.2 0.0 copy-start.1
  42.2 0.7 %copy-done.1 = f32[8,128]{1,0:T(8,128)S(1)} copy-done((f32[8,128]{1,0:T(8,128)S(1)}, f32[8,128]{1,0:T(8,128)}, u32[]{:S(2)}) %copy-start.1) | copy-done | bytes 4120
  42.9 0.3 x_section.1
  43.2 14.7 %all_to_all.10.got_ref = f32[16,8,128]{2,1,0:T(8,128)S(1)} all-to-all(f32[16,8,128]{2,1,0:T(8,128)S(1)} %x_section.1), channel_id=1, replica_groups={{0,8,16,24,32,40,48,56,64,72,80,88,96,104,112,120},{1,9,17,25,33,41,49,..., dimensions={0} | all-to-all | bytes 131072 | tf_op jit(solution)/shard_map/all_to_all | solution.py:965
  57.9 0.7 %order_sum.1 = f32[2,2,8,32]{3,2,1,0:T(8,128)} custom-call(f32[16,8,128]{2,1,0:T(8,128)S(1)} %all_to_all.10.got_ref), custom_call_target="tpu_custom_call" | custom-call | bytes 3000000 | tf_op jit(solution)/shard_map/order_sum/pallas_call | solution.py:966
Async XLA Ops:
  3.1 11.6 %collective-permute-start = (f32[52,8,128]{2,1,0:T(8,128)}, f32[52,8,128]{2,1,0:T(8,128)}, u32[]{:S(2)}, u32[]{:S(2)}) collective-permute-start(f32[52,8,128]{2,1,0:T(8,128)} %get-tuple-element.24), channel_id=1, source_target_pairs={{0,248},{8,16},{16,8},{24,32},{32,24},{40,48},{48,40},{56,64},{64,... | collective-permute-start | bytes 638984 | tf_op jit(solution)/shard_map/ppermute | solution.py:29
  6.2 8.5 %collective-permute-start.1 = (f32[52,8,128]{2,1,0:T(8,128)}, f32[52,8,128]{2,1,0:T(8,128)}, u32[]{:S(2)}, u32[]{:S(2)}) collective-permute-start(f32[52,8,128]{2,1,0:T(8,128)} %get-tuple-element.25), channel_id=1, source_target_pairs={{0,8},{8,0},{16,24},{24,16},{32,40},{40,32},{48,56},{56,48},{64,72... | collective-permute-start | bytes 638984 | tf_op jit(solution)/shard_map/ppermute | solution.py:29
  17.0 9.2 %collective-permute-start.2 = (f32[4,40,128]{2,1,0:T(8,128)}, f32[4,40,128]{2,1,0:T(8,128)}, u32[]{:S(2)}, u32[]{:S(2)}) collective-permute-start(f32[4,40,128]{2,1,0:T(8,128)} %get-tuple-element.34), channel_id=1, source_target_pairs={{0,7},{1,2},{2,1},{3,4},{4,3},{5,6},{6,5},{7,0},{8,15},{9,10},{10,... | collective-permute-start | bytes 245768 | tf_op jit(solution)/shard_map/ppermute | solution.py:29
  22.0 4.3 %collective-permute-start.3 = (f32[4,40,128]{2,1,0:T(8,128)}, f32[4,40,128]{2,1,0:T(8,128)}, u32[]{:S(2)}, u32[]{:S(2)}) collective-permute-start(f32[4,40,128]{2,1,0:T(8,128)} %get-tuple-element.35), channel_id=1, source_target_pairs={{0,1},{1,0},{2,3},{3,2},{4,5},{5,4},{6,7},{7,6},{8,9},{9,8},{10,11... | collective-permute-start | bytes 245768 | tf_op jit(solution)/shard_map/ppermute | solution.py:29
  29.6 12.6 %all-to-all-start = ((f32[16,32,128]{2,1,0:T(8,128)}), f32[16,32,128]{2,1,0:T(8,128)S(1)}, u32[]{:S(2)}, u32[]{:S(2)}) async-start(f32[16,32,128]{2,1,0:T(8,128)} %bitcast.1), calls=%async_computation | async-start | bytes 524288 | tf_op jit(solution)/shard_map/all_to_all | solution.py:945
  34.7 7.5 %copy-start = (f32[128,128]{1,0:T(8,128)S(1)}, f32[128,128]{1,0:T(8,128)}, u32[]{:S(2)}) copy-start(f32[128,128]{1,0:T(8,128)} %get-tuple-element.39.wave_ref) | copy-start | bytes 196612
  42.2 0.7 %copy-start.1 = (f32[8,128]{1,0:T(8,128)S(1)}, f32[8,128]{1,0:T(8,128)}, u32[]{:S(2)}) copy-start(f32[8,128]{1,0:T(8,128)} %get-tuple-element.40.after_hbm) | copy-start | bytes 12292

commit v5 on v4

--- a/solution.py
+++ b/solution.py
@@ -15,7 +15,7 @@
 ROWS = 32
 COLS = 128
 EXT = 40
-MAIN_BLOCKS = 52
+MAIN_BLOCKS = 48
 VMEM = pltpu.VMEM
 SMEM = pltpu.SMEM
 
@@ -145,18 +145,21 @@
     arrived(small)
     table = coef_table(base_ref, mode_ref, node_ref)
     table_ref[...] = table
-    arrived(large)
-    for n in range(13):
+    row = lax.broadcasted_iota(jnp.int32, (8, COLS), 0)
+    for n in range(12):
+        if n % 6 == 0:
+            arrived(large[0:2] if n == 0 else large[2:])
         for quad in range(NZ // 4):
             blocks = []
             for k in range(2):
                 pieces = []
                 for z in range(4 * quad, 4 * quad + 4):
-                    if n == 12:
-                        values = look_up(table, material_ref[k, z] * 16 + pattern_ref[k, z])
-                    else:
-                        ref = e_ref if n < 6 else h_ref
-                        values = ref[k, (n % 6) // 3, n % 3, z]
+                    ref = e_ref if n < 6 else h_ref
+                    values = ref[k, (n % 6) // 3, n % 3, z]
+                    if n == 6:
+                        coef = look_up(table, material_ref[k, z] * 16 + pattern_ref[k, z])
+                        coef = roll(coef, -1 if k else 1, 0)
+                        values = jnp.where(row == (6 if k else 1), coef, values)
                     pieces.append(values[6 * k : 6 * k + 2])
                 blocks.append(jnp.concatenate(pieces, axis=0))
             first_swap_ref[4 * n + quad] = jnp.where(even, blocks[1], blocks[0])
@@ -166,21 +169,22 @@
 def messages(own_ref, rows, first_swap_ref, second_swap_ref):
     even = is_even("gy")
     place = lanes_of((rows.stop - rows.start, COLS)) % 8
-    for c in range(4):
-        if c == 3:
-            right = left = own_ref[12, rows, :]
-        else:
-            e_re, e_im, h_re, h_im = (own_ref[3 * k + c, rows, :] for k in range(4))
-            right = jnp.where(
-                place < 4,
-                jnp.where(place < 2, roll(h_re, -4, 1), roll(h_im, -2, 1)),
-                jnp.where(place < 6, e_re, roll(e_im, 2, 1)),
-            )
-            left = jnp.where(
-                place < 4,
-                jnp.where(place < 2, roll(h_im, -6, 1), roll(h_re, -4, 1)),
-                jnp.where(place < 6, roll(e_im, -2, 1), e_re),
-            )
+    for c in range(3):
+        e_re, e_im, h_re, h_im = (own_ref[3 * k + c] for k in range(4))
+        right = jnp.where(
+            place < 4,
+            jnp.where(place < 2, roll(h_re, -4, 1), roll(h_im, -2, 1)),
+            jnp.where(place < 6, e_re, roll(e_im, 2, 1)),
+        )
+        left = jnp.where(
+            place < 4,
+            jnp.where(place < 2, roll(h_im, -6, 1), roll(h_re, -4, 1)),
+            jnp.where(place < 6, roll(e_im, -2, 1), e_re),
+        )
+        if c == 1:
+            coef = own_ref[12]
+            right = jnp.where(place == 0, roll(coef, -5, 1), right)
+            left = jnp.where(place == 3, roll(coef, -3, 1), left)
         first_swap_ref[c, rows, :] = jnp.where(even, right, left)
         second_swap_ref[c, rows, :] = jnp.where(even, left, right)
 
@@ -210,9 +214,10 @@
     table = table_ref[...]
     for z in range(NZ):
         coef_ref[z] = look_up(table, material_ref[z] * 16 + pattern_ref[z])
-    arrived(large)
     group = lanes_of((ROWS, COLS)) // 8
     for n in range(13):
+        if n in (0, 6):
+            arrived(large[n // 6 : n // 6 + 1])
         packed = jnp.zeros((ROWS, COLS), jnp.float32)
         for z in range(NZ):
             values = coef_ref[z] if n == 12 else plane_of(e_ref, h_ref, n, z)
@@ -241,13 +246,12 @@
 
 
 def pack_kernel(
-    own_hbm,
     main_a_hbm,
     main_b_hbm,
     rows_b_hbm,
     rows_a_hbm,
     phase_hbm,
-    all_ref,
+    tail_ref,
     first_swap_ref,
     second_swap_ref,
     rot_ref,
@@ -260,7 +264,6 @@
     copies = fetch_swapped((rows_a_hbm, rows_b_hbm), next_ref, prev_ref, is_even("gx"), sem, 1)
     mains = fetch(
         [
-            (own_hbm, all_ref.at[:, 0:ROWS]),
             (main_a_hbm, first_swap_ref.at[:, 0:ROWS]),
             (main_b_hbm, second_swap_ref.at[:, 0:ROWS]),
         ],
@@ -286,17 +289,21 @@
         return total + roll(total, 4, 0)
 
     quads = range(NZ // 4)
-    for n in (0, 1, 2, 6, 7, 8, 12):
-        parts = 1 if n == 12 else 2
-        sides = []
-        for ref, cos, sin in ((next_ref, rot[0], rot[1]), (prev_ref, rot[2], rot[3])):
-            found = [packed([ref[4 * (n + 3 * part) + quad] for quad in quads]) for part in range(parts)]
-            sides.append(turned(found[0], found[1], cos, sin) if parts == 2 else found)
-        for part in range(parts):
-            all_ref[n + 3 * part, ROWS:EXT, :] = jnp.where(
-                row < 2, sides[0][part], jnp.where(row < 6, 0.0, sides[1][part])
-            )
-    messages(all_ref, slice(ROWS, EXT), first_swap_ref, second_swap_ref)
+    def joined(ahead, behind):
+        return jnp.where(row < 2, ahead, jnp.where(row < 6, 0.0, behind))
+
+    for n in (0, 1, 2, 6, 7, 8):
+        found = [
+            [packed([ref[4 * (n + 3 * part) + quad] for quad in quads]) for part in range(2)]
+            for ref in (next_ref, prev_ref)
+        ]
+        if n == 6:
+            tail_ref[12] = joined(roll(found[0][0], -1, 0), roll(found[1][0], 1, 0))
+        ahead = turned(*found[0], rot[0], rot[1])
+        behind = turned(*found[1], rot[2], rot[3])
+        for part in range(2):
+            tail_ref[n + 3 * part] = joined(ahead[part], behind[part])
+    messages(tail_ref, slice(ROWS, EXT), first_swap_ref, second_swap_ref)
     arrived(mains)
 
 
@@ -325,7 +332,7 @@
         for part in range(2):
             strip[3 * part + c] = joined(3 * part + c, e_right[part], e_left[part])
             strip[6 + 3 * part + c] = joined(6 + 3 * part + c, h_right[part], h_left[part])
-    strip[12] = joined(12, right[3], roll(left[3], -4, 1))
+    strip[12] = joined(12, roll(right[1], 5, 1), roll(left[1], -1, 1))
     return strip
 
 
@@ -379,11 +386,26 @@
 
 
 def feet_kernel(
-    rows_b_hbm, rows_a_hbm, rot_hbm, e_ref, h_ref, coef_ref, next_ref, prev_ref, rot_ref, sem
+    counts,
+    rows_b_hbm,
+    rows_a_hbm,
+    rot_hbm,
+    phase_hbm,
+    e_ref,
+    h_ref,
+    coef_ref,
+    y_ref,
+    x_ref,
+    next_ref,
+    prev_ref,
+    rot_ref,
+    phase_ref,
+    sem,
 ):
-    copies = fetch([(rot_hbm, rot_ref)], sem)
-    copies += fetch_swapped((rows_a_hbm, rows_b_hbm), next_ref, prev_ref, is_even("gx"), sem, 1)
+    copies = fetch([(phase_hbm, phase_ref), (rot_hbm, rot_ref)], sem)
+    copies += fetch_swapped((rows_a_hbm, rows_b_hbm), next_ref, prev_ref, is_even("gx"), sem, 2)
     arrived(copies)
+    fill_tables(*counts, phase_ref[0], phase_ref[1], y_ref, x_ref)
     rot = [rot_ref[k : k + 1, :] for k in range(8)]
     row = lax.broadcasted_iota(jnp.int32, (8, COLS), 0)
 
@@ -404,14 +426,24 @@
                 for part in range(2):
                     for k in range(4):
                         target[part, c, 4 * quad + k] = foot(ahead[part], behind[part], k)
+        ahead = roll(next_ref[24 + quad], -1, 0)
+        behind = roll(prev_ref[24 + quad], 1, 0)
         for k in range(4):
-            coef_ref[4 * quad + k] = foot(next_ref[48 + quad], prev_ref[48 + quad], k)
-
-
-def fetch_edges(own_hbm, cols_hbm, rot_hbm, edges, sem, first):
+            coef_ref[4 * quad + k] = foot(ahead, behind, k)
+
+
+def fetch_edges(own_hbm, tail_hbm, cols_hbm, rot_hbm, edges, sem, first):
     own_ref, right_ref, left_ref, rot_ref = edges
-    copies = fetch([(own_hbm, own_ref), (rot_hbm, rot_ref)], sem, first)
-    copies += fetch_swapped(cols_hbm, left_ref, right_ref, is_even("gy"), sem, first + 2)
+    copies = fetch(
+        [
+            (own_hbm, own_ref.at[:, 0:ROWS]),
+            (tail_hbm, own_ref.at[:, ROWS:EXT]),
+            (rot_hbm, rot_ref),
+        ],
+        sem,
+        first,
+    )
+    copies += fetch_swapped(cols_hbm, left_ref, right_ref, is_even("gy"), sem, first + 3)
     return copies
 
 
@@ -420,8 +452,8 @@
         VMEM(shape, jnp.float32)
         for shape in (
             (13, EXT, COLS),
-            (4, EXT, COLS),
-            (4, EXT, COLS),
+            (3, EXT, COLS),
+            (3, EXT, COLS),
             (8, COLS),
         )
     ]
@@ -446,8 +478,8 @@
             h_all[at, c, 0] = jnp.zeros((EXT, COLS), jnp.float32)
     strip = strip_of(
         [own_ref[a] for a in range(13)],
-        [right_ref[a] for a in range(4)],
-        [left_ref[a] for a in range(4)],
+        [right_ref[a] for a in range(3)],
+        [left_ref[a] for a in range(3)],
         rot,
     )
     for at, part in enumerate(parts):
@@ -507,9 +539,10 @@
                     e, h, h_down, (prev_row(h[1]), prev_row(h[2])), h_yp, coef_all[z]
                 )
                 new.append((at, z, values))
+        rows = slice(0, EXT if step == 0 else ROWS)
         for at, z, values in new:
             for c in range(3):
-                e_all[at, c, z] = values[c]
+                e_all[at, c, z, rows, :] = values[c][rows]
 
     return do_h, do_e
 
@@ -522,6 +555,7 @@
     h_foot_hbm,
     coef_foot_hbm,
     own_hbm,
+    tail_hbm,
     cols_b_hbm,
     cols_a_hbm,
     rot_hbm,
@@ -533,7 +567,7 @@
     edges, block = scratch[0:4], scratch[4:8]
     wave_ref, sem = scratch[8:10]
     e_all, h_all, coef_all, edge_ref = block
-    copies = fetch_edges(own_hbm, (cols_a_hbm, cols_b_hbm), rot_hbm, edges, sem, 0)
+    copies = fetch_edges(own_hbm, tail_hbm, (cols_a_hbm, cols_b_hbm), rot_hbm, edges, sem, 0)
     level = monitor_ref[0]
     low = jnp.clip(level - 2, 0, NZ - 5)
     here, there = pl.ds(low, 5), pl.ds(low + 1, 5)
@@ -548,7 +582,7 @@
             (wave_hbm, wave_ref),
         ],
         sem,
-        4,
+        5,
     )
     arrived(copies)
     fill_edges(edges, block, (0, 1))
@@ -619,16 +653,16 @@
         h_foot_hbm,
         coef_foot_hbm,
         own_hbm,
+        tail_hbm,
         cols_b_hbm,
         cols_a_hbm,
         rot_hbm,
-    ) = refs[0:10]
-    e_out, h_out, token_ref = refs[inputs : inputs + 3]
-    token_ref[...] = jnp.zeros_like(token_ref)
+    ) = refs[0:11]
+    e_out, h_out, token_hbm = refs[inputs : inputs + 3]
     scratch = refs[inputs + 3 :]
     edges, block, sem = scratch[0:4], scratch[4:8], scratch[8]
     e_all, h_all, coef_all, _ = block
-    copies = fetch_edges(own_hbm, (cols_a_hbm, cols_b_hbm), rot_hbm, edges, sem, 0)
+    copies = fetch_edges(own_hbm, tail_hbm, (cols_a_hbm, cols_b_hbm), rot_hbm, edges, sem, 0)
     some = slice(parts[0], parts[-1] + 1)
     quads = range(NZ // 4)
     loads = []
@@ -645,10 +679,11 @@
                     (coef_foot_hbm.at[here], coef_all.at[here, ROWS:EXT, :]),
                 ],
                 sem,
-                6 + 6 * quad,
+                7 + 6 * quad,
             )
         )
     arrived(copies)
+    token = fetch([(edges[3], token_hbm)], sem)
     fill_edges(edges, block, parts)
     do_h, do_e = updates(block, len(parts))
 
@@ -656,9 +691,9 @@
         layers = [4 * quad + k for k in range(4)]
         here, there = pl.ds(4 * quad, 4), pl.ds(4 * quad + 1, 4)
         do_h(1, layers)
-        fetch([(h_all.at[:, :, there, 0:ROWS, :], h_out.at[some, :, here])], sem, 4)
+        fetch([(h_all.at[:, :, there, 0:ROWS, :], h_out.at[some, :, here])], sem, 5)
         do_e(1, layers)
-        fetch([(e_all.at[:, :, here, 0:ROWS, :], e_out.at[some, :, here])], sem, 5)
+        fetch([(e_all.at[:, :, here, 0:ROWS, :], e_out.at[some, :, here])], sem, 6)
 
     arrived(loads[0])
     for quad in quads:
@@ -670,12 +705,13 @@
         if quad > 0:
             finish(quad - 1)
     finish(quads[-1])
+    arrived(token)
     stored = (
         (h_all.at[:, :, 1 : NZ + 1, 0:ROWS, :], h_out.at[some]),
         (e_all.at[:, :, 0:NZ, 0:ROWS, :], e_out.at[some]),
     )
     for k, (source, target) in enumerate(stored):
-        pltpu.make_async_copy(source, target, sem.at[4 + k]).wait()
+        pltpu.make_async_copy(source, target, sem.at[5 + k]).wait()
 
 
 def y_section(re, im, wave_ref, spread_ref):
@@ -749,12 +785,8 @@
             out_ref[c, part] = total[:, start : start + each]
 
 
-def table_kernel(
-    count_x, count_y, phase_hbm, after_hbm, y_ref, x_ref, phase_ref, sem
-):
-    arrived(fetch([(phase_hbm, phase_ref)], sem))
+def fill_tables(count_x, count_y, theta_x, theta_y, y_ref, x_ref):
     index_x, index_y = lax.axis_index("gx"), lax.axis_index("gy")
-    theta_x, theta_y = phase_ref[0], phase_ref[1]
     total_x, total_y = ROWS * count_x, COLS * count_y
 
     def waves(product, place, total, theta):
@@ -853,8 +885,8 @@
         own_kernel,
         out_shape=(
             f32(13, ROWS, COLS),
-            f32(4, ROWS, COLS),
-            f32(4, ROWS, COLS),
+            f32(3, ROWS, COLS),
+            f32(3, ROWS, COLS),
             f32(NZ, ROWS, COLS),
         ),
         in_specs=[hbm] * 5,
@@ -871,68 +903,61 @@
         cost_estimate=cost(4),
         name="own",
     )(e_field, h_field, material, pattern, table)
-    own, cols_a, cols_b, rot = pl.pallas_call(
+    tail, cols_a, cols_b, rot = pl.pallas_call(
         pack_kernel,
         out_shape=(
-            f32(13, EXT, COLS),
-            f32(4, EXT, COLS),
-            f32(4, EXT, COLS),
+            f32(13, EXT - ROWS, COLS),
+            f32(3, EXT, COLS),
+            f32(3, EXT, COLS),
             f32(8, COLS),
         ),
-        in_specs=[hbm] * 6,
+        in_specs=[hbm] * 5,
         out_specs=(vmem,) * 4,
         scratch_shapes=[
             f32_vmem(MAIN_BLOCKS, 8, COLS),
             f32_vmem(MAIN_BLOCKS, 8, COLS),
             SMEM((2,), jnp.float32),
-            dma((6,)),
+            dma((5,)),
         ],
         compiler_params=params(64),
         cost_estimate=cost(2),
         name="pack",
-    )(own, cols_a, cols_b, rows_b, rows_a, bloch_phase)
-    y_wave, x_wave = pl.pallas_call(
-        functools.partial(table_kernel, count_x, count_y),
-        out_shape=(f32(2 * COLS, ORD_Y), f32(ORD_X // 2, 4 * ROWS)),
-        in_specs=[hbm, hbm],
-        out_specs=(vmem,) * 2,
-        scratch_shapes=[SMEM((2,), jnp.float32), dma((1,))],
-        compiler_params=params(64),
-        cost_estimate=cost(2),
-        name="tables",
-    )(bloch_phase, rot)
+    )(cols_a, cols_b, rows_b, rows_a, bloch_phase)
     cols_b = swapped(cols_b, "gy", False)
     cols_a = swapped(cols_a, "gy", True)
-    feet = pl.pallas_call(
-        feet_kernel,
+    *feet, y_wave, x_wave = pl.pallas_call(
+        functools.partial(feet_kernel, (count_x, count_y)),
         out_shape=(
             f32(2, 3, NZ, EXT - ROWS, COLS),
             f32(2, 3, NZ, EXT - ROWS, COLS),
             f32(NZ, EXT - ROWS, COLS),
+            f32(2 * COLS, ORD_Y),
+            f32(ORD_X // 2, 4 * ROWS),
         ),
-        in_specs=[hbm] * 3,
-        out_specs=(vmem,) * 3,
+        in_specs=[hbm] * 4,
+        out_specs=(vmem,) * 5,
         scratch_shapes=[
             f32_vmem(MAIN_BLOCKS, 8, COLS),
             f32_vmem(MAIN_BLOCKS, 8, COLS),
             f32_vmem(8, COLS),
-            dma((3,)),
+            SMEM((2,), jnp.float32),
+            dma((4,)),
         ],
         compiler_params=params(64),
         cost_estimate=cost(2),
         name="feet",
-    )(rows_b, rows_a, rot)
-    around = (e_field, h_field, coef, *feet, own, cols_b, cols_a, rot)
+    )(rows_b, rows_a, rot, bloch_phase)
+    around = (e_field, h_field, coef, *feet, own, tail, cols_b, cols_a, rot)
     spread = pl.pallas_call(
         plane_kernel,
         out_shape=f32(2, count_y, ROWS, 4 * each_q),
-        in_specs=[hbm] * 11 + [pl.BlockSpec(memory_space=SMEM)],
+        in_specs=[hbm] * 12 + [pl.BlockSpec(memory_space=SMEM)],
         out_specs=vmem,
         scratch_shapes=[
             *edge_scratch(),
             *block_scratch(2),
             f32_vmem(*y_wave.shape),
-            dma((11,)),
+            dma((12,)),
         ],
         compiler_params=params(60),
         cost_estimate=cost(3),
@@ -944,11 +969,11 @@
     spread = spread.reshape(2 * count_y, ROWS, 4 * each_q)
     got = lax.all_to_all(spread, both, 0, 0, tiled=True, axis_index_groups=near)
     e_out, h_out, token = pl.pallas_call(
-        functools.partial(field_kernel, (0, 1), 11),
+        functools.partial(field_kernel, (0, 1), 12),
         out_shape=(f32(*e_field.shape), f32(*h_field.shape), f32(8, COLS)),
-        in_specs=[hbm] * 11,
-        out_specs=(hbm, hbm, vmem),
-        scratch_shapes=[*edge_scratch(), *block_scratch(2), dma((30,))],
+        in_specs=[hbm] * 12,
+        out_specs=(hbm, hbm, hbm),
+        scratch_shapes=[*edge_scratch(), *block_scratch(2), dma((31,))],
         compiler_params=params(60),
         cost_estimate=cost(6),
         name="fields",

time: 59 us -> 58.5 us (level)
  Pallas kernels: 23.2 us -> 20.6 us
  blocking collectives: 14.7 us -> 15.8 us
  waiting for transfers between devices: 0.73 us -> 1.82 us
    pallas_call x5 -> x4, Pallas kernels: 16.5 us -> 13.9 us  [the longest x1 6.12 us: shards(): pl.pallas_call(functools.partial(field_kernel, (0, 1), 12), out_shape=(f3...]
    all_to_all x1, blocking collectives: 14.7 us -> 15.8 us  [shards(): got = lax.all_to_all(partial, both, 0, 0, tiled=True, axis_index_groups=far)]
    all_to_all x1, waiting for transfers between devices: 0.72 us -> 1.35 us  [shards(): got = lax.all_to_all(spread, both, 0, 0, tiled=True, axis_index_groups=near)]
  transfers between devices with their start and end apart: 5 -> 5, of which waited for: 1 -> 2; matrix products, arithmetic and copies ran while one was open for 0% -> 0% of each run, Pallas kernels for 24% -> 20%
where the time goes in v5:
time: 58.5 us; the launch traced here: 58.1 us
  Pallas kernels  20.6 us (35%)
  starting transfers between devices  17.8 us (30%)
  blocking collectives  15.8 us (27%)
  waiting for transfers between devices  1.82 us (3%)
  between operations  1.38 us (2%)
  local copies, waits for them, and re-layouts  0.69 us (1%)
    all_to_all x1, blocking collectives, shards(): got = lax.all_to_all(partial, both, 0, 0, tiled=True, axis_index_groups=far)  15.8 us
    ppermute x4, starting transfers between devices, swapped(): return lax.ppermute(block, axis, route)  12.8 us
    pallas_call x1, Pallas kernels, shards(): pl.pallas_call(functools.partial(field_kernel, (0, 1), 12), out_shape=(f3...  6.12 us
    all_to_all x1, starting transfers between devices, shards(): got = lax.all_to_all(spread, both, 0, 0, tiled=True, axis_index_groups=near)  5.01 us
    pallas_call x1, Pallas kernels, shards(): pl.pallas_call(own_kernel, out_shape=(f32(13, ROWS, COLS), f32(3, ROWS, C...  3.39 us
    pallas_call x1, Pallas kernels, shards(): pl.pallas_call(plane_kernel, out_shape=f32(2, count_y, ROWS, 4 * each_q),...  3.36 us
    pallas_call x1, Pallas kernels, shards(): pl.pallas_call(rows_kernel, out_shape=(f32(8, COLS), f32(MAIN_BLOCKS, 8,...  2.42 us
    pallas_call x1, Pallas kernels, shards(): pl.pallas_call(functools.partial(feet_kernel, (count_x, count_y)), out_sh...  2.26 us
  transfers between devices with their start and end apart: 5, of which 2 were waited for; matrix products, arithmetic and copies ran while one was open for 0% of the time, Pallas kernels for 20%

profile of v5, /device:TPU:1, one launch (start us, length us, event | category | flops | bytes accessed | tf_op | source)
XLA Modules:
  0.0 58.1 jit_solution(2258516590991943320)
XLA Ops:
  0.6 2.4 %rows.1 = (f32[8,128]{1,0:T(8,128)}, f32[48,8,128]{2,1,0:T(8,128)}, f32[48,8,128]{2,1,0:T(8,128)}) custom-call(f32[2,3,16,32,128]{4,3,2,1,0:T(8,128)} %refs_0_.1, f32[2,3,16,32,128]{4,3,2,1,0:T(8,128)} %refs_1_.1, s32[16,32,128]{2,1,0:T(8,128)} %material_hbm.3, s32[16,32,128]{2,1,0:T(8,128)} %pattern_hbm.3, f32[8]{0:T(128)} %base_hbm.1, f32[4,16]{1,0:T(4,128)} %mode_hbm.1, ...), custom_call_target="tpu_custom_call" | custom-call | bytes 9000000 | tf_op jit(solution)/shard_map/rows/pallas_call | solution.py:859
  3.1 3.1 %collective-permute-start = (f32[48,8,128]{2,1,0:T(8,128)}, f32[48,8,128]{2,1,0:T(8,128)}, u32[]{:S(2)}, u32[]{:S(2)}) collective-permute-start(f32[48,8,128]{2,1,0:T(8,128)} %get-tuple-element.24), channel_id=1, source_target_pairs={{0,248},{8,16},{16,8},{24,32},{32,24},{40,48},{48,40},{56,64},{64,... | collective-permute-start | bytes 589832 | tf_op jit(solution)/shard_map/ppermute | solution.py:29
  6.2 4.7 %collective-permute-start.1 = (f32[48,8,128]{2,1,0:T(8,128)}, f32[48,8,128]{2,1,0:T(8,128)}, u32[]{:S(2)}, u32[]{:S(2)}) collective-permute-start(f32[48,8,128]{2,1,0:T(8,128)} %get-tuple-element.25), channel_id=1, source_target_pairs={{0,8},{8,0},{16,24},{24,16},{32,40},{40,32},{48,56},{56,48},{64,72... | collective-permute-start | bytes 589832 | tf_op jit(solution)/shard_map/ppermute | solution.py:29
  10.9 3.4 %own.1 = (f32[13,32,128]{2,1,0:T(8,128)}, f32[3,32,128]{2,1,0:T(8,128)}, f32[3,32,128]{2,1,0:T(8,128)}, f32[16,32,128]{2,1,0:T(8,128)}) custom-call(f32[2,3,16,32,128]{4,3,2,1,0:T(8,128)} %refs_0_.1, f32[2,3,16,32,128]{4,3,2,1,0:T(8,128)} %refs_1_.1, s32[16,32,128]{2,1,0:T(8,128)} %material_hbm.3, s32[16,32,128]{2,1,0:T(8,128)} %pattern_hbm.3, ...), custom_call_target="tpu_custom_call" | custom-call | bytes 12000000 | tf_op jit(solution)/shard_map/own/pallas_call | solution.py:884
  14.3 0.0 collective-permute-done.rows_b_hbm
  14.3 0.0 collective-permute-done.1.rows_a_hbm
  14.3 2.1 %pack.1 = (f32[13,8,128]{2,1,0:T(8,128)}, f32[3,40,128]{2,1,0:T(8,128)}, f32[3,40,128]{2,1,0:T(8,128)}, f32[8,128]{1,0:T(8,128)}) custom-call(f32[3,32,128]{2,1,0:T(8,128)} %get-tuple-element.26.main_a_hbm, f32[3,32,128]{2,1,0:T(8,128)} %get-tuple-element.27.main_b_hbm, f32[48,8,128]{2,1,0:T(8,128)} %collective-permute-done.rows_b_hbm, ...), custom_call_target="tpu_custom_call" | custom-call | bytes 6000000 | tf_op jit(solution)/shard_map/pack/pallas_call | solution.py:906
  16.4 5.0 %collective-permute-start.2 = (f32[3,40,128]{2,1,0:T(8,128)}, f32[3,40,128]{2,1,0:T(8,128)}, u32[]{:S(2)}, u32[]{:S(2)}) collective-permute-start(f32[3,40,128]{2,1,0:T(8,128)} %get-tuple-element.34), channel_id=1, source_target_pairs={{0,7},{1,2},{2,1},{3,4},{4,3},{5,6},{6,5},{7,0},{8,15},{9,10},{10,... | collective-permute-start | bytes 184328 | tf_op jit(solution)/shard_map/ppermute | solution.py:29
  21.4 0.0 collective-permute-start.3
  22.1 2.3 %feet.1 = (f32[2,3,16,8,128]{4,3,2,1,0:T(8,128)}, f32[2,3,16,8,128]{4,3,2,1,0:T(8,128)}, f32[16,8,128]{2,1,0:T(8,128)}, f32[256,256]{1,0:T(8,128)}, f32[128,128]{1,0:T(8,128)}) custom-call(f32[48,8,128]{2,1,0:T(8,128)} %collective-permute-done.rows_b_hbm, f32[48,8,128]{2,1,0:T(8,128)} %collective-permute-done.1.rows_a_hbm, ...), custom_call_target="tpu_custom_call" | custom-call | bytes 6000000 | tf_op jit(solution)/shard_map/feet/pallas_call | solution.py:928
  24.3 0.0 collective-permute-done.2.cols_b_hbm.refs_8_
  24.3 0.5 collective-permute-done.3.cols_a_hbm.refs_9_
  24.8 3.4 %plane.1 = f32[2,8,32,128]{3,2,1,0:T(8,128)} custom-call(f32[2,3,16,32,128]{4,3,2,1,0:T(8,128)} %refs_0_.1, f32[2,3,16,32,128]{4,3,2,1,0:T(8,128)} %refs_1_.1, f32[16,32,128]{2,1,0:T(8,128)} %get-tuple-element.23.coef_hbm.refs_2_, f32[2,3,16,8,128]{4,3,2,1,0:T(8,128)} %get-tuple-element.29.e_foot_hbm.refs_3_, ...), custom_call_target="tpu_custom_call" | custom-call | bytes 9000000 | tf_op jit(solution)/shard_map/plane/pallas_call | solution.py:951
  28.2 5.0 %all-to-all-start = ((f32[16,32,128]{2,1,0:T(8,128)}), f32[16,32,128]{2,1,0:T(8,128)S(1)}, u32[]{:S(2)}, u32[]{:S(2)}) async-start(f32[16,32,128]{2,1,0:T(8,128)} %bitcast.1), calls=%async_computation | async-start | bytes 524288 | tf_op jit(solution)/shard_map/all_to_all | solution.py:970
  33.2 0.0 copy-start
  33.2 6.1 %fields.1 = (f32[2,3,16,32,128]{4,3,2,1,0:T(8,128)}, f32[2,3,16,32,128]{4,3,2,1,0:T(8,128)}, f32[8,128]{1,0:T(8,128)}) custom-call(f32[2,3,16,32,128]{4,3,2,1,0:T(8,128)} %refs_0_.1, f32[2,3,16,32,128]{4,3,2,1,0:T(8,128)} %refs_1_.1, f32[16,32,128]{2,1,0:T(8,128)} %get-tuple-element.23.coef_hbm.refs_2_, ...), custom_call_target="tpu_custom_call" | custom-call | bytes 18000000 | tf_op jit(solution)/shard_map/fields/pallas_call | solution.py:971
  39.3 1.4 %all-to-all-done.got_ref = f32[16,32,128]{2,1,0:T(8,128)S(1)} async-done(((f32[16,32,128]{2,1,0:T(8,128)}), f32[16,32,128]{2,1,0:T(8,128)S(1)}, u32[]{:S(2)}, u32[]{:S(2)}) %all-to-all-start) | async-done | bytes 262176 | tf_op jit(solution)/shard_map/all_to_all | solution.py:970
  40.7 0.0 copy-done
  40.7 0.0 copy-start.1
  40.7 0.7 %copy-done.1 = f32[8,128]{1,0:T(8,128)S(1)} copy-done((f32[8,128]{1,0:T(8,128)S(1)}, f32[8,128]{1,0:T(8,128)}, u32[]{:S(2)}) %copy-start.1) | copy-done | bytes 4120
  41.4 0.3 x_section.1
  41.6 15.8 %all_to_all.10.got_ref = f32[16,8,128]{2,1,0:T(8,128)S(1)} all-to-all(f32[16,8,128]{2,1,0:T(8,128)S(1)} %x_section.1), channel_id=1, replica_groups={{0,8,16,24,32,40,48,56,64,72,80,88,96,104,112,120},{1,9,17,25,33,41,49,..., dimensions={0} | all-to-all | bytes 131072 | tf_op jit(solution)/shard_map/all_to_all | solution.py:990
  57.4 0.7 %order_sum.1 = f32[2,2,8,32]{3,2,1,0:T(8,128)} custom-call(f32[16,8,128]{2,1,0:T(8,128)S(1)} %all_to_all.10.got_ref), custom_call_target="tpu_custom_call" | custom-call | bytes 3000000 | tf_op jit(solution)/shard_map/order_sum/pallas_call | solution.py:991
Async XLA Ops:
  3.1 11.2 %collective-permute-start = (f32[48,8,128]{2,1,0:T(8,128)}, f32[48,8,128]{2,1,0:T(8,128)}, u32[]{:S(2)}, u32[]{:S(2)}) collective-permute-start(f32[48,8,128]{2,1,0:T(8,128)} %get-tuple-element.24), channel_id=1, source_target_pairs={{0,248},{8,16},{16,8},{24,32},{32,24},{40,48},{48,40},{56,64},{64,... | collective-permute-start | bytes 589832 | tf_op jit(solution)/shard_map/ppermute | solution.py:29
  6.2 8.1 %collective-permute-start.1 = (f32[48,8,128]{2,1,0:T(8,128)}, f32[48,8,128]{2,1,0:T(8,128)}, u32[]{:S(2)}, u32[]{:S(2)}) collective-permute-start(f32[48,8,128]{2,1,0:T(8,128)} %get-tuple-element.25), channel_id=1, source_target_pairs={{0,8},{8,0},{16,24},{24,16},{32,40},{40,32},{48,56},{56,48},{64,72... | collective-permute-start | bytes 589832 | tf_op jit(solution)/shard_map/ppermute | solution.py:29
  16.4 7.9 %collective-permute-start.2 = (f32[3,40,128]{2,1,0:T(8,128)}, f32[3,40,128]{2,1,0:T(8,128)}, u32[]{:S(2)}, u32[]{:S(2)}) collective-permute-start(f32[3,40,128]{2,1,0:T(8,128)} %get-tuple-element.34), channel_id=1, source_target_pairs={{0,7},{1,2},{2,1},{3,4},{4,3},{5,6},{6,5},{7,0},{8,15},{9,10},{10,... | collective-permute-start | bytes 184328 | tf_op jit(solution)/shard_map/ppermute | solution.py:29
  21.4 3.4 %collective-permute-start.3 = (f32[3,40,128]{2,1,0:T(8,128)}, f32[3,40,128]{2,1,0:T(8,128)}, u32[]{:S(2)}, u32[]{:S(2)}) collective-permute-start(f32[3,40,128]{2,1,0:T(8,128)} %get-tuple-element.35), channel_id=1, source_target_pairs={{0,1},{1,0},{2,3},{3,2},{4,5},{5,4},{6,7},{7,6},{8,9},{9,8},{10,11... | collective-permute-start | bytes 184328 | tf_op jit(solution)/shard_map/ppermute | solution.py:29
  28.2 12.5 %all-to-all-start = ((f32[16,32,128]{2,1,0:T(8,128)}), f32[16,32,128]{2,1,0:T(8,128)S(1)}, u32[]{:S(2)}, u32[]{:S(2)}) async-start(f32[16,32,128]{2,1,0:T(8,128)} %bitcast.1), calls=%async_computation | async-start | bytes 524288 | tf_op jit(solution)/shard_map/all_to_all | solution.py:970
  33.2 7.5 %copy-start = (f32[128,128]{1,0:T(8,128)S(1)}, f32[128,128]{1,0:T(8,128)}, u32[]{:S(2)}) copy-start(f32[128,128]{1,0:T(8,128)} %get-tuple-element.39.wave_ref) | copy-start | bytes 196612
  40.7 0.7 %copy-start.1 = (f32[8,128]{1,0:T(8,128)S(1)}, f32[8,128]{1,0:T(8,128)}, u32[]{:S(2)}) copy-start(f32[8,128]{1,0:T(8,128)} %get-tuple-element.40.after_hbm) | copy-start | bytes 12292

commit v6 on v5

--- a/solution.py
+++ b/solution.py
@@ -718,15 +718,14 @@
     wave = wave_ref[...]
     _, owners, _, lanes = spread_ref.shape
     each = lanes // 4
-    out = [
-        jnp.dot(
-            jnp.concatenate(pair, axis=1),
-            wave,
-            precision=lax.Precision.HIGHEST,
-            preferred_element_type=jnp.float32,
-        )
-        for pair in ((re, im), (im, -re))
-    ]
+    rows = re.shape[0]
+    both = jnp.concatenate(
+        [jnp.concatenate([re, im], axis=1), jnp.concatenate([im, -re], axis=1)], axis=0
+    )
+    both = jnp.dot(
+        both, wave, precision=lax.Precision.HIGHEST, preferred_element_type=jnp.float32
+    )
+    out = (both[0:rows], both[rows:])
     for owner in range(owners):
         pieces = [
             out[part][c * ROWS : (c + 1) * ROWS, owner * each : (owner + 1) * each]

time: 58.5 us -> 58.3 us (level)
  no operation moved by 1% of the time
where the time goes in v6:
time: 58.3 us; the launch traced here: 58 us
  Pallas kernels  20.5 us (35%)
  starting transfers between devices  17.8 us (31%)
  blocking collectives  15.8 us (27%)
  waiting for transfers between devices  1.82 us (3%)
  between operations  1.38 us (2%)
  local copies, waits for them, and re-layouts  0.69 us (1%)
    all_to_all x1, blocking collectives, shards(): got = lax.all_to_all(partial, both, 0, 0, tiled=True, axis_index_groups=far)  15.8 us
    ppermute x4, starting transfers between devices, swapped(): return lax.ppermute(block, axis, route)  12.8 us
    pallas_call x1, Pallas kernels, shards(): pl.pallas_call(functools.partial(field_kernel, (0, 1), 12), out_shape=(f3...  6.12 us
    all_to_all x1, starting transfers between devices, shards(): got = lax.all_to_all(spread, both, 0, 0, tiled=True, axis_index_groups=near)  5.01 us
    pallas_call x1, Pallas kernels, shards(): pl.pallas_call(own_kernel, out_shape=(f32(13, ROWS, COLS), f32(3, ROWS, C...  3.39 us
    pallas_call x1, Pallas kernels, shards(): pl.pallas_call(plane_kernel, out_shape=f32(2, count_y, ROWS, 4 * each_q),...  3.21 us
    pallas_call x1, Pallas kernels, shards(): pl.pallas_call(rows_kernel, out_shape=(f32(8, COLS), f32(MAIN_BLOCKS, 8,...  2.42 us
    pallas_call x1, Pallas kernels, shards(): pl.pallas_call(functools.partial(feet_kernel, (count_x, count_y)), out_sh...  2.26 us
  transfers between devices with their start and end apart: 5, of which 2 were waited for; matrix products, arithmetic and copies ran while one was open for 0% of the time, Pallas kernels for 20%

profile of v6, /device:TPU:1, one launch (start us, length us, event | category | flops | bytes accessed | tf_op | source)
XLA Modules:
  0.0 58.0 jit_solution(10902416063108660820)
XLA Ops:
  0.6 2.4 %rows.1 = (f32[8,128]{1,0:T(8,128)}, f32[48,8,128]{2,1,0:T(8,128)}, f32[48,8,128]{2,1,0:T(8,128)}) custom-call(f32[2,3,16,32,128]{4,3,2,1,0:T(8,128)} %refs_0_.1, f32[2,3,16,32,128]{4,3,2,1,0:T(8,128)} %refs_1_.1, s32[16,32,128]{2,1,0:T(8,128)} %material_hbm.3, s32[16,32,128]{2,1,0:T(8,128)} %pattern_hbm.3, f32[8]{0:T(128)} %base_hbm.1, f32[4,16]{1,0:T(4,128)} %mode_hbm.1, ...), custom_call_target="tpu_custom_call" | custom-call | bytes 9000000 | tf_op jit(solution)/shard_map/rows/pallas_call | solution.py:858
  3.1 3.1 %collective-permute-start = (f32[48,8,128]{2,1,0:T(8,128)}, f32[48,8,128]{2,1,0:T(8,128)}, u32[]{:S(2)}, u32[]{:S(2)}) collective-permute-start(f32[48,8,128]{2,1,0:T(8,128)} %get-tuple-element.24), channel_id=1, source_target_pairs={{0,248},{8,16},{16,8},{24,32},{32,24},{40,48},{48,40},{56,64},{64,... | collective-permute-start | bytes 589832 | tf_op jit(solution)/shard_map/ppermute | solution.py:29
  6.2 4.7 %collective-permute-start.1 = (f32[48,8,128]{2,1,0:T(8,128)}, f32[48,8,128]{2,1,0:T(8,128)}, u32[]{:S(2)}, u32[]{:S(2)}) collective-permute-start(f32[48,8,128]{2,1,0:T(8,128)} %get-tuple-element.25), channel_id=1, source_target_pairs={{0,8},{8,0},{16,24},{24,16},{32,40},{40,32},{48,56},{56,48},{64,72... | collective-permute-start | bytes 589832 | tf_op jit(solution)/shard_map/ppermute | solution.py:29
  10.9 3.4 %own.1 = (f32[13,32,128]{2,1,0:T(8,128)}, f32[3,32,128]{2,1,0:T(8,128)}, f32[3,32,128]{2,1,0:T(8,128)}, f32[16,32,128]{2,1,0:T(8,128)}) custom-call(f32[2,3,16,32,128]{4,3,2,1,0:T(8,128)} %refs_0_.1, f32[2,3,16,32,128]{4,3,2,1,0:T(8,128)} %refs_1_.1, s32[16,32,128]{2,1,0:T(8,128)} %material_hbm.3, s32[16,32,128]{2,1,0:T(8,128)} %pattern_hbm.3, ...), custom_call_target="tpu_custom_call" | custom-call | bytes 12000000 | tf_op jit(solution)/shard_map/own/pallas_call | solution.py:883
  14.3 0.0 collective-permute-done.rows_b_hbm
  14.3 0.0 collective-permute-done.1.rows_a_hbm
  14.3 2.1 %pack.1 = (f32[13,8,128]{2,1,0:T(8,128)}, f32[3,40,128]{2,1,0:T(8,128)}, f32[3,40,128]{2,1,0:T(8,128)}, f32[8,128]{1,0:T(8,128)}) custom-call(f32[3,32,128]{2,1,0:T(8,128)} %get-tuple-element.26.main_a_hbm, f32[3,32,128]{2,1,0:T(8,128)} %get-tuple-element.27.main_b_hbm, f32[48,8,128]{2,1,0:T(8,128)} %collective-permute-done.rows_b_hbm, ...), custom_call_target="tpu_custom_call" | custom-call | bytes 6000000 | tf_op jit(solution)/shard_map/pack/pallas_call | solution.py:905
  16.4 5.0 %collective-permute-start.2 = (f32[3,40,128]{2,1,0:T(8,128)}, f32[3,40,128]{2,1,0:T(8,128)}, u32[]{:S(2)}, u32[]{:S(2)}) collective-permute-start(f32[3,40,128]{2,1,0:T(8,128)} %get-tuple-element.34), channel_id=1, source_target_pairs={{0,7},{1,2},{2,1},{3,4},{4,3},{5,6},{6,5},{7,0},{8,15},{9,10},{10,... | collective-permute-start | bytes 184328 | tf_op jit(solution)/shard_map/ppermute | solution.py:29
  21.4 0.0 collective-permute-start.3
  22.1 2.3 %feet.1 = (f32[2,3,16,8,128]{4,3,2,1,0:T(8,128)}, f32[2,3,16,8,128]{4,3,2,1,0:T(8,128)}, f32[16,8,128]{2,1,0:T(8,128)}, f32[256,256]{1,0:T(8,128)}, f32[128,128]{1,0:T(8,128)}) custom-call(f32[48,8,128]{2,1,0:T(8,128)} %collective-permute-done.rows_b_hbm, f32[48,8,128]{2,1,0:T(8,128)} %collective-permute-done.1.rows_a_hbm, ...), custom_call_target="tpu_custom_call" | custom-call | bytes 6000000 | tf_op jit(solution)/shard_map/feet/pallas_call | solution.py:927
  24.3 0.0 collective-permute-done.2.cols_b_hbm.refs_8_
  24.3 0.5 collective-permute-done.3.cols_a_hbm.refs_9_
  24.8 3.2 %plane.1 = f32[2,8,32,128]{3,2,1,0:T(8,128)} custom-call(f32[2,3,16,32,128]{4,3,2,1,0:T(8,128)} %refs_0_.1, f32[2,3,16,32,128]{4,3,2,1,0:T(8,128)} %refs_1_.1, f32[16,32,128]{2,1,0:T(8,128)} %get-tuple-element.23.coef_hbm.refs_2_, f32[2,3,16,8,128]{4,3,2,1,0:T(8,128)} %get-tuple-element.29.e_foot_hbm.refs_3_, ...), custom_call_target="tpu_custom_call" | custom-call | bytes 9000000 | tf_op jit(solution)/shard_map/plane/pallas_call | solution.py:950
  28.0 5.0 %all-to-all-start = ((f32[16,32,128]{2,1,0:T(8,128)}), f32[16,32,128]{2,1,0:T(8,128)S(1)}, u32[]{:S(2)}, u32[]{:S(2)}) async-start(f32[16,32,128]{2,1,0:T(8,128)} %bitcast.1), calls=%async_computation | async-start | bytes 524288 | tf_op jit(solution)/shard_map/all_to_all | solution.py:969
  33.0 0.0 copy-start
  33.0 6.1 %fields.1 = (f32[2,3,16,32,128]{4,3,2,1,0:T(8,128)}, f32[2,3,16,32,128]{4,3,2,1,0:T(8,128)}, f32[8,128]{1,0:T(8,128)}) custom-call(f32[2,3,16,32,128]{4,3,2,1,0:T(8,128)} %refs_0_.1, f32[2,3,16,32,128]{4,3,2,1,0:T(8,128)} %refs_1_.1, f32[16,32,128]{2,1,0:T(8,128)} %get-tuple-element.23.coef_hbm.refs_2_, ...), custom_call_target="tpu_custom_call" | custom-call | bytes 18000000 | tf_op jit(solution)/shard_map/fields/pallas_call | solution.py:970
  39.2 1.4 %all-to-all-done.got_ref = f32[16,32,128]{2,1,0:T(8,128)S(1)} async-done(((f32[16,32,128]{2,1,0:T(8,128)}), f32[16,32,128]{2,1,0:T(8,128)S(1)}, u32[]{:S(2)}, u32[]{:S(2)}) %all-to-all-start) | async-done | bytes 262176 | tf_op jit(solution)/shard_map/all_to_all | solution.py:969
  40.5 0.0 copy-done
  40.5 0.0 copy-start.1
  40.5 0.7 %copy-done.1 = f32[8,128]{1,0:T(8,128)S(1)} copy-done((f32[8,128]{1,0:T(8,128)S(1)}, f32[8,128]{1,0:T(8,128)}, u32[]{:S(2)}) %copy-start.1) | copy-done | bytes 4120
  41.2 0.3 x_section.1
  41.5 15.8 %all_to_all.10.got_ref = f32[16,8,128]{2,1,0:T(8,128)S(1)} all-to-all(f32[16,8,128]{2,1,0:T(8,128)S(1)} %x_section.1), channel_id=1, replica_groups={{0,8,16,24,32,40,48,56,64,72,80,88,96,104,112,120},{1,9,17,25,33,41,49,..., dimensions={0} | all-to-all | bytes 131072 | tf_op jit(solution)/shard_map/all_to_all | solution.py:989
  57.3 0.7 %order_sum.1 = f32[2,2,8,32]{3,2,1,0:T(8,128)} custom-call(f32[16,8,128]{2,1,0:T(8,128)S(1)} %all_to_all.10.got_ref), custom_call_target="tpu_custom_call" | custom-call | bytes 3000000 | tf_op jit(solution)/shard_map/order_sum/pallas_call | solution.py:990
Async XLA Ops:
  3.1 11.2 %collective-permute-start = (f32[48,8,128]{2,1,0:T(8,128)}, f32[48,8,128]{2,1,0:T(8,128)}, u32[]{:S(2)}, u32[]{:S(2)}) collective-permute-start(f32[48,8,128]{2,1,0:T(8,128)} %get-tuple-element.24), channel_id=1, source_target_pairs={{0,248},{8,16},{16,8},{24,32},{32,24},{40,48},{48,40},{56,64},{64,... | collective-permute-start | bytes 589832 | tf_op jit(solution)/shard_map/ppermute | solution.py:29
  6.2 8.1 %collective-permute-start.1 = (f32[48,8,128]{2,1,0:T(8,128)}, f32[48,8,128]{2,1,0:T(8,128)}, u32[]{:S(2)}, u32[]{:S(2)}) collective-permute-start(f32[48,8,128]{2,1,0:T(8,128)} %get-tuple-element.25), channel_id=1, source_target_pairs={{0,8},{8,0},{16,24},{24,16},{32,40},{40,32},{48,56},{56,48},{64,72... | collective-permute-start | bytes 589832 | tf_op jit(solution)/shard_map/ppermute | solution.py:29
  16.4 7.9 %collective-permute-start.2 = (f32[3,40,128]{2,1,0:T(8,128)}, f32[3,40,128]{2,1,0:T(8,128)}, u32[]{:S(2)}, u32[]{:S(2)}) collective-permute-start(f32[3,40,128]{2,1,0:T(8,128)} %get-tuple-element.34), channel_id=1, source_target_pairs={{0,7},{1,2},{2,1},{3,4},{4,3},{5,6},{6,5},{7,0},{8,15},{9,10},{10,... | collective-permute-start | bytes 184328 | tf_op jit(solution)/shard_map/ppermute | solution.py:29
  21.4 3.4 %collective-permute-start.3 = (f32[3,40,128]{2,1,0:T(8,128)}, f32[3,40,128]{2,1,0:T(8,128)}, u32[]{:S(2)}, u32[]{:S(2)}) collective-permute-start(f32[3,40,128]{2,1,0:T(8,128)} %get-tuple-element.35), channel_id=1, source_target_pairs={{0,1},{1,0},{2,3},{3,2},{4,5},{5,4},{6,7},{7,6},{8,9},{9,8},{10,11... | collective-permute-start | bytes 184328 | tf_op jit(solution)/shard_map/ppermute | solution.py:29
  28.0 12.5 %all-to-all-start = ((f32[16,32,128]{2,1,0:T(8,128)}), f32[16,32,128]{2,1,0:T(8,128)S(1)}, u32[]{:S(2)}, u32[]{:S(2)}) async-start(f32[16,32,128]{2,1,0:T(8,128)} %bitcast.1), calls=%async_computation | async-start | bytes 524288 | tf_op jit(solution)/shard_map/all_to_all | solution.py:969
  33.0 7.5 %copy-start = (f32[128,128]{1,0:T(8,128)S(1)}, f32[128,128]{1,0:T(8,128)}, u32[]{:S(2)}) copy-start(f32[128,128]{1,0:T(8,128)} %get-tuple-element.39.wave_ref) | copy-start | bytes 196612
  40.5 0.7 %copy-start.1 = (f32[8,128]{1,0:T(8,128)S(1)}, f32[8,128]{1,0:T(8,128)}, u32[]{:S(2)}) copy-start(f32[8,128]{1,0:T(8,128)} %get-tuple-element.40.after_hbm) | copy-start | bytes 12292

commit v7 on v6

--- a/solution.py
+++ b/solution.py
@@ -567,7 +567,6 @@
     edges, block = scratch[0:4], scratch[4:8]
     wave_ref, sem = scratch[8:10]
     e_all, h_all, coef_all, edge_ref = block
-    copies = fetch_edges(own_hbm, tail_hbm, (cols_a_hbm, cols_b_hbm), rot_hbm, edges, sem, 0)
     level = monitor_ref[0]
     low = jnp.clip(level - 2, 0, NZ - 5)
     here, there = pl.ds(low, 5), pl.ds(low + 1, 5)
@@ -584,6 +583,7 @@
         sem,
         5,
     )
+    copies = fetch_edges(own_hbm, tail_hbm, (cols_a_hbm, cols_b_hbm), rot_hbm, edges, sem, 0)
     arrived(copies)
     fill_edges(edges, block, (0, 1))
     arrived(large)

time: 58.3 us -> 58.6 us (level)
  no operation moved by 1% of the time
where the time goes in v7:
time: 58.6 us; the launch traced here: 58.2 us
  Pallas kernels  20.8 us (35%)
  starting transfers between devices  17.8 us (30%)
  blocking collectives  15.8 us (27%)
  waiting for transfers between devices  1.82 us (3%)
  between operations  1.38 us (2%)
  local copies, waits for them, and re-layouts  0.69 us (1%)
    all_to_all x1, blocking collectives, shards(): got = lax.all_to_all(partial, both, 0, 0, tiled=True, axis_index_groups=far)  15.8 us
    ppermute x4, starting transfers between devices, swapped(): return lax.ppermute(block, axis, route)  12.8 us
    pallas_call x1, Pallas kernels, shards(): pl.pallas_call(functools.partial(field_kernel, (0, 1), 12), out_shape=(f3...  6.12 us
    all_to_all x1, starting transfers between devices, shards(): got = lax.all_to_all(spread, both, 0, 0, tiled=True, axis_index_groups=near)  5.01 us
    pallas_call x1, Pallas kernels, shards(): pl.pallas_call(plane_kernel, out_shape=f32(2, count_y, ROWS, 4 * each_q),...  3.48 us
    pallas_call x1, Pallas kernels, shards(): pl.pallas_call(own_kernel, out_shape=(f32(13, ROWS, COLS), f32(3, ROWS, C...  3.39 us
    pallas_call x1, Pallas kernels, shards(): pl.pallas_call(rows_kernel, out_shape=(f32(8, COLS), f32(MAIN_BLOCKS, 8,...  2.42 us
    pallas_call x1, Pallas kernels, shards(): pl.pallas_call(functools.partial(feet_kernel, (count_x, count_y)), out_sh...  2.26 us
  transfers between devices with their start and end apart: 5, of which 2 were waited for; matrix products, arithmetic and copies ran while one was open for 0% of the time, Pallas kernels for 20%

profile of v7, /device:TPU:1, one launch (start us, length us, event | category | flops | bytes accessed | tf_op | source)
XLA Modules:
  0.0 58.2 jit_solution(2257667646927461303)
XLA Ops:
  0.6 2.4 %rows.1 = (f32[8,128]{1,0:T(8,128)}, f32[48,8,128]{2,1,0:T(8,128)}, f32[48,8,128]{2,1,0:T(8,128)}) custom-call(f32[2,3,16,32,128]{4,3,2,1,0:T(8,128)} %refs_0_.1, f32[2,3,16,32,128]{4,3,2,1,0:T(8,128)} %refs_1_.1, s32[16,32,128]{2,1,0:T(8,128)} %material_hbm.3, s32[16,32,128]{2,1,0:T(8,128)} %pattern_hbm.3, f32[8]{0:T(128)} %base_hbm.1, f32[4,16]{1,0:T(4,128)} %mode_hbm.1, ...), custom_call_target="tpu_custom_call" | custom-call | bytes 9000000 | tf_op jit(solution)/shard_map/rows/pallas_call | solution.py:858
  3.1 3.1 %collective-permute-start = (f32[48,8,128]{2,1,0:T(8,128)}, f32[48,8,128]{2,1,0:T(8,128)}, u32[]{:S(2)}, u32[]{:S(2)}) collective-permute-start(f32[48,8,128]{2,1,0:T(8,128)} %get-tuple-element.24), channel_id=1, source_target_pairs={{0,248},{8,16},{16,8},{24,32},{32,24},{40,48},{48,40},{56,64},{64,... | collective-permute-start | bytes 589832 | tf_op jit(solution)/shard_map/ppermute | solution.py:29
  6.2 4.7 %collective-permute-start.1 = (f32[48,8,128]{2,1,0:T(8,128)}, f32[48,8,128]{2,1,0:T(8,128)}, u32[]{:S(2)}, u32[]{:S(2)}) collective-permute-start(f32[48,8,128]{2,1,0:T(8,128)} %get-tuple-element.25), channel_id=1, source_target_pairs={{0,8},{8,0},{16,24},{24,16},{32,40},{40,32},{48,56},{56,48},{64,72... | collective-permute-start | bytes 589832 | tf_op jit(solution)/shard_map/ppermute | solution.py:29
  10.9 3.4 %own.1 = (f32[13,32,128]{2,1,0:T(8,128)}, f32[3,32,128]{2,1,0:T(8,128)}, f32[3,32,128]{2,1,0:T(8,128)}, f32[16,32,128]{2,1,0:T(8,128)}) custom-call(f32[2,3,16,32,128]{4,3,2,1,0:T(8,128)} %refs_0_.1, f32[2,3,16,32,128]{4,3,2,1,0:T(8,128)} %refs_1_.1, s32[16,32,128]{2,1,0:T(8,128)} %material_hbm.3, s32[16,32,128]{2,1,0:T(8,128)} %pattern_hbm.3, ...), custom_call_target="tpu_custom_call" | custom-call | bytes 12000000 | tf_op jit(solution)/shard_map/own/pallas_call | solution.py:883
  14.3 0.0 collective-permute-done.rows_b_hbm
  14.3 0.0 collective-permute-done.1.rows_a_hbm
  14.3 2.1 %pack.1 = (f32[13,8,128]{2,1,0:T(8,128)}, f32[3,40,128]{2,1,0:T(8,128)}, f32[3,40,128]{2,1,0:T(8,128)}, f32[8,128]{1,0:T(8,128)}) custom-call(f32[3,32,128]{2,1,0:T(8,128)} %get-tuple-element.26.main_a_hbm, f32[3,32,128]{2,1,0:T(8,128)} %get-tuple-element.27.main_b_hbm, f32[48,8,128]{2,1,0:T(8,128)} %collective-permute-done.rows_b_hbm, ...), custom_call_target="tpu_custom_call" | custom-call | bytes 6000000 | tf_op jit(solution)/shard_map/pack/pallas_call | solution.py:905
  16.4 5.0 %collective-permute-start.2 = (f32[3,40,128]{2,1,0:T(8,128)}, f32[3,40,128]{2,1,0:T(8,128)}, u32[]{:S(2)}, u32[]{:S(2)}) collective-permute-start(f32[3,40,128]{2,1,0:T(8,128)} %get-tuple-element.34), channel_id=1, source_target_pairs={{0,7},{1,2},{2,1},{3,4},{4,3},{5,6},{6,5},{7,0},{8,15},{9,10},{10,... | collective-permute-start | bytes 184328 | tf_op jit(solution)/shard_map/ppermute | solution.py:29
  21.4 0.0 collective-permute-start.3
  22.1 2.3 %feet.1 = (f32[2,3,16,8,128]{4,3,2,1,0:T(8,128)}, f32[2,3,16,8,128]{4,3,2,1,0:T(8,128)}, f32[16,8,128]{2,1,0:T(8,128)}, f32[256,256]{1,0:T(8,128)}, f32[128,128]{1,0:T(8,128)}) custom-call(f32[48,8,128]{2,1,0:T(8,128)} %collective-permute-done.rows_b_hbm, f32[48,8,128]{2,1,0:T(8,128)} %collective-permute-done.1.rows_a_hbm, ...), custom_call_target="tpu_custom_call" | custom-call | bytes 6000000 | tf_op jit(solution)/shard_map/feet/pallas_call | solution.py:927
  24.3 0.0 collective-permute-done.2.cols_b_hbm.refs_8_
  24.3 0.5 collective-permute-done.3.cols_a_hbm.refs_9_
  24.8 3.5 %plane.1 = f32[2,8,32,128]{3,2,1,0:T(8,128)} custom-call(f32[2,3,16,32,128]{4,3,2,1,0:T(8,128)} %refs_0_.1, f32[2,3,16,32,128]{4,3,2,1,0:T(8,128)} %refs_1_.1, f32[16,32,128]{2,1,0:T(8,128)} %get-tuple-element.23.coef_hbm.refs_2_, f32[2,3,16,8,128]{4,3,2,1,0:T(8,128)} %get-tuple-element.29.e_foot_hbm.refs_3_, ...), custom_call_target="tpu_custom_call" | custom-call | bytes 9000000 | tf_op jit(solution)/shard_map/plane/pallas_call | solution.py:950
  28.3 5.0 %all-to-all-start = ((f32[16,32,128]{2,1,0:T(8,128)}), f32[16,32,128]{2,1,0:T(8,128)S(1)}, u32[]{:S(2)}, u32[]{:S(2)}) async-start(f32[16,32,128]{2,1,0:T(8,128)} %bitcast.1), calls=%async_computation | async-start | bytes 524288 | tf_op jit(solution)/shard_map/all_to_all | solution.py:969
  33.3 0.0 copy-start
  33.3 6.1 %fields.1 = (f32[2,3,16,32,128]{4,3,2,1,0:T(8,128)}, f32[2,3,16,32,128]{4,3,2,1,0:T(8,128)}, f32[8,128]{1,0:T(8,128)}) custom-call(f32[2,3,16,32,128]{4,3,2,1,0:T(8,128)} %refs_0_.1, f32[2,3,16,32,128]{4,3,2,1,0:T(8,128)} %refs_1_.1, f32[16,32,128]{2,1,0:T(8,128)} %get-tuple-element.23.coef_hbm.refs_2_, ...), custom_call_target="tpu_custom_call" | custom-call | bytes 18000000 | tf_op jit(solution)/shard_map/fields/pallas_call | solution.py:970
  39.4 1.4 %all-to-all-done.got_ref = f32[16,32,128]{2,1,0:T(8,128)S(1)} async-done(((f32[16,32,128]{2,1,0:T(8,128)}), f32[16,32,128]{2,1,0:T(8,128)S(1)}, u32[]{:S(2)}, u32[]{:S(2)}) %all-to-all-start) | async-done | bytes 262176 | tf_op jit(solution)/shard_map/all_to_all | solution.py:969
  40.8 0.0 copy-done
  40.8 0.0 copy-start.1
  40.8 0.7 %copy-done.1 = f32[8,128]{1,0:T(8,128)S(1)} copy-done((f32[8,128]{1,0:T(8,128)S(1)}, f32[8,128]{1,0:T(8,128)}, u32[]{:S(2)}) %copy-start.1) | copy-done | bytes 4120
  41.5 0.3 x_section.1
  41.8 15.8 %all_to_all.10.got_ref = f32[16,8,128]{2,1,0:T(8,128)S(1)} all-to-all(f32[16,8,128]{2,1,0:T(8,128)S(1)} %x_section.1), channel_id=1, replica_groups={{0,8,16,24,32,40,48,56,64,72,80,88,96,104,112,120},{1,9,17,25,33,41,49,..., dimensions={0} | all-to-all | bytes 131072 | tf_op jit(solution)/shard_map/all_to_all | solution.py:989
  57.5 0.7 %order_sum.1 = f32[2,2,8,32]{3,2,1,0:T(8,128)} custom-call(f32[16,8,128]{2,1,0:T(8,128)S(1)} %all_to_all.10.got_ref), custom_call_target="tpu_custom_call" | custom-call | bytes 3000000 | tf_op jit(solution)/shard_map/order_sum/pallas_call | solution.py:990
Async XLA Ops:
  3.1 11.2 %collective-permute-start = (f32[48,8,128]{2,1,0:T(8,128)}, f32[48,8,128]{2,1,0:T(8,128)}, u32[]{:S(2)}, u32[]{:S(2)}) collective-permute-start(f32[48,8,128]{2,1,0:T(8,128)} %get-tuple-element.24), channel_id=1, source_target_pairs={{0,248},{8,16},{16,8},{24,32},{32,24},{40,48},{48,40},{56,64},{64,... | collective-permute-start | bytes 589832 | tf_op jit(solution)/shard_map/ppermute | solution.py:29
  6.2 8.1 %collective-permute-start.1 = (f32[48,8,128]{2,1,0:T(8,128)}, f32[48,8,128]{2,1,0:T(8,128)}, u32[]{:S(2)}, u32[]{:S(2)}) collective-permute-start(f32[48,8,128]{2,1,0:T(8,128)} %get-tuple-element.25), channel_id=1, source_target_pairs={{0,8},{8,0},{16,24},{24,16},{32,40},{40,32},{48,56},{56,48},{64,72... | collective-permute-start | bytes 589832 | tf_op jit(solution)/shard_map/ppermute | solution.py:29
  16.4 7.9 %collective-permute-start.2 = (f32[3,40,128]{2,1,0:T(8,128)}, f32[3,40,128]{2,1,0:T(8,128)}, u32[]{:S(2)}, u32[]{:S(2)}) collective-permute-start(f32[3,40,128]{2,1,0:T(8,128)} %get-tuple-element.34), channel_id=1, source_target_pairs={{0,7},{1,2},{2,1},{3,4},{4,3},{5,6},{6,5},{7,0},{8,15},{9,10},{10,... | collective-permute-start | bytes 184328 | tf_op jit(solution)/shard_map/ppermute | solution.py:29
  21.4 3.4 %collective-permute-start.3 = (f32[3,40,128]{2,1,0:T(8,128)}, f32[3,40,128]{2,1,0:T(8,128)}, u32[]{:S(2)}, u32[]{:S(2)}) collective-permute-start(f32[3,40,128]{2,1,0:T(8,128)} %get-tuple-element.35), channel_id=1, source_target_pairs={{0,1},{1,0},{2,3},{3,2},{4,5},{5,4},{6,7},{7,6},{8,9},{9,8},{10,11... | collective-permute-start | bytes 184328 | tf_op jit(solution)/shard_map/ppermute | solution.py:29
  28.3 12.5 %all-to-all-start = ((f32[16,32,128]{2,1,0:T(8,128)}), f32[16,32,128]{2,1,0:T(8,128)S(1)}, u32[]{:S(2)}, u32[]{:S(2)}) async-start(f32[16,32,128]{2,1,0:T(8,128)} %bitcast.1), calls=%async_computation | async-start | bytes 524288 | tf_op jit(solution)/shard_map/all_to_all | solution.py:969
  33.3 7.5 %copy-start = (f32[128,128]{1,0:T(8,128)S(1)}, f32[128,128]{1,0:T(8,128)}, u32[]{:S(2)}) copy-start(f32[128,128]{1,0:T(8,128)} %get-tuple-element.39.wave_ref) | copy-start | bytes 196612
  40.8 0.7 %copy-start.1 = (f32[8,128]{1,0:T(8,128)S(1)}, f32[8,128]{1,0:T(8,128)}, u32[]{:S(2)}) copy-start(f32[8,128]{1,0:T(8,128)} %get-tuple-element.40.after_hbm) | copy-start | bytes 12292
